TPU v7x, 32 devices: a whole 2x2x4 slice. The times are simulated.
32 devices in a mesh: dp: 2 (over core), seq: 16 (over z, y, x).
Axes of the slice: x: 2, y: 2, z: 4, core: 2. Of those that a mesh axis runs over, the one named last changes fastest.
Arguments:
- joints_x: bfloat16 [2, 256, 16, 1536], P('dp', 'seq'), may hold values from -6 to 6
- cotangent: bfloat16 [2, 256, 16, 1536], P('dp', 'seq'), may hold values from -6 to 6
- hidden: int32 [2, 256, 16], P('dp', 'seq'), may hold values 0 or 1
- stream_clip: int32 [2, 256], P('dp'), may hold values from 0 to 271, as said below
- stream_kind: int32 [2, 256], P('dp'), may hold values from 0 to 3, as said below
- adjacency: int32 [4, 136, 136], replicated, may hold values 0 or 1
- mask_token: bfloat16 [1536], replicated, may hold values from -6 to 6
- norm_gain: float32 [1536], replicated, may hold values from 0.1 to 1.9
- w_qkv: bfloat16 [1536, 2304], replicated, may hold values from -0.15625 to 0.15625
- w_out: bfloat16 [768, 1536], replicated, may hold values from -0.21875 to 0.21875
- graph_coef: float32 [12], replicated, may hold values from 0.5 to 260
Outputs:
- layer_out: bfloat16 [2, 256, 16, 1536], P('dp', 'seq')
- grad_x: bfloat16 [2, 256, 16, 1536], P('dp', 'seq')
- grad_token: float32 [1536], replicated
- grad_gain: float32 [1536], replicated
- grad_coef: float32 [12], replicated
Inputs may be any that keep to these rules, and one draw needn't show every extreme that they name: `stream_clip`: the slots of a clip are consecutive, clip numbers rise in slot order, starting at 0, at most 16 of them; every slot after the last clip, the last slot always among them, is padding numbered 16 plus its slot index. `stream_kind`: constant within a clip; a clip of kind 0, 1, 2, 3 has 17, 25, 52, 133 slots; slot 0 starts a clip of kind 3; padding slots have kind 0.
All inputs are finite; a program needn't handle non-finite values. No bound on the sum of `hidden` on one device may be relied on, other than what follows from the above.
Results may differ from a plain program's by a relative error of at most 0.0089.
Values may be sent and summed in bfloat16 or wider, within the bound.
No kernel may reach another device: no remote copies, remote signals or barrier semaphores. Data moves between devices by JAX's collectives and lax.ppermute only.
A program may use at most 128 MiB of HBM per device.

v0:
```python
import jax
import jax.numpy as jnp
from jax import lax
from jax.sharding import PartitionSpec as P


def product(form, left, right):
    return jnp.einsum(form, left, right, preferred_element_type=jnp.float32)


def frame_tables(clip_ids, kind_ids, adjacency):
    slot_count = clip_ids.shape[0]
    kind_count, joint_max = (adjacency.shape[0], adjacency.shape[1])
    slot_ids = jnp.arange(slot_count, dtype=jnp.int32)
    same_clip = clip_ids[:, None] == clip_ids[None, :]
    first_slot = jnp.min(jnp.where(same_clip, slot_ids[None, :], slot_count), axis=1)
    joint_idx = slot_ids - first_slot
    table_row = kind_ids * joint_max + joint_idx
    row_pick = (
        table_row[:, None] == jnp.arange(kind_count * joint_max, dtype=jnp.int32)[None, :]
    ).astype(jnp.float32)
    adj_table = adjacency.reshape(kind_count * joint_max, joint_max).astype(jnp.float32)
    picked = jnp.dot(
        row_pick, adj_table, precision=lax.Precision.HIGHEST, preferred_element_type=jnp.float32
    )
    col_pick = (joint_idx[:, None] == jnp.arange(joint_max, dtype=jnp.int32)[None, :]).astype(
        jnp.float32
    )
    graph_link = jnp.dot(
        picked, col_pick.T, precision=lax.Precision.HIGHEST, preferred_element_type=jnp.float32
    )
    return (same_clip, graph_link)


def project_out(context, w_out):
    return product("jfe,ed->jfd", context, w_out).astype(jnp.bfloat16)


def project_back(cot_rows, w_out):
    return product("jfd,ed->jfe", cot_rows, w_out).astype(jnp.bfloat16)


def attend(x_normed, same_clip, graph_link, graph_coef, w_qkv, head_width):
    slot_count, frame_count = (x_normed.shape[0], x_normed.shape[1])
    head_count = graph_coef.shape[0]
    head_size = head_width // head_count
    score_scale = head_size ** (-0.5)
    united = product("jfd,de->jfe", x_normed, w_qkv).astype(jnp.bfloat16)
    query_part = united[..., :head_width].reshape(slot_count, frame_count, head_count, head_size)
    key_part = united[..., head_width : 2 * head_width].reshape(
        slot_count, frame_count, head_count, head_size
    )
    value_part = united[..., 2 * head_width :].reshape(
        slot_count, frame_count, head_count, head_size
    )
    scores = product("ifhc,jfhc->fhij", query_part, key_part) * score_scale
    scores = scores + graph_coef[None, :, None, None] * graph_link[None, None]
    scores = jnp.where(same_clip[None, None], scores, -jnp.inf)
    row_top = jnp.max(scores, axis=-1, keepdims=True)
    shifted = jnp.exp(scores - row_top)
    weights_f = shifted / jnp.sum(shifted, axis=-1, keepdims=True)
    weights_b = weights_f.astype(jnp.bfloat16)
    context = product("fhij,jfhc->ifhc", weights_b, value_part).astype(jnp.bfloat16)
    context = context.reshape(slot_count, frame_count, head_width)
    return (context, (query_part, key_part, value_part, weights_f, weights_b))


def attend_back(grad_context, saved, graph_link, w_qkv):
    query_part, key_part, value_part, weights_f, weights_b = saved
    slot_count, frame_count, head_count, head_size = query_part.shape
    head_width = head_count * head_size
    score_scale = head_size ** (-0.5)
    grad_context = grad_context.reshape(slot_count, frame_count, head_count, head_size)
    grad_weights = product("ifhc,jfhc->fhij", grad_context, value_part)
    row_total = jnp.sum(weights_f * grad_weights, axis=-1, keepdims=True)
    grad_scores = weights_f * (grad_weights - row_total)
    coef_term = jnp.sum(grad_scores * graph_link[None, None], axis=(0, 2, 3))
    scaled_b = (grad_scores * score_scale).astype(jnp.bfloat16)
    grad_query = product("fhij,jfhc->ifhc", scaled_b, key_part).reshape(
        slot_count, frame_count, head_width
    )
    grad_key = product("fhij,ifhc->jfhc", scaled_b, query_part).reshape(
        slot_count, frame_count, head_width
    )
    grad_value = product("fhij,ifhc->jfhc", weights_b, grad_context).reshape(
        slot_count, frame_count, head_width
    )
    grad_united = jnp.concatenate([grad_query, grad_key, grad_value], axis=-1).astype(jnp.bfloat16)
    grad_normed = product("jfe,de->jfd", grad_united, w_qkv).astype(jnp.bfloat16)
    return (grad_normed, coef_term)


def normalize(x_rows, hidden_on, mask_token, norm_gain):
    x_in = jnp.where(hidden_on, mask_token, x_rows)
    x_float = x_in.astype(jnp.float32)
    root_mean = jnp.sqrt(jnp.mean(x_float * x_float, axis=-1, keepdims=True) + 1e-06)
    x_unit = x_float / root_mean
    x_normed = (x_unit * norm_gain).astype(jnp.bfloat16)
    return (x_float, root_mean, x_unit, x_normed)


def finish(x_float, root_mean, x_unit, hidden_on, attn_back, grad_normed, cot_rows, norm_gain):
    layer_out = (x_float + attn_back.astype(jnp.float32)).astype(jnp.bfloat16)
    gain_grad = grad_normed.astype(jnp.float32) * norm_gain
    grad_input = (
        cot_rows.astype(jnp.float32)
        + (gain_grad - x_unit * jnp.mean(gain_grad * x_unit, axis=-1, keepdims=True)) / root_mean
    )
    grad_x = jnp.where(hidden_on, jnp.float32(0.0), grad_input).astype(jnp.bfloat16)
    lead_axes = tuple(range(grad_input.ndim - 1))
    token_term = jnp.sum(jnp.where(hidden_on, grad_input, jnp.float32(0.0)), axis=lead_axes)
    gain_term = jnp.sum(grad_normed.astype(jnp.float32) * x_unit, axis=lead_axes)
    return (layer_out, grad_x, token_term, gain_term)


def on_device(
    joints_x,
    cotangent,
    hidden,
    stream_clip,
    stream_kind,
    adjacency,
    mask_token,
    norm_gain,
    w_qkv,
    w_out,
    graph_coef,
):
    head_width = w_out.shape[0]
    x_rows = joints_x[0]
    cot_rows = cotangent[0]
    hidden_on = (hidden[0] == 1)[..., None]
    same_clip, graph_link = frame_tables(stream_clip[0], stream_kind[0], adjacency)
    x_float, root_mean, x_unit, x_normed = normalize(x_rows, hidden_on, mask_token, norm_gain)
    spread_x = lax.all_to_all(x_normed, "seq", split_axis=1, concat_axis=0, tiled=True)
    context, saved = attend(spread_x, same_clip, graph_link, graph_coef, w_qkv, head_width)
    return_rows = project_out(context, w_out)
    arrived_rows = lax.all_to_all(return_rows, "seq", split_axis=0, concat_axis=1, tiled=True)
    spread_cot = lax.all_to_all(cot_rows, "seq", split_axis=1, concat_axis=0, tiled=True)
    grad_context = project_back(spread_cot, w_out)
    grad_spread, coef_term = attend_back(grad_context, saved, graph_link, w_qkv)
    grad_normed = lax.all_to_all(grad_spread, "seq", split_axis=0, concat_axis=1, tiled=True)
    layer_out, grad_x, token_term, gain_term = finish(
        x_float, root_mean, x_unit, hidden_on, arrived_rows, grad_normed, cot_rows, norm_gain
    )
    token_sum, gain_sum, coef_sum = lax.psum((token_term, gain_term, coef_term), ("dp", "seq"))
    return (layer_out[None], grad_x[None], token_sum, gain_sum, coef_sum)


def solution(mesh):
    return jax.shard_map(
        on_device,
        mesh=mesh,
        in_specs=(
            P("dp", "seq", None, None),
            P("dp", "seq", None, None),
            P("dp", "seq", None),
            P("dp", None),
            P("dp", None),
            P(),
            P(),
            P(),
            P(),
            P(),
            P(),
        ),
        out_specs=(P("dp", "seq", None, None), P("dp", "seq", None, None), P(), P(), P()),
        check_vma=False,
    )
```

profile of v0, /device:TPU:0, one launch (start us, length us, event | category | flops | bytes accessed | tf_op | source)
XLA Modules:
  0.0 193.8 jit_solution(11773581437030897731)
XLA Ops:
  0.7 0.9 compare_bitcast_fusion
  1.6 2.0 %fusion.14 = f32[16,16]{0,1:T(8,128)S(1)} fusion(pred[16,16]{0,1:T(8,128)(4,1)S(1)} %copy.48, bf16[1,16,16,1536]{3,2,1,0:T(8,128)(2,1)} %param.11, bf16[1536]{0:T(1024)(128)(2,1)} %param.17), kind=kLoop, calls=%fused_computation.25 | loop fusion | flops 1572608 | bytes 790784 | tf_op jit(solution)/shard_map/reduce_sum | solution.py:96
  3.7 2.6 %multiply_convert_fusion.1 = bf16[16,16,1536]{2,0,1:T(8,128)(2,1)} fusion(f32[1536]{0:T(1024)} %param.18, f32[16,16]{0,1:T(8,128)S(1)} %add_sqrt_fusion, bf16[1,16,16,1536]{3,2,1,0:T(8,128)(2,1)} %param.11, bf16[1536]{0:T(1024)(128)(2,1)} %param.17, pred[16,16]{0,1:T(8,128)(4,1)S(1)} %copy.48), kind=kLoop, calls=%fused_computation.35 | loop fusion | flops 1966080 | bytes 1583360 | tf_op jit(solution)/shard_map/convert_element_type | solution.py:98
  6.2 8.4 %all-to-all-start = ((bf16[16,16,1536]{2,0,1:T(8,128)(2,1)}), bf16[16,16,1536]{2,0,1:T(8,128)(2,1)}, u32[]{:S(2)}, u32[]{:S(2)}) async-start(bf16[16,16,1536]{2,0,1:T(8,128)(2,1)} %multiply_convert_fusion.1), calls=%async_computation | async-start | bytes 1572864 | tf_op jit(solution)/shard_map/all_to_all | solution.py:135
  14.6 1.3 copy.90
  16.1 0.7 broadcast_compare_fusion
  16.8 17.6 %all-to-all-done = bf16[16,16,1536]{2,0,1:T(8,128)(2,1)} async-done(((bf16[16,16,1536]{2,0,1:T(8,128)(2,1)}), bf16[16,16,1536]{2,0,1:T(8,128)(2,1)}, u32[]{:S(2)}, u32[]{:S(2)}) %all-to-all-start) | async-done | bytes 786464 | tf_op jit(solution)/shard_map/all_to_all | solution.py:135
  34.4 5.0 %all-to-all-start.2 = ((bf16[16,16,1536]{2,0,1:T(8,128)(2,1)}), bf16[16,16,1536]{2,0,1:T(8,128)(2,1)}, u32[]{:S(2)}, u32[]{:S(2)}) async-start(bf16[16,16,1536]{2,0,1:T(8,128)(2,1)} %bitcast.102), calls=%async_computation.2 | async-start | bytes 1572864 | tf_op jit(solution)/shard_map/all_to_all | solution.py:139
  39.4 1.1 convert_element_type.126
  40.5 0.7 fusion.27
  41.2 1.0 fusion.41
  42.3 5.3 %fusion.2 = bf16[256,1,2304]{2,0,1:T(8,128)(2,1)S(1)} fusion(bf16[256,1536]{1,0:T(8,128)(2,1)} %bitcast.4, bf16[1536,2304]{1,0:T(8,128)(2,1)} %param.19), kind=kOutput, calls=%fused_computation.3 | convolution fusion | flops 1812529152 | bytes 9043968 | tf_op jit(solution)/shard_map/jfd,de->jfe/dot_general | solution.py:8
  47.6 0.9 copy.53
  48.5 0.9 copy.54
  49.5 0.2 copy.52
  49.6 8.4 %all-to-all-done.2 = bf16[16,16,1536]{2,0,1:T(8,128)(2,1)} async-done(((bf16[16,16,1536]{2,0,1:T(8,128)(2,1)}), bf16[16,16,1536]{2,0,1:T(8,128)(2,1)}, u32[]{:S(2)}, u32[]{:S(2)}) %all-to-all-start.2) | async-done | bytes 786464 | tf_op jit(solution)/shard_map/all_to_all | solution.py:139
  58.1 2.7 %convolution_convert_fusion.6 = bf16[256,768]{1,0:T(8,128)(2,1)} fusion(bf16[256,1536]{1,0:T(8,128)(2,1)} %bitcast.21, bf16[768,1536]{1,0:T(8,128)(2,1)S(1)} %copy-done), kind=kOutput, calls=%fused_computation.40 | convolution fusion | flops 604176384 | bytes 3538944 | tf_op jit(solution)/shard_map/jfd,ed->jfe/dot_general | solution.py:8
  60.8 1.2 copy.60
  62.0 2.3 %fusion.53 = f32[12,256,256]{1,2,0:T(8,128)} fusion(bf16[256,12,64]{0,2,1:T(8,128)(2,1)S(1)} %bitcast.107, bf16[256,12,64]{0,2,1:T(8,128)(2,1)S(1)} %bitcast.104), kind=kOutput, calls=%fused_computation.77 | convolution fusion | flops 100663296 | bytes 3932160 | tf_op jit(solution)/shard_map/ifhc,jfhc->fhij/dot_general | solution.py:8
  64.3 4.7 %fusion.52 = (f32[12,256]{1,0:T(8,128)}, f32[12,256,256]{1,2,0:T(8,128)}) fusion(f32[256,256]{0,1:T(8,128)} %fusion.41, f32[12]{0:T(128)S(1)} %copy-done.15, pred[256,256]{0,1:T(8,128)(4,1)} %broadcast_compare_fusion, bf16[256,12,64]{0,2,1:T(8,128)(2,1)S(1)} %bitcast.111, bf16[256,12,64]{0,2,1:T(8,128)(2,1)} %bitcast.113), kind=kOutput, calls=%fused_computation.76 | convolution fusion | flops 105382144 | bytes 4272176 | tf_op jit(solution)/shard_map/sub | solution.py:60
  69.1 6.6 %convolution_convert_fusion.5 = bf16[12,64,256]{2,1,0:T(8,128)(2,1)} fusion(bf16[256,12,64]{0,2,1:T(8,128)(2,1)} %bitcast.114, f32[12,256,256]{1,2,0:T(8,128)} %fusion.53, f32[12,256,256]{1,2,0:T(8,128)} %get-tuple-element.28, f32[12,256]{1,0:T(8,128)} %get-tuple-element.27), kind=kOutput, calls=%fused_computation.39 | convolution fusion | flops 106368256 | bytes 7090176 | tf_op jit(solution)/shard_map/fhij,jfhc->ifhc/dot_general | solution.py:8
  75.6 6.4 %convolution_convert_fusion.4 = bf16[12,64,256]{2,1,0:T(8,128)(2,1)} fusion(bf16[256,12,64]{0,2,1:T(8,128)(2,1)S(1)} %bitcast.112, f32[12,256,256]{1,2,0:T(8,128)} %fusion.53, f32[12,256,256]{1,2,0:T(8,128)} %get-tuple-element.28, f32[12,256]{1,0:T(8,128)} %get-tuple-element.27), kind=kOutput, calls=%fused_computation.38 | convolution fusion | flops 106368256 | bytes 7090176 | tf_op jit(solution)/shard_map/fhij,ifhc->jfhc/dot_general | solution.py:8
  82.1 2.6 %convolution_convert_fusion.3 = bf16[12,64,256]{2,1,0:T(8,128)(2,1)S(1)} fusion(bf16[256,12,64]{0,2,1:T(8,128)(2,1)S(1)} %bitcast.108, f32[12,256,256]{1,2,0:T(8,128)} %get-tuple-element.28, f32[12,256]{1,0:T(8,128)} %get-tuple-element.27), kind=kOutput, calls=%fused_computation.37 | convolution fusion | flops 102432768 | bytes 3944448 | tf_op jit(solution)/shard_map/fhij,ifhc->jfhc/dot_general | solution.py:8
  84.7 6.0 %fusion.7 = bf16[256,1,1536]{2,0,1:T(8,128)(2,1)} fusion(bf16[1536,2304]{1,0:T(8,128)(2,1)} %param.19, bf16[256,768]{0,1:T(8,128)(2,1)S(1)} %bitcast.120, bf16[256,768]{0,1:T(8,128)(2,1)S(1)} %bitcast.119, bf16[256,768]{0,1:T(8,128)(2,1)S(1)} %bitcast.118), kind=kOutput, calls=%fused_computation.14 | convolution fusion | flops 1815871488 | bytes 9043968 | tf_op jit(solution)/shard_map/jfe,de->jfd/dot_general | solution.py:8
  90.6 0.5 broadcast.106
  91.1 2.3 %reduce.8 = bf16[256,1536]{1,0:T(8,128)(2,1)S(1)} reduce(bf16[256,1,1536]{2,0,1:T(8,128)(2,1)} %fusion.7, bf16[]{:T(256)} %broadcast.106), dimensions={1}, to_apply=%copy.64.reduce_sub_computation | reduce | bytes 1572866 | tf_op jit(solution)/shard_map/convert_element_type | solution.py:89
  93.5 1.4 reshape.263
  94.9 5.0 %all-to-all-start.3 = ((bf16[16,2,12288]{2,1,0:T(2,128)(2,1)}), bf16[16,2,12288]{2,1,0:T(2,128)(2,1)}, u32[]{:S(2)}, u32[]{:S(2)}) async-start(bf16[16,2,12288]{2,1,0:T(2,128)(2,1)} %reshape.263), calls=%async_computation.3 | async-start | bytes 1572864 | tf_op jit(solution)/shard_map/all_to_all | solution.py:142
  99.9 2.3 %convolution_convert_fusion.7 = bf16[12,64,256]{2,1,0:T(8,128)(2,1)S(1)} fusion(bf16[256,12,64]{0,2,1:T(8,128)(2,1)S(1)} %bitcast.105, f32[12,256,256]{1,2,0:T(8,128)} %get-tuple-element.28, f32[12,256]{1,0:T(8,128)} %get-tuple-element.27), kind=kOutput, calls=%fused_computation.41 | convolution fusion | flops 102432768 | bytes 3944448 | tf_op jit(solution)/shard_map/fhij,jfhc->ifhc/dot_general | solution.py:8
  102.2 0.8 fusion.6
  103.0 1.9 reduce.9
  104.9 3.3 %reshape.261 = bf16[16,2,12288]{2,1,0:T(2,128)(2,1)} reshape(bf16[256,1536]{1,0:T(8,128)(2,1)} %reduce.9) | data formatting | bytes 1572864
  108.2 10.4 %all-to-all-done.3 = bf16[16,2,12288]{2,1,0:T(2,128)(2,1)} async-done(((bf16[16,2,12288]{2,1,0:T(2,128)(2,1)}), bf16[16,2,12288]{2,1,0:T(2,128)(2,1)}, u32[]{:S(2)}, u32[]{:S(2)}) %all-to-all-start.3) | async-done | bytes 786464 | tf_op jit(solution)/shard_map/all_to_all | solution.py:142
  118.5 4.9 %all-to-all-start.1 = ((bf16[16,2,12288]{2,1,0:T(2,128)(2,1)}), bf16[16,2,12288]{2,1,0:T(2,128)(2,1)}, u32[]{:S(2)}, u32[]{:S(2)}) async-start(bf16[16,2,12288]{2,1,0:T(2,128)(2,1)} %reshape.261), calls=%async_computation.1 | async-start | bytes 1572864 | tf_op jit(solution)/shard_map/all_to_all | solution.py:138
  123.5 4.2 %multiply_reduce_fusion = f32[12]{0:T(128)S(1)} fusion(f32[256,256]{0,1:T(8,128)S(1)} %copy-done.10, bf16[256,12,64]{0,2,1:T(8,128)(2,1)S(1)} %bitcast.109, bf16[256,12,64]{0,2,1:T(8,128)(2,1)S(1)} %bitcast.106, f32[12,256,256]{1,2,0:T(8,128)} %get-tuple-element.28, f32[12,256]{1,0:T(8,128)S(1)} %copy-done.18), kind=kOutput, calls=%fused_computation.4 | convolution fusion | flops 206834928 | bytes 4206640 | tf_op jit(solution)/shard_map/sub | solution.py:76
  127.8 5.3 %reshape.264 = bf16[256,1,1536]{2,1,0:T(2,128)(2,1)} reshape(bf16[16,2,12288]{2,1,0:T(2,128)(2,1)} %all-to-all-done.3) | data formatting | bytes 1572864
  133.1 1.6 copy.73
  134.7 1.1 multiply_reduce_fusion.3
  135.9 1.4 multiply_reduce_fusion.2
  137.2 4.9 %all-to-all-done.1 = bf16[16,2,12288]{2,1,0:T(2,128)(2,1)} async-done(((bf16[16,2,12288]{2,1,0:T(2,128)(2,1)}), bf16[16,2,12288]{2,1,0:T(2,128)(2,1)}, u32[]{:S(2)}, u32[]{:S(2)}) %all-to-all-start.1) | async-done | bytes 786464 | tf_op jit(solution)/shard_map/all_to_all | solution.py:138
  142.2 5.2 %reshape.262 = bf16[256,1,1536]{2,1,0:T(2,128)(2,1)} reshape(bf16[16,2,12288]{2,1,0:T(2,128)(2,1)} %all-to-all-done.1) | data formatting | bytes 1572864
  147.4 1.7 copy.72
  149.1 0.2 copy-done.2
  149.3 0.2 copy-done.6
  149.5 1.5 select_convert_fusion
  151.0 1.3 copy.65
  152.3 1.3 copy.66
  153.6 40.2 %all-reduce = (f32[1536]{0:T(1024)}, f32[1536]{0:T(1024)}, f32[12]{0:T(128)}) all-reduce(f32[1536]{0:T(1024)S(1)} %get-tuple-element.16, f32[1536]{0:T(1024)S(1)} %get-tuple-element.15, f32[12]{0:T(128)S(1)} %multiply_reduce_fusion), channel_id=1, replica_groups=mesh['dp'=2,'seq'=16] {'dp','seq'}, use_global_device_ids=true, to_apply=%region_7.8 | all-reduce | flops 3084 | bytes 24672 | tf_op jit(solution)/shard_map/psum | solution.py:146
  (43 shorter events, 0.4 us)
Async XLA Ops:
  0.6 57.4 %copy-start = (bf16[768,1536]{1,0:T(8,128)(2,1)S(1)}, bf16[768,1536]{1,0:T(8,128)(2,1)}, u32[]{:S(2)}) copy-start(bf16[768,1536]{1,0:T(8,128)(2,1)} %param.20) | copy-start | bytes 7077892
  0.6 14.0 %copy-start.4 = (bf16[1,16,16,1536]{3,2,1,0:T(8,128)(2,1)S(1)}, bf16[1,16,16,1536]{3,2,1,0:T(8,128)(2,1)}, u32[]{:S(2)}) copy-start(bf16[1,16,16,1536]{3,2,1,0:T(8,128)(2,1)} %param.12) | copy-start | bytes 2359300
  0.7 15.3 %copy-start.13 = (s32[1,256]{1,0:T(1,128)S(1)}, s32[1,256]{1,0:T(1,128)}, u32[]{:S(2)}) copy-start(s32[1,256]{1,0:T(1,128)} %param.14) | copy-start | bytes 3076
  0.7 15.4 %copy-start.14 = (s32[1,256]{1,0:T(1,128)S(1)}, s32[1,256]{1,0:T(1,128)}, u32[]{:S(2)}) copy-start(s32[1,256]{1,0:T(1,128)} %param.15) | copy-start | bytes 3076
  6.2 28.2 %all-to-all-start = ((bf16[16,16,1536]{2,0,1:T(8,128)(2,1)}), bf16[16,16,1536]{2,0,1:T(8,128)(2,1)}, u32[]{:S(2)}, u32[]{:S(2)}) async-start(bf16[16,16,1536]{2,0,1:T(8,128)(2,1)} %multiply_convert_fusion.1), calls=%async_computation | async-start | bytes 1572864 | tf_op jit(solution)/shard_map/all_to_all | solution.py:135
  34.4 23.7 %all-to-all-start.2 = ((bf16[16,16,1536]{2,0,1:T(8,128)(2,1)}), bf16[16,16,1536]{2,0,1:T(8,128)(2,1)}, u32[]{:S(2)}, u32[]{:S(2)}) async-start(bf16[16,16,1536]{2,0,1:T(8,128)(2,1)} %bitcast.102), calls=%async_computation.2 | async-start | bytes 1572864 | tf_op jit(solution)/shard_map/all_to_all | solution.py:139
  60.8 3.6 %copy-start.9 = (bf16[256,1,768]{0,2,1:T(8,128)(2,1)S(1)}, bf16[256,1,768]{0,2,1:T(8,128)(2,1)}, u32[]{:S(2)}) copy-start(bf16[256,1,768]{0,2,1:T(8,128)(2,1)} %copy.53) | copy-start | bytes 1179652
  60.8 3.6 %copy-start.15 = (f32[12]{0:T(128)S(1)}, f32[12]{0:T(128)}, u32[]{:S(2)}) copy-start(f32[12]{0:T(128)} %param.21) | copy-start | bytes 148
  62.0 20.1 %copy-start.7 = (bf16[256,768]{0,1:T(8,128)(2,1)}, bf16[256,768]{0,1:T(8,128)(2,1)S(1)}, u32[]{:S(2)}) copy-start(bf16[256,768]{0,1:T(8,128)(2,1)S(1)} %copy.60) | copy-start | bytes 1179652
  82.1 2.6 %copy-start.16 = (bf16[12,64,256]{2,1,0:T(8,128)(2,1)S(1)}, bf16[12,64,256]{2,1,0:T(8,128)(2,1)}, u32[]{:S(2)}) copy-start(bf16[12,64,256]{2,1,0:T(8,128)(2,1)} %convolution_convert_fusion.5) | copy-start | bytes 1179652
  82.1 2.6 %copy-start.17 = (bf16[12,64,256]{2,1,0:T(8,128)(2,1)S(1)}, bf16[12,64,256]{2,1,0:T(8,128)(2,1)}, u32[]{:S(2)}) copy-start(bf16[12,64,256]{2,1,0:T(8,128)(2,1)} %convolution_convert_fusion.4) | copy-start | bytes 1179652
  94.9 23.6 %all-to-all-start.3 = ((bf16[16,2,12288]{2,1,0:T(2,128)(2,1)}), bf16[16,2,12288]{2,1,0:T(2,128)(2,1)}, u32[]{:S(2)}, u32[]{:S(2)}) async-start(bf16[16,2,12288]{2,1,0:T(2,128)(2,1)} %reshape.263), calls=%async_computation.3 | async-start | bytes 1572864 | tf_op jit(solution)/shard_map/all_to_all | solution.py:142
  104.8 18.6 %copy-start.8 = (bf16[256,768]{0,1:T(8,128)(2,1)S(1)}, bf16[256,768]{0,1:T(8,128)(2,1)}, u32[]{:S(2)}) copy-start(bf16[256,768]{0,1:T(8,128)(2,1)} %copy-done.7) | copy-start | bytes 1179652
  104.9 18.6 %copy-start.10 = (f32[256,256]{0,1:T(8,128)S(1)}, f32[256,256]{0,1:T(8,128)}, u32[]{:S(2)}) copy-start(f32[256,256]{0,1:T(8,128)} %fusion.41) | copy-start | bytes 786436
  104.9 18.7 %copy-start.18 = (f32[12,256]{1,0:T(8,128)S(1)}, f32[12,256]{1,0:T(8,128)}, u32[]{:S(2)}) copy-start(f32[12,256]{1,0:T(8,128)} %get-tuple-element.27) | copy-start | bytes 36868
  118.5 23.6 %all-to-all-start.1 = ((bf16[16,2,12288]{2,1,0:T(2,128)(2,1)}), bf16[16,2,12288]{2,1,0:T(2,128)(2,1)}, u32[]{:S(2)}, u32[]{:S(2)}) async-start(bf16[16,2,12288]{2,1,0:T(2,128)(2,1)} %reshape.261), calls=%async_computation.1 | async-start | bytes 1572864 | tf_op jit(solution)/shard_map/all_to_all | solution.py:138
  127.8 6.9 %copy-start.3 = (bf16[1,16,16,1536]{3,2,1,0:T(8,128)(2,1)S(1)}, bf16[1,16,16,1536]{3,2,1,0:T(8,128)(2,1)}, u32[]{:S(2)}) copy-start(bf16[1,16,16,1536]{3,2,1,0:T(8,128)(2,1)} %param.11) | copy-start | bytes 2359300
  127.8 7.0 %copy-start.11 = (f32[1536]{0:T(1024)S(1)}, f32[1536]{0:T(1024)}, u32[]{:S(2)}) copy-start(f32[1536]{0:T(1024)} %param.18) | copy-start | bytes 18436
  127.8 7.0 %copy-start.12 = (bf16[1536]{0:T(1024)(128)(2,1)S(1)}, bf16[1536]{0:T(1024)(128)(2,1)}, u32[]{:S(2)}) copy-start(bf16[1536]{0:T(1024)(128)(2,1)} %param.17) | copy-start | bytes 9220
  133.1 2.8 %copy-start.5 = (bf16[1,16,16,1536]{3,2,1,0:T(8,128)(2,1)S(1)}, bf16[1,16,16,1536]{3,2,1,0:T(8,128)(2,1)}, u32[]{:S(2)}) copy-start(bf16[1,16,16,1536]{3,2,1,0:T(8,128)(2,1)} %param.12) | copy-start | bytes 2359300
  134.7 1.2 copy-start.1
  147.4 1.9 copy-start.2
  147.4 2.1 %copy-start.6 = (bf16[1,16,16,1536]{3,2,1,0:T(8,128)(2,1)S(1)}, bf16[1,16,16,1536]{3,2,1,0:T(8,128)(2,1)}, u32[]{:S(2)}) copy-start(bf16[1,16,16,1536]{3,2,1,0:T(8,128)(2,1)} %param.12) | copy-start | bytes 2359300
where the time goes:
time: 195 us; the launch traced here: 194 us
  matrix products  45.6 us (23%)
  waiting for transfers between devices  41.4 us (21%)
  blocking collectives  40.2 us (21%)
  local copies, waits for them, and re-layouts  26.9 us (14%)
  starting transfers between devices  23.2 us (12%)
  other arithmetic  15.6 us (8%)
    psum x1, blocking collectives, on_device(): lax.psum((token_term, gain_term, coef_term), ('dp', 'seq'))  40.2 us
    dot_general x9, matrix products, product(): return jnp.einsum(form, left, right, preferred_element_type=jnp.float32)  34.9 us
    unnamed x47, local copies, waits for them, and re-layouts  23 us
    all_to_all x1, waiting for transfers between devices, on_device(): lax.all_to_all(x_normed, 'seq', split_axis=1, concat_axis=0, tiled=True)  17.6 us
    all_to_all x1, waiting for transfers between devices, on_device(): lax.all_to_all(grad_spread, 'seq', split_axis=0, concat_axis=1, tiled=True)  10.4 us
    all_to_all x1, waiting for transfers between devices, on_device(): lax.all_to_all(cot_rows, 'seq', split_axis=1, concat_axis=0, tiled=True)  8.43 us
    all_to_all x1, starting transfers between devices, on_device(): lax.all_to_all(x_normed, 'seq', split_axis=1, concat_axis=0, tiled=True)  8.36 us
    all_to_all x1, starting transfers between devices, on_device(): lax.all_to_all(grad_spread, 'seq', split_axis=0, concat_axis=1, tiled=True)  4.96 us
  transfers between devices with their start and end apart: 4, of which 4 were waited for; matrix products, arithmetic and copies ran while one was open for 18% of the time, Pallas kernels for 0%

commit v1 on v0

v1 whole, which is shorter than its diff:
```python
import functools

import jax
import jax.numpy as jnp
import numpy as np
from jax import lax
from jax.experimental import pallas as pl
from jax.experimental.pallas import tpu as pltpu
from jax.sharding import PartitionSpec as P

BF = jnp.bfloat16
F32 = jnp.float32
BIG_CLIP = 133
HIDDEN_MARK = 64.0
MASKED = -1e30
EP = 16
EQ = 8


def dot_nn(a, b):
    return lax.dot_general(a, b, (((1,), (0,)), ((), ())), preferred_element_type=F32)


def dot_nt(a, b):
    return lax.dot_general(a, b, (((1,), (1,)), ((), ())), preferred_element_type=F32)


def dot_tn(a, b):
    return lax.dot_general(a, b, (((0,), (0,)), ((), ())), preferred_element_type=F32)


def iota(shape, axis):
    return lax.broadcasted_iota(jnp.int32, shape, axis)


def hidden_column(hid, slots, frames, frame_major):
    rows = slots * frames
    r = iota((rows, 1), 0)
    slot_of = r % slots if frame_major else r // frames
    frame_of = r // slots if frame_major else r % frames
    pick_slot = (slot_of == iota((rows, slots), 1)).astype(BF)
    by_slot = dot_nn(pick_slot, hid.astype(F32).astype(BF))
    return jnp.sum(jnp.where(frame_of == iota((rows, frames), 1), by_slot, 0.0), axis=1, keepdims=True)


def row_swap(slots, frames, to_frame_major):
    rows = slots * frames
    r = iota((rows, 1), 0)
    if to_frame_major:
        source = (r % slots) * frames + r // slots
    else:
        source = (r % frames) * slots + r // frames
    return (iota((rows, rows), 1) == source).astype(BF)


def send_kernel(slots, frames, x_ref, cot_ref, hid_ref, w_out_ref, out_ref, token_ref):
    width = x_ref.shape[1]
    swap = row_swap(slots, frames, True)
    gc = dot_nt(cot_ref[...], w_out_ref[...]).astype(BF)
    out_ref[:, width:] = dot_nn(swap, gc).astype(BF)
    hid_t = hidden_column(hid_ref[...], slots, frames, True)
    moved = dot_nn(swap, x_ref[...])
    first = jnp.where(
        (iota((moved.shape[0], 128), 1) == 0) & (hid_t > 0.5), HIDDEN_MARK, moved[:, :128]
    )
    out_ref[:, :128] = first.astype(BF)
    out_ref[:, 128:width] = moved[:, 128:].astype(BF)
    hid_s = hidden_column(hid_ref[...], slots, frames, False)
    token_ref[...] = jnp.sum(
        jnp.where(hid_s > 0.5, cot_ref[...].astype(F32), 0.0), axis=0, keepdims=True
    )


def final_kernel(
    slots, frames, recv_ref, x_ref, cot_ref, hid_ref, tok_ref, w_out_ref, out_ref, grad_ref
):
    hw = w_out_ref.shape[0]
    swap = row_swap(slots, frames, False)
    ctx = dot_nn(swap, recv_ref[:, :hw]).astype(BF)
    attn = dot_nn(ctx, w_out_ref[...]).astype(BF)
    hid = hidden_column(hid_ref[...], slots, frames, False) > 0.5
    x_in = jnp.where(hid, tok_ref[...].astype(F32), x_ref[...].astype(F32))
    out_ref[...] = (x_in + attn.astype(F32)).astype(BF)
    delta = dot_nn(swap, recv_ref[:, hw:])
    grad_ref[...] = jnp.where(hid, 0.0, cot_ref[...].astype(F32) + delta).astype(BF)


def frame_kernel(
    blocks,
    nf,
    sb,
    guests,
    recv_ref,
    ext_ref,
    link_ref,
    link_e_ref,
    coef_ref,
    coef_e_ref,
    flag_ref,
    tok_ref,
    gain_ref,
    token_in_ref,
    w_hbm,
    out_ref,
    ext_out_ref,
    sums_ref,
    w_ref,
    xn_s,
    q_s,
    k_s,
    v_s,
    g_s,
    gq_s,
    gk_s,
    gv_s,
    ctx_s,
    sem,
):
    d = gain_ref.shape[1]
    hw = w_ref.shape[1] // 3
    main = blocks * sb
    keys = main + EP
    rows = nf * main
    all_rows = rows + nf * EP
    heads = coef_ref.shape[0]
    hs = hw // heads
    seg_rows = nf * guests

    copies = []
    for c in range(3):
        cp = pltpu.make_async_copy(
            w_hbm.at[:, pl.ds(c * hw, hw)], w_ref.at[:, pl.ds(c * hw, hw)], sem.at[c]
        )
        cp.start()
        copies.append(cp)

    def gather(value):
        if sb % 16 == 0:
            return jnp.concatenate(
                [
                    value[(j * nf + f) * sb : (j * nf + f + 1) * sb]
                    for f in range(nf)
                    for j in range(blocks)
                ],
                axis=0,
            )
        r = iota((rows, 1), 0)
        slot = r % main
        source = ((slot // sb) * nf + r // main) * sb + slot % sb
        return dot_nn((iota((rows, rows), 1) == source).astype(BF), value).astype(BF)

    def scatter(value):
        if sb % 16 == 0:
            return jnp.concatenate(
                [
                    value[f * main + j * sb : f * main + (j + 1) * sb]
                    for j in range(blocks)
                    for f in range(nf)
                ],
                axis=0,
            )
        r = iota((rows, 1), 0)
        pair = r // sb
        source = (pair % nf) * main + (pair // nf) * sb + r % sb
        return dot_nn((iota((rows, rows), 1) == source).astype(BF), value).astype(BF)

    er = iota((nf * EP, 1), 0)
    guest_row = jnp.where(er % EP < guests, (er // EP) * guests + er % EP, 1 << 20)

    def guest_segment(seg):
        pick = (iota((nf * EP, ext_ref.shape[0]), 1) == guest_row + seg * seg_rows).astype(BF)
        return dot_nn(pick, ext_ref[...]).astype(BF)

    x_all = jnp.concatenate(
        [
            gather(recv_ref[:, :d]),
            jnp.concatenate([guest_segment(s) for s in range(d // hw)], axis=1),
        ],
        axis=0,
    ).astype(F32)
    hid = x_all[:, 0:1] > 0.5 * HIDDEN_MARK
    x_all = jnp.where(hid, tok_ref[...].astype(F32), x_all)
    inv = 1.0 / jnp.sqrt(jnp.mean(x_all * x_all, axis=1, keepdims=True) + 1e-6)
    x_unit = x_all * inv
    xn_s[...] = (x_unit * gain_ref[...]).astype(BF)

    gc_main = gather(recv_ref[:, d:])
    gc_ext = guest_segment(d // hw)
    for f in range(nf):
        g_s[f, :main] = gc_main[f * main : (f + 1) * main]
        g_s[f, main:] = gc_ext[f * EP : (f + 1) * EP]

    for c, ref in enumerate((q_s, k_s, v_s)):
        copies[c].wait()
        part = dot_nn(xn_s[...], w_ref[:, c * hw : (c + 1) * hw]).astype(BF)
        if c == 0:
            part = part * BF(hs**-0.5)
        for f in range(nf):
            ref[f, :main] = part[f * main : (f + 1) * main]
            ref[f, main:] = part[rows + f * EP : rows + (f + 1) * EP]

    own = (iota((heads * EQ, hw), 0) // EQ == iota((heads * EQ, hw), 1) // hs)
    link_e = link_e_ref[...]
    bias_e = jnp.where(link_e < 0, MASKED, coef_e_ref[...] * link_e)
    coef_lanes = jnp.zeros((1, heads * EQ), F32)

    def spread(value):
        tall = jnp.concatenate([value] * heads, axis=0)
        return jnp.where(own, tall, jnp.zeros_like(tall))

    def fold(value):
        kept = jnp.where(own, value, 0.0)
        total = kept[0:EQ]
        for h in range(1, heads):
            total = total + kept[h * EQ : (h + 1) * EQ]
        return jnp.concatenate([total, jnp.zeros((EP - EQ, hw), F32)], axis=0)

    for f in range(nf):
        q_e = spread(q_s[f, main:].astype(F32)[:EQ]).astype(BF)
        g_e = spread(g_s[f, main:].astype(F32)[:EQ]).astype(BF)
        s_t = dot_nt(k_s[f], q_e) + bias_e
        p_t = jnp.exp(s_t - jnp.max(s_t, axis=0, keepdims=True))
        w_t = p_t * (1.0 / jnp.sum(p_t, axis=0, keepdims=True))
        w_b = w_t.astype(BF)
        gw = dot_nt(v_s[f], g_e)
        ds = w_t * (gw - jnp.sum(w_t * gw, axis=0, keepdims=True))
        coef_lanes = coef_lanes + jnp.sum(ds * link_e, axis=0, keepdims=True)
        ds_b = ds.astype(BF)
        ctx_s[f, main:] = fold(dot_tn(w_b, v_s[f])).astype(BF)
        gq_s[f, main:] = fold(dot_tn(ds_b, k_s[f]) * hs**-0.5).astype(BF)
        gk_s[f] = dot_nn(ds_b, q_e)
        gv_s[f] = dot_nn(w_b, g_e)

    lane = iota((1, 128), 1)
    coef_out = jnp.zeros((1, 128), F32)
    for h in range(heads):
        coef_out = coef_out + jnp.where(
            lane == h, jnp.sum(coef_lanes[:, h * EQ : (h + 1) * EQ]), 0.0
        )

    pair_w = 2 * hs
    low = iota((main, pair_w), 1) < hs
    zero = jnp.zeros((main, pair_w), BF)
    link = link_ref[...]
    for p in range(heads // 2):
        cols = slice(p * pair_w, (p + 1) * pair_w)
        bias = jnp.concatenate(
            [
                jnp.where(link < 0, MASKED, coef_ref[2 * p] * link),
                jnp.where(link < 0, MASKED, coef_ref[2 * p + 1] * link),
            ],
            axis=1,
        )
        ds_sum = jnp.zeros((keys, 2 * main), F32)
        for f in range(nf):
            k = k_s[f, :, cols]
            v = v_s[f, :, cols]
            q = q_s[f, :main, cols]
            g = g_s[f, :main, cols]
            qq = jnp.concatenate([jnp.where(low, q, zero), jnp.where(low, zero, q)], axis=0)
            gg = jnp.concatenate([jnp.where(low, g, zero), jnp.where(low, zero, g)], axis=0)
            s_t = dot_nt(k, qq) + bias
            p_t = jnp.exp(s_t - jnp.max(s_t, axis=0, keepdims=True))
            w_t = p_t * (1.0 / jnp.sum(p_t, axis=0, keepdims=True))
            w_b = w_t.astype(BF)
            gw = dot_nt(v, gg)
            ds = w_t * (gw - jnp.sum(w_t * gw, axis=0, keepdims=True))
            ds_sum = ds_sum + ds
            ds_b = ds.astype(BF)
            ctx_t = dot_tn(v, w_b)
            ctx_t = jnp.concatenate([ctx_t[:hs, :main], ctx_t[hs:, main:]], axis=0)
            ctx_s[f, :main, cols] = ctx_t.T.astype(BF)
            gq_t = dot_tn(k, ds_b)
            gq_t = jnp.concatenate([gq_t[:hs, :main], gq_t[hs:, main:]], axis=0)
            gq_s[f, :main, cols] = (gq_t.T * hs**-0.5).astype(BF)
            gk_s[f, :, cols] += dot_nn(ds_b, qq)
            gv_s[f, :, cols] += dot_nn(w_b, gg)
        lanes = jnp.sum(ds_sum * jnp.concatenate([link, link], axis=1), axis=0, keepdims=True)
        coef_out = coef_out + jnp.where(lane == 2 * p, jnp.sum(lanes[:, :main]), 0.0)
        coef_out = coef_out + jnp.where(lane == 2 * p + 1, jnp.sum(lanes[:, main:]), 0.0)

    def stacked(ref):
        return jnp.concatenate(
            [ref[f, :main].astype(BF) for f in range(nf)]
            + [ref[f, main:].astype(BF) for f in range(nf)],
            axis=0,
        )

    gn = dot_nt(stacked(gq_s), w_ref[:, :hw])
    gn = gn + dot_nt(stacked(gk_s), w_ref[:, hw : 2 * hw])
    gn = gn + dot_nt(stacked(gv_s), w_ref[:, 2 * hw :])
    first_half = flag_ref[0] == 1
    r = iota((all_rows, 1), 0)
    is_guest = r >= rows
    place = jnp.where(is_guest, (r - rows) % EP, r % main)
    guest_limit = jnp.where(first_half, guests, 0)
    main_limit = jnp.where(first_half, 0, guests)
    valid = (is_guest & (place < guest_limit)) | (~is_guest & (place >= main_limit))
    gx = gn * x_unit
    g_gain = gn * gain_ref[...]
    mean_gx = jnp.mean(g_gain * x_unit, axis=1, keepdims=True)
    delta = (g_gain - x_unit * mean_gx) * inv
    sums_ref[:, :d] = token_in_ref[...] + jnp.sum(
        jnp.where(valid & hid, delta, 0.0), axis=0, keepdims=True
    )
    sums_ref[:, d : 2 * d] = jnp.sum(jnp.where(valid, gx, 0.0), axis=0, keepdims=True)
    sums_ref[:, 2 * d :] = coef_out
    delta = delta.astype(BF)
    ctx = stacked(ctx_s)
    out_ref[:, :hw] = scatter(ctx[:rows])
    out_ref[:, hw:] = scatter(delta[:rows])

    orow = iota((ext_out_ref.shape[0], 1), 0)
    inner = orow % seg_rows
    ext_total = jnp.zeros(ext_out_ref.shape, F32)
    for s in range(1 + d // hw):
        piece = ctx[rows:] if s == 0 else delta[rows:, (s - 1) * hw : s * hw]
        source = jnp.where(
            orow // seg_rows == s, (inner // guests) * EP + inner % guests, 1 << 20
        )
        ext_total = ext_total + dot_nn(
            (iota((ext_out_ref.shape[0], nf * EP), 1) == source).astype(BF), piece
        )
    ext_out_ref[...] = ext_total.astype(BF)


VMEM = pl.BlockSpec(memory_space=pltpu.VMEM)
SMEM = pl.BlockSpec(memory_space=pltpu.SMEM)
HBM = pl.BlockSpec(memory_space=pl.ANY)


def table_kernel(half_slots, guests, heads, flag_ref, clip_ref, kind_ref, adj_ref, link_ref, link_e_ref, adj_s):
    first_half = flag_ref[0]
    total = clip_ref.shape[1]
    kind_count, joint_max = adj_ref.shape[0], adj_ref.shape[1]
    keys = half_slots + EP
    adj_s[...] = jnp.zeros(adj_s.shape, F32)
    adj_s[:, :joint_max, :joint_max] = adj_ref[...].astype(F32)
    i = iota((keys, 1), 0)
    slot = jnp.where(i < half_slots, i + jnp.where(first_half == 1, 0, half_slots), i)
    valid = ((i < half_slots) & (i >= jnp.where(first_half == 1, 0, guests))) | (
        (i >= half_slots) & (i < jnp.where(first_half == 1, half_slots + guests, 0))
    )
    lanes = iota((keys, total), 1)
    at = lanes == slot
    clip_row = clip_ref[...].astype(F32)
    clip = jnp.sum(jnp.where(at, clip_row, 0.0), axis=1, keepdims=True)
    kind = jnp.sum(jnp.where(at, kind_ref[...].astype(F32), 0.0), axis=1, keepdims=True)
    first = jnp.min(
        jnp.where(clip_row == clip, lanes.astype(F32), 1.0 * total), axis=1, keepdims=True
    )
    joint = slot.astype(F32) - first
    clip = jnp.where(valid, clip, -1.0 - i.astype(F32))
    pick = (iota((keys, adj_s.shape[1]), 1).astype(F32) == joint).astype(BF)
    picked = jnp.zeros((keys, adj_s.shape[2]), F32)
    for k in range(kind_count):
        picked = picked + jnp.where(kind == 1.0 * k, dot_nn(pick, adj_s[k].astype(BF)), 0.0)
    link = dot_nt(pick, picked.astype(BF))
    eye = iota((keys, keys), 0) == iota((keys, keys), 1)
    clip_across = jnp.sum(jnp.where(eye, clip, 0.0), axis=0, keepdims=True)
    link = jnp.where(clip == clip_across, link, -1.0)
    link_ref[...] = link[:, :half_slots]
    tile = (iota((EP, heads * EQ), 1) % EQ == iota((EP, heads * EQ), 0)).astype(BF)
    link_e_ref[...] = dot_nn(link[:, half_slots:].astype(BF), tile)


def on_device(
    n,
    joints_x,
    cotangent,
    hidden,
    stream_clip,
    stream_kind,
    adjacency,
    mask_token,
    norm_gain,
    w_qkv,
    w_out,
    graph_coef,
):
    _, slots, frames, d = joints_x.shape
    hw = w_out.shape[0]
    heads = graph_coef.shape[0]
    total = stream_clip.shape[1]
    half = n // 2
    nf = frames // half
    half_slots = total // 2
    guests = BIG_CLIP - half_slots
    rows = slots * frames
    wide = d + hw
    segs = wide // hw
    me = lax.axis_index("seq")
    first_half = me < half
    groups = [list(range(half)), list(range(half, n))]

    x = joints_x.reshape(rows, d)
    cot = cotangent.reshape(rows, d)
    hid = hidden[0]
    tok = mask_token.reshape(1, d)

    send, token_cot = pl.pallas_call(
        functools.partial(send_kernel, slots, frames),
        out_shape=(
            jax.ShapeDtypeStruct((rows, wide), BF),
            jax.ShapeDtypeStruct((1, d), F32),
        ),
        in_specs=[VMEM] * 4,
        out_specs=(VMEM, VMEM),
        compiler_params=pltpu.CompilerParams(vmem_limit_bytes=40 << 20),
        name="send",
    )(x, cot, hid, w_out)

    recv = lax.all_to_all(send, "seq", 0, 0, axis_index_groups=groups, tiled=True)

    flag = first_half.astype(jnp.int32).reshape(1)
    joint_pad = -(-adjacency.shape[1] // 256) * 256
    link, link_e = pl.pallas_call(
        functools.partial(table_kernel, half_slots, guests, heads),
        out_shape=(
            jax.ShapeDtypeStruct((half_slots + EP, half_slots), F32),
            jax.ShapeDtypeStruct((half_slots + EP, heads * EQ), F32),
        ),
        in_specs=[SMEM, VMEM, VMEM, VMEM],
        out_specs=(VMEM, VMEM),
        scratch_shapes=[pltpu.VMEM((adjacency.shape[0], joint_pad, joint_pad), F32)],
        compiler_params=pltpu.CompilerParams(vmem_limit_bytes=24 << 20),
        cost_estimate=pl.CostEstimate(flops=400_000_000, bytes_accessed=600_000, transcendentals=0),
        name="tables",
    )(flag, stream_clip, stream_kind, adjacency)

    def buffer_row(f, e):
        return ((e // slots) * nf + f) * slots + e % slots

    run = min(slots, guests)
    starts = [
        (buffer_row(f, e), min(run, guests - e)) for f in range(nf) for e in range(0, guests, run)
    ]
    ext_rows = -(-segs * nf * guests // 16) * 16
    pieces = [
        recv[a : a + c, s * hw : (s + 1) * hw] for s in range(segs) for a, c in starts
    ]
    pieces.append(jnp.zeros((ext_rows - segs * nf * guests, hw), BF))
    ext = lax.ppermute(
        jnp.concatenate(pieces, axis=0), "seq", [(half + i, i) for i in range(half)]
    )

    main = half_slots
    all_rows = rows + nf * EP
    out, ext_out, sums = pl.pallas_call(
        functools.partial(frame_kernel, half, nf, slots, guests),
        out_shape=(
            jax.ShapeDtypeStruct((rows, wide), BF),
            jax.ShapeDtypeStruct((ext_rows, hw), BF),
            jax.ShapeDtypeStruct((1, 2 * d + 128), F32),
        ),
        in_specs=[VMEM, VMEM, VMEM, VMEM, SMEM, VMEM, SMEM, VMEM, VMEM, VMEM, HBM],
        out_specs=(VMEM, VMEM, VMEM),
        scratch_shapes=[
            pltpu.VMEM((d, 3 * hw), BF),
            pltpu.VMEM((all_rows, d), BF),
            pltpu.VMEM((nf, main + EP, hw), BF),
            pltpu.VMEM((nf, main + EP, hw), BF),
            pltpu.VMEM((nf, main + EP, hw), BF),
            pltpu.VMEM((nf, main + EP, hw), BF),
            pltpu.VMEM((nf, main + EP, hw), BF),
            pltpu.VMEM((nf, main + EP, hw), F32),
            pltpu.VMEM((nf, main + EP, hw), F32),
            pltpu.VMEM((nf, main + EP, hw), BF),
            pltpu.SemaphoreType.DMA((3,)),
        ],
        compiler_params=pltpu.CompilerParams(vmem_limit_bytes=56 << 20),
        name="frames",
    )(
        recv,
        ext,
        link,
        link_e,
        graph_coef,
        jnp.repeat(graph_coef, EQ).reshape(1, heads * EQ),
        flag,
        tok,
        norm_gain.reshape(1, d),
        token_cot,
        w_qkv,
    )

    back = lax.ppermute(ext_out, "seq", [(i, half + i) for i in range(half)])
    at = 0
    merged = out
    for a, c in starts:
        new = jnp.concatenate(
            [back[s * nf * guests + at : s * nf * guests + at + c] for s in range(segs)], axis=1
        )
        new = jnp.where(first_half, out[a : a + c], new)
        merged = merged.at[a : a + c].set(new)
        at += c
    returned = lax.all_to_all(merged, "seq", 0, 0, axis_index_groups=groups, tiled=True)

    sums = sums + lax.ppermute(sums, "dp", [(0, 1), (1, 0)])
    k = 1
    while k < n:
        sums = sums + lax.ppermute(sums, "seq", [(i, i ^ k) for i in range(n)])
        k *= 2

    layer_out, grad_x = pl.pallas_call(
        functools.partial(final_kernel, slots, frames),
        out_shape=(
            jax.ShapeDtypeStruct((rows, d), BF),
            jax.ShapeDtypeStruct((rows, d), BF),
        ),
        in_specs=[VMEM] * 6,
        out_specs=(VMEM, VMEM),
        compiler_params=pltpu.CompilerParams(vmem_limit_bytes=48 << 20),
        name="final",
    )(returned, x, cot, hid, tok, w_out)

    shape = (1, slots, frames, d)
    return (
        layer_out.reshape(shape),
        grad_x.reshape(shape),
        sums[0, :d],
        sums[0, d : 2 * d],
        sums[0, 2 * d : 2 * d + heads],
    )


def solution(mesh):
    return jax.shard_map(
        functools.partial(on_device, mesh.shape["seq"]),
        mesh=mesh,
        in_specs=(
            P("dp", "seq", None, None),
            P("dp", "seq", None, None),
            P("dp", "seq", None),
            P("dp", None),
            P("dp", None),
            P(),
            P(),
            P(),
            P(),
            P(),
            P(),
        ),
        out_specs=(P("dp", "seq", None, None), P("dp", "seq", None, None), P(), P(), P()),
        check_vma=False,
    )
```

time: 195 us -> 97.6 us (0.50)
  matrix products: 45.6 us -> 0 us
  waiting for transfers between devices: 41.4 us -> 20.4 us
  Pallas kernels: 0 us -> 19.7 us
  blocking collectives: 40.2 us -> 22.7 us
  other arithmetic: 15.6 us -> 1.6 us
  local copies, waits for them, and re-layouts: 26.9 us -> 15.2 us
  starting transfers between devices: 23.2 us -> 16.3 us
    all_to_all x4 -> x1, waiting for transfers between devices: 41.4 us -> 0.01 us  [on_device(): lax.all_to_all(merged, 'seq', 0, 0, axis_index_groups=groups, tiled=True)]
    psum x1 -> x0, blocking collectives: 40.2 us -> none  [on_device(): lax.psum((token_term, gain_term, coef_term), ('dp', 'seq'))]
    dot_general x11 -> x0, matrix products: 36.6 us -> none  [the longest x9 34.9 us: product(): return jnp.einsum(form, left, right, preferred_element_type=jnp.float32)]
    all_to_all x0 -> x1, blocking collectives: none -> 22.7 us  [on_device(): lax.all_to_all(send, 'seq', 0, 0, axis_index_groups=groups, tiled=True)]
    ppermute x0 -> x7, waiting for transfers between devices: none -> 20.4 us  [the longest x4 14.8 us: on_device(): sums = sums + lax.ppermute(sums, 'seq', [(i, i ^ k) for i in range(n)])]
    pallas_call x0 -> x4, Pallas kernels: none -> 19.7 us  [the longest x1 14.9 us: on_device(): pl.pallas_call(functools.partial(frame_kernel, half, nf, slots, guests),...]
    all_to_all x4 -> x1, starting transfers between devices: 23.2 us -> 3.7 us  [on_device(): lax.all_to_all(merged, 'seq', 0, 0, axis_index_groups=groups, tiled=True)]
    unnamed x47 -> x40, local copies, waits for them, and re-layouts: 23 us -> 8.82 us
  transfers between devices with their start and end apart: 4 -> 8, of which waited for: 4 -> 7; matrix products, arithmetic and copies ran while one was open for 18% -> 4% of each run, Pallas kernels for 0% -> 1%
where the time goes in v1:
time: 97.6 us; the launch traced here: 96.8 us
  blocking collectives  22.7 us (23%)
  waiting for transfers between devices  20.4 us (21%)
  Pallas kernels  19.7 us (20%)
  starting transfers between devices  16.3 us (17%)
  local copies, waits for them, and re-layouts  15.2 us (16%)
  other arithmetic  1.6 us (2%)
    all_to_all x1, blocking collectives, on_device(): lax.all_to_all(send, 'seq', 0, 0, axis_index_groups=groups, tiled=True)  22.7 us
    pallas_call x1, Pallas kernels, on_device(): pl.pallas_call(functools.partial(frame_kernel, half, nf, slots, guests),...  14.9 us
    ppermute x4, waiting for transfers between devices, on_device(): sums = sums + lax.ppermute(sums, 'seq', [(i, i ^ k) for i in range(n)])  14.8 us
    unnamed x40, local copies, waits for them, and re-layouts  8.82 us
    ppermute x4, starting transfers between devices, on_device(): sums = sums + lax.ppermute(sums, 'seq', [(i, i ^ k) for i in range(n)])  7.99 us
    all_to_all x1, starting transfers between devices, on_device(): lax.all_to_all(merged, 'seq', 0, 0, axis_index_groups=groups, tiled=True)  3.7 us
    ppermute x1, starting transfers between devices, on_device(): back = lax.ppermute(ext_out, 'seq', [(i, half + i) for i in range(half)])  3.21 us
    scatter x2, local copies, waits for them, and re-layouts, on_device(): merged = merged.at[a:a + c].set(new)  2.92 us
  transfers between devices with their start and end apart: 8, of which 7 were waited for; matrix products, arithmetic and copies ran while one was open for 4% of the time, Pallas kernels for 1%

profile of v1, /device:TPU:0, one launch (start us, length us, event | category | flops | bytes accessed | tf_op | source)
XLA Modules:
  0.0 96.8 jit_solution(1155257727423456177)
XLA Ops:
  0.6 0.0 copy-start
  0.6 1.7 %copy-done = bf16[768,1536]{1,0:T(8,128)(2,1)S(1)} copy-done((bf16[768,1536]{1,0:T(8,128)(2,1)S(1)}, bf16[768,1536]{1,0:T(8,128)(2,1)}, u32[]{:S(2)}) %copy-start) | copy-done | bytes 2359320
  2.3 1.1 %copy-done.2 = bf16[1,16,16,1536]{3,2,1,0:T(8,128)(2,1)S(1)} copy-done((bf16[1,16,16,1536]{3,2,1,0:T(8,128)(2,1)S(1)}, bf16[1,16,16,1536]{3,2,1,0:T(8,128)(2,1)}, u32[]{:S(2)}) %copy-start.2) | copy-done | bytes 786456
  3.4 1.1 %copy-done.4 = bf16[1,16,16,1536]{3,2,1,0:T(8,128)(2,1)S(1)} copy-done((bf16[1,16,16,1536]{3,2,1,0:T(8,128)(2,1)S(1)}, bf16[1,16,16,1536]{3,2,1,0:T(8,128)(2,1)}, u32[]{:S(2)}) %copy-start.4) | copy-done | bytes 786456
  4.6 0.7 copy-done.9
  5.3 1.8 %send.1 = (bf16[256,2304]{1,0:T(8,128)(2,1)S(1)}, f32[1,1536]{1,0:T(1,128)S(1)}) custom-call(bf16[256,1536]{1,0:T(8,128)(2,1)S(1)} %bitcast.13, bf16[256,1536]{1,0:T(8,128)(2,1)S(1)} %bitcast.15, s32[16,16]{1,0:T(8,128)S(1)} %bitcast.18, bf16[768,1536]{1,0:T(8,128)(2,1)S(1)} %copy-done), custom_call_target="tpu_custom_call" | custom-call | tf_op jit(solution)/shard_map/send/pallas_call | solution.py:401
  7.0 0.0 copy-start.11
  7.0 0.0 copy-start.19
  7.1 0.0 copy-start.17
  7.1 0.0 copy-start.12
  7.1 0.0 copy-start.14
  7.1 22.7 %all_to_all.22 = bf16[8,32,2304]{2,1,0:T(8,128)(2,1)S(1)} all-to-all(bf16[8,32,2304]{2,1,0:T(8,128)(2,1)S(1)} %bitcast.17), channel_id=1, replica_groups={{0,1,2,3,4,5,6,7},{8,9,10,11,12,13,14,15},{16,17,18,19,20,21,22,23},{24..., dimensions={0} | all-to-all | bytes 2359296 | tf_op jit(solution)/shard_map/all_to_all | solution.py:413
  29.9 0.4 concatenate.13
  30.2 1.3 %collective-permute-start = (bf16[32,768]{1,0:T(8,128)(2,1)S(1)}, bf16[32,768]{1,0:T(8,128)(2,1)S(1)}, u32[]{:S(2)}, u32[]{:S(2)}) collective-permute-start(bf16[32,768]{1,0:T(8,128)(2,1)S(1)} %concatenate.13), channel_id=1, source_target_pairs={{8,0},{9,1},{10,2},{11,3},{12,4},{13,5},{14,6},{15,7},{24,16},{25,... | collective-permute-start | bytes 147464 | tf_op jit(solution)/shard_map/ppermute | solution.py:443
  31.6 0.1 broadcast_in_dim.7
  31.6 0.7 reshape_reshape.3.coef_e_ref
  32.3 0.6 reshape.90.tok_ref
  32.9 0.6 reshape.91.gain_ref
  33.5 0.6 tables.1
  34.1 0.0 copy-start.6
  34.2 0.6 copy-done.6
  34.8 0.6 copy-done.7
  35.4 2.2 %collective-permute-done.ext_ref = bf16[32,768]{1,0:T(8,128)(2,1)S(1)} collective-permute-done((bf16[32,768]{1,0:T(8,128)(2,1)S(1)}, bf16[32,768]{1,0:T(8,128)(2,1)S(1)}, u32[]{:S(2)}, u32[]{:S(2)}) %collective-permute-start) | collective-permute-done | bytes 49184 | tf_op jit(solution)/shard_map/ppermute | solution.py:443
  37.7 0.6 copy-done.16
  38.3 14.9 %frames.1 = (bf16[256,2304]{1,0:T(8,128)(2,1)}, bf16[32,768]{1,0:T(8,128)(2,1)}, f32[1,3200]{1,0:T(1,128)}) custom-call(bf16[256,2304]{1,0:T(8,128)(2,1)} %bitcast.21, bf16[32,768]{1,0:T(8,128)(2,1)} %copy-done.16, f32[144,128]{1,0:T(8,128)} %copy-done.6, f32[144,96]{1,0:T(8,128)} %copy-done.7, f32[12]{0:T(128)} %coef_ref.1, ...), custom_call_target="tpu_custom_call" | custom-call | tf_op jit(solution)/shard_map/frames/pallas_call | solution.py:449
  53.1 3.2 %collective-permute-start.1 = (bf16[32,768]{1,0:T(8,128)(2,1)}, bf16[32,768]{1,0:T(8,128)(2,1)S(1)}, u32[]{:S(2)}, u32[]{:S(2)}) collective-permute-start(bf16[32,768]{1,0:T(8,128)(2,1)} %get-tuple-element.43), channel_id=1, source_target_pairs={{0,8},{1,9},{2,10},{3,11},{4,12},{5,13},{6,14},{7,15},{16,24},{17,... | collective-permute-start | bytes 147464 | tf_op jit(solution)/shard_map/ppermute | solution.py:487
  56.3 2.0 %collective-permute-done.1 = bf16[32,768]{1,0:T(8,128)(2,1)S(1)} collective-permute-done((bf16[32,768]{1,0:T(8,128)(2,1)}, bf16[32,768]{1,0:T(8,128)(2,1)S(1)}, u32[]{:S(2)}, u32[]{:S(2)}) %collective-permute-start.1) | collective-permute-done | bytes 49184 | tf_op jit(solution)/shard_map/ppermute | solution.py:487
  58.4 0.8 maximum_select_fusion.1
  59.2 1.5 %scatter.6 = bf16[256,2304]{1,0:T(8,128)(2,1)} dynamic-update-slice(bf16[256,2304]{1,0:T(8,128)(2,1)} %get-tuple-element.42, bf16[5,2304]{1,0:T(8,128)(2,1)S(1)} %get-tuple-element.50, s32[]{:T(128)} %constant.62.clone.1, s32[]{:T(128)} %constant.62.clone.1) | dynamic-update-slice | bytes 46084 | tf_op jit(solution)/shard_map/scatter | solution.py:495
  60.7 1.5 %scatter.9 = bf16[256,2304]{1,0:T(8,128)(2,1)} dynamic-update-slice(bf16[256,2304]{1,0:T(8,128)(2,1)} %scatter.6, bf16[5,2304]{1,0:T(8,128)(2,1)S(1)} %get-tuple-element.49, s32[]{:T(128)} %constant.63.clone.1, s32[]{:T(128)} %constant.62.clone.1) | dynamic-update-slice | bytes 46084 | tf_op jit(solution)/shard_map/scatter | solution.py:495
  62.2 3.7 %all-to-all-start.1 = ((bf16[8,32,2304]{2,1,0:T(8,128)(2,1)}), bf16[8,32,2304]{2,1,0:T(8,128)(2,1)S(1)}, u32[]{:S(2)}, u32[]{:S(2)}) async-start(bf16[8,32,2304]{2,1,0:T(8,128)(2,1)} %bitcast.22), calls=%async_computation.1 | async-start | bytes 2359296 | tf_op jit(solution)/shard_map/all_to_all | solution.py:497
  65.9 0.1 collective-permute-start.2
  66.0 1.4 %collective-permute-done.2 = f32[1,3200]{1,0:T(1,128)S(1)} collective-permute-done((f32[1,3200]{1,0:T(1,128)}, f32[1,3200]{1,0:T(1,128)S(1)}, u32[]{:S(2)}, u32[]{:S(2)}) %collective-permute-start.2) | collective-permute-done | bytes 12832 | tf_op jit(solution)/shard_map/ppermute | solution.py:499
  67.3 0.7 add.19
  68.1 1.9 %collective-permute-start.3 = (f32[1,3200]{1,0:T(1,128)S(1)}, f32[1,3200]{1,0:T(1,128)S(1)}, u32[]{:S(2)}, u32[]{:S(2)}) collective-permute-start(f32[1,3200]{1,0:T(1,128)S(1)} %add.19), channel_id=1, source_target_pairs={{0,1},{1,0},{2,3},{3,2},{4,5},{5,4},{6,7},{7,6},{8,9},{9,8},{10,11... | collective-permute-start | bytes 38408 | tf_op jit(solution)/shard_map/ppermute | solution.py:502
  70.0 8.6 %collective-permute-done.3 = f32[1,3200]{1,0:T(1,128)S(1)} collective-permute-done((f32[1,3200]{1,0:T(1,128)S(1)}, f32[1,3200]{1,0:T(1,128)S(1)}, u32[]{:S(2)}, u32[]{:S(2)}) %collective-permute-start.3) | collective-permute-done | bytes 12832 | tf_op jit(solution)/shard_map/ppermute | solution.py:502
  78.6 1.5 %collective-permute-start.4 = (f32[1,3200]{1,0:T(1,128)S(1)}, f32[1,3200]{1,0:T(1,128)S(1)}, u32[]{:S(2)}, u32[]{:S(2)}) collective-permute-start(f32[1,3200]{1,0:T(1,128)S(1)} %add.20), channel_id=1, source_target_pairs={{0,2},{1,3},{2,0},{3,1},{4,6},{5,7},{6,4},{7,5},{8,10},{9,11},{10,... | collective-permute-start | bytes 38408 | tf_op jit(solution)/shard_map/ppermute | solution.py:502
  80.1 2.2 %collective-permute-done.4 = f32[1,3200]{1,0:T(1,128)S(1)} collective-permute-done((f32[1,3200]{1,0:T(1,128)S(1)}, f32[1,3200]{1,0:T(1,128)S(1)}, u32[]{:S(2)}, u32[]{:S(2)}) %collective-permute-start.4) | collective-permute-done | bytes 12832 | tf_op jit(solution)/shard_map/ppermute | solution.py:502
  82.3 1.5 %collective-permute-start.5 = (f32[1,3200]{1,0:T(1,128)S(1)}, f32[1,3200]{1,0:T(1,128)S(1)}, u32[]{:S(2)}, u32[]{:S(2)}) collective-permute-start(f32[1,3200]{1,0:T(1,128)S(1)} %add.21), channel_id=1, source_target_pairs={{0,4},{1,5},{2,6},{3,7},{4,0},{5,1},{6,2},{7,3},{8,12},{9,13},{10,... | collective-permute-start | bytes 38408 | tf_op jit(solution)/shard_map/ppermute | solution.py:502
  83.9 2.3 %collective-permute-done.5 = f32[1,3200]{1,0:T(1,128)S(1)} collective-permute-done((f32[1,3200]{1,0:T(1,128)S(1)}, f32[1,3200]{1,0:T(1,128)S(1)}, u32[]{:S(2)}, u32[]{:S(2)}) %collective-permute-start.5) | collective-permute-done | bytes 12832 | tf_op jit(solution)/shard_map/ppermute | solution.py:502
  86.2 3.0 %collective-permute-start.6 = (f32[1,3200]{1,0:T(1,128)S(1)}, f32[1,3200]{1,0:T(1,128)S(1)}, u32[]{:S(2)}, u32[]{:S(2)}) collective-permute-start(f32[1,3200]{1,0:T(1,128)S(1)} %add.22), channel_id=1, source_target_pairs={{0,8},{1,9},{2,10},{3,11},{4,12},{5,13},{6,14},{7,15},{8,0},{9,1},... | collective-permute-start | bytes 38408 | tf_op jit(solution)/shard_map/ppermute | solution.py:502
  89.2 1.7 %collective-permute-done.6 = f32[1,3200]{1,0:T(1,128)S(1)} collective-permute-done((f32[1,3200]{1,0:T(1,128)S(1)}, f32[1,3200]{1,0:T(1,128)S(1)}, u32[]{:S(2)}, u32[]{:S(2)}) %collective-permute-start.6) | collective-permute-done | bytes 12832 | tf_op jit(solution)/shard_map/ppermute | solution.py:502
  90.9 0.6 slice_reduce_fusion
  91.5 0.5 slice_bitcast_fusion
  92.1 0.0 copy-start.3
  92.1 1.1 %copy-done.3 = bf16[1,16,16,1536]{3,2,1,0:T(8,128)(2,1)S(1)} copy-done((bf16[1,16,16,1536]{3,2,1,0:T(8,128)(2,1)S(1)}, bf16[1,16,16,1536]{3,2,1,0:T(8,128)(2,1)}, u32[]{:S(2)}) %copy-start.3) | copy-done | bytes 786456
  93.2 1.1 %copy-done.5 = bf16[1,16,16,1536]{3,2,1,0:T(8,128)(2,1)S(1)} copy-done((bf16[1,16,16,1536]{3,2,1,0:T(8,128)(2,1)S(1)}, bf16[1,16,16,1536]{3,2,1,0:T(8,128)(2,1)}, u32[]{:S(2)}) %copy-start.5) | copy-done | bytes 786456
  94.3 2.4 %final.1 = (bf16[256,1536]{1,0:T(8,128)(2,1)}, bf16[256,1536]{1,0:T(8,128)(2,1)}) custom-call(bf16[256,2304]{1,0:T(8,128)(2,1)S(1)} %bitcast.12, bf16[256,1536]{1,0:T(8,128)(2,1)S(1)} %bitcast.14, bf16[256,1536]{1,0:T(8,128)(2,1)S(1)} %bitcast.16, s32[16,16]{1,0:T(8,128)S(1)} %bitcast.19, bf16[1,1536]{1,0:T(2,128)(2,1)S(1)} %copy-done.8, ...), custom_call_target="tpu_custom_call" | custom-call | tf_op jit(solution)/shard_map/final/pallas_call | solution.py:505
  (31 shorter events, 0.1 us)
Async XLA Ops:
  0.6 1.7 %copy-start = (bf16[768,1536]{1,0:T(8,128)(2,1)S(1)}, bf16[768,1536]{1,0:T(8,128)(2,1)}, u32[]{:S(2)}) copy-start(bf16[768,1536]{1,0:T(8,128)(2,1)} %w_out_ref.3) | copy-start | bytes 7077892
  2.3 1.1 %copy-start.2 = (bf16[1,16,16,1536]{3,2,1,0:T(8,128)(2,1)S(1)}, bf16[1,16,16,1536]{3,2,1,0:T(8,128)(2,1)}, u32[]{:S(2)}) copy-start(bf16[1,16,16,1536]{3,2,1,0:T(8,128)(2,1)} %param.15) | copy-start | bytes 2359300
  3.4 1.1 %copy-start.4 = (bf16[1,16,16,1536]{3,2,1,0:T(8,128)(2,1)S(1)}, bf16[1,16,16,1536]{3,2,1,0:T(8,128)(2,1)}, u32[]{:S(2)}) copy-start(bf16[1,16,16,1536]{3,2,1,0:T(8,128)(2,1)} %param.16) | copy-start | bytes 2359300
  4.6 0.7 copy-start.9
  7.0 22.8 %copy-start.11 = (f32[1,1536]{1,0:T(1,128)}, f32[1,1536]{1,0:T(1,128)S(1)}, u32[]{:S(2)}) copy-start(f32[1,1536]{1,0:T(1,128)S(1)} %get-tuple-element.41.token_in_ref) | copy-start | bytes 18436
  7.0 24.5 %copy-start.19 = (f32[12]{0:T(128)S(1)}, f32[12]{0:T(128)}, u32[]{:S(2)}) copy-start(f32[12]{0:T(128)} %coef_ref.1) | copy-start | bytes 148
  7.0 25.2 %copy-start.18 = (bf16[1536]{0:T(1024)(128)(2,1)S(1)}, bf16[1536]{0:T(1024)(128)(2,1)}, u32[]{:S(2)}) copy-start(bf16[1536]{0:T(1024)(128)(2,1)} %param.21) | copy-start | bytes 9220
  7.1 25.8 %copy-start.17 = (f32[1536]{0:T(1024)S(1)}, f32[1536]{0:T(1024)}, u32[]{:S(2)}) copy-start(f32[1536]{0:T(1024)} %param.22) | copy-start | bytes 18436
  7.1 26.4 %copy-start.12 = (s32[4,136,136]{2,1,0:T(8,128)S(1)}, s32[4,136,136]{2,1,0:T(8,128)}, u32[]{:S(2)}) copy-start(s32[4,136,136]{2,1,0:T(8,128)} %adj_ref.1) | copy-start | bytes 887812
  7.1 26.4 %copy-start.13 = (s32[1,256]{1,0:T(1,128)S(1)}, s32[1,256]{1,0:T(1,128)}, u32[]{:S(2)}) copy-start(s32[1,256]{1,0:T(1,128)} %clip_ref.1) | copy-start | bytes 3076
  7.1 26.4 %copy-start.14 = (s32[1,256]{1,0:T(1,128)S(1)}, s32[1,256]{1,0:T(1,128)}, u32[]{:S(2)}) copy-start(s32[1,256]{1,0:T(1,128)} %kind_ref.1) | copy-start | bytes 3076
  29.8 7.8 %copy-start.15 = (bf16[8,32,2304]{2,1,0:T(8,128)(2,1)}, bf16[8,32,2304]{2,1,0:T(8,128)(2,1)S(1)}, u32[]{:S(2)}) copy-start(bf16[8,32,2304]{2,1,0:T(8,128)(2,1)S(1)} %all_to_all.22) | copy-start | bytes 3538948
  30.2 7.4 %collective-permute-start = (bf16[32,768]{1,0:T(8,128)(2,1)S(1)}, bf16[32,768]{1,0:T(8,128)(2,1)S(1)}, u32[]{:S(2)}, u32[]{:S(2)}) collective-permute-start(bf16[32,768]{1,0:T(8,128)(2,1)S(1)} %concatenate.13), channel_id=1, source_target_pairs={{8,0},{9,1},{10,2},{11,3},{12,4},{13,5},{14,6},{15,7},{24,16},{25,... | collective-permute-start | bytes 147464 | tf_op jit(solution)/shard_map/ppermute | solution.py:443
  34.1 0.6 copy-start.6
  34.8 0.6 copy-start.7
  37.7 0.6 copy-start.16
  53.1 5.3 %collective-permute-start.1 = (bf16[32,768]{1,0:T(8,128)(2,1)}, bf16[32,768]{1,0:T(8,128)(2,1)S(1)}, u32[]{:S(2)}, u32[]{:S(2)}) collective-permute-start(bf16[32,768]{1,0:T(8,128)(2,1)} %get-tuple-element.43), channel_id=1, source_target_pairs={{0,8},{1,9},{2,10},{3,11},{4,12},{5,13},{6,14},{7,15},{16,24},{17,... | collective-permute-start | bytes 147464 | tf_op jit(solution)/shard_map/ppermute | solution.py:487
  62.2 29.9 %copy-start.1 = (bf16[768,1536]{1,0:T(8,128)(2,1)S(1)}, bf16[768,1536]{1,0:T(8,128)(2,1)}, u32[]{:S(2)}) copy-start(bf16[768,1536]{1,0:T(8,128)(2,1)} %w_out_ref.3) | copy-start | bytes 7077892
  62.2 29.9 %copy-start.8 = (bf16[1,1536]{1,0:T(2,128)(2,1)S(1)}, bf16[1,1536]{1,0:T(2,128)(2,1)}, u32[]{:S(2)}) copy-start(bf16[1,1536]{1,0:T(2,128)(2,1)} %reshape.90.tok_ref) | copy-start | bytes 9220
  62.2 29.9 %copy-start.10 = (s32[1,16,16]{2,1,0:T(8,128)S(1)}, s32[1,16,16]{2,1,0:T(8,128)}, u32[]{:S(2)}) copy-start(s32[1,16,16]{2,1,0:T(8,128)} %param.17) | copy-start | bytes 3076
  62.2 29.9 %all-to-all-start.1 = ((bf16[8,32,2304]{2,1,0:T(8,128)(2,1)}), bf16[8,32,2304]{2,1,0:T(8,128)(2,1)S(1)}, u32[]{:S(2)}, u32[]{:S(2)}) async-start(bf16[8,32,2304]{2,1,0:T(8,128)(2,1)} %bitcast.22), calls=%async_computation.1 | async-start | bytes 2359296 | tf_op jit(solution)/shard_map/all_to_all | solution.py:497
  65.9 1.5 %collective-permute-start.2 = (f32[1,3200]{1,0:T(1,128)}, f32[1,3200]{1,0:T(1,128)S(1)}, u32[]{:S(2)}, u32[]{:S(2)}) collective-permute-start(f32[1,3200]{1,0:T(1,128)} %get-tuple-element.46), channel_id=1, source_target_pairs={{0,16},{16,0},{1,17},{17,1},{2,18},{18,2},{3,19},{19,3},{4,20},{20... | collective-permute-start | bytes 38408 | tf_op jit(solution)/shard_map/ppermute | solution.py:499
  68.1 10.5 %collective-permute-start.3 = (f32[1,3200]{1,0:T(1,128)S(1)}, f32[1,3200]{1,0:T(1,128)S(1)}, u32[]{:S(2)}, u32[]{:S(2)}) collective-permute-start(f32[1,3200]{1,0:T(1,128)S(1)} %add.19), channel_id=1, source_target_pairs={{0,1},{1,0},{2,3},{3,2},{4,5},{5,4},{6,7},{7,6},{8,9},{9,8},{10,11... | collective-permute-start | bytes 38408 | tf_op jit(solution)/shard_map/ppermute | solution.py:502
  78.6 3.8 %collective-permute-start.4 = (f32[1,3200]{1,0:T(1,128)S(1)}, f32[1,3200]{1,0:T(1,128)S(1)}, u32[]{:S(2)}, u32[]{:S(2)}) collective-permute-start(f32[1,3200]{1,0:T(1,128)S(1)} %add.20), channel_id=1, source_target_pairs={{0,2},{1,3},{2,0},{3,1},{4,6},{5,7},{6,4},{7,5},{8,10},{9,11},{10,... | collective-permute-start | bytes 38408 | tf_op jit(solution)/shard_map/ppermute | solution.py:502
  82.3 3.8 %collective-permute-start.5 = (f32[1,3200]{1,0:T(1,128)S(1)}, f32[1,3200]{1,0:T(1,128)S(1)}, u32[]{:S(2)}, u32[]{:S(2)}) collective-permute-start(f32[1,3200]{1,0:T(1,128)S(1)} %add.21), channel_id=1, source_target_pairs={{0,4},{1,5},{2,6},{3,7},{4,0},{5,1},{6,2},{7,3},{8,12},{9,13},{10,... | collective-permute-start | bytes 38408 | tf_op jit(solution)/shard_map/ppermute | solution.py:502
  86.2 4.7 %collective-permute-start.6 = (f32[1,3200]{1,0:T(1,128)S(1)}, f32[1,3200]{1,0:T(1,128)S(1)}, u32[]{:S(2)}, u32[]{:S(2)}) collective-permute-start(f32[1,3200]{1,0:T(1,128)S(1)} %add.22), channel_id=1, source_target_pairs={{0,8},{1,9},{2,10},{3,11},{4,12},{5,13},{6,14},{7,15},{8,0},{9,1},... | collective-permute-start | bytes 38408 | tf_op jit(solution)/shard_map/ppermute | solution.py:502
  92.1 1.1 %copy-start.3 = (bf16[1,16,16,1536]{3,2,1,0:T(8,128)(2,1)S(1)}, bf16[1,16,16,1536]{3,2,1,0:T(8,128)(2,1)}, u32[]{:S(2)}) copy-start(bf16[1,16,16,1536]{3,2,1,0:T(8,128)(2,1)} %param.15) | copy-start | bytes 2359300
  93.2 1.1 %copy-start.5 = (bf16[1,16,16,1536]{3,2,1,0:T(8,128)(2,1)S(1)}, bf16[1,16,16,1536]{3,2,1,0:T(8,128)(2,1)}, u32[]{:S(2)}) copy-start(bf16[1,16,16,1536]{3,2,1,0:T(8,128)(2,1)} %param.16) | copy-start | bytes 2359300

commit v2 on v0

v2 whole, which is shorter than its diff:
```python
import functools

import jax
import jax.numpy as jnp
import numpy as np
from jax import lax
from jax.experimental import pallas as pl
from jax.experimental.pallas import tpu as pltpu
from jax.sharding import PartitionSpec as P

BF = jnp.bfloat16
F32 = jnp.float32
BIG_CLIP = 133
HIDDEN_MARK = 64.0
MASKED = -1e30
EP = 16
EQ = 8
VMEM_LIMIT = 16 << 20
FRAMES_LIMIT = 50 << 20
SEND_LIMIT = 56 << 20
SUMS = 5
LANES = 256


def dot_nn(a, b):
    return lax.dot_general(a, b, (((1,), (0,)), ((), ())), preferred_element_type=F32)


def dot_nt(a, b):
    return lax.dot_general(a, b, (((1,), (1,)), ((), ())), preferred_element_type=F32)


def dot_tn(a, b):
    return lax.dot_general(a, b, (((0,), (0,)), ((), ())), preferred_element_type=F32)


def iota(shape, axis):
    return lax.broadcasted_iota(jnp.int32, shape, axis)


def hidden_column(hid, slots, frames, frame_major):
    rows = slots * frames
    r = iota((rows, 1), 0)
    slot_of = r % slots if frame_major else r // frames
    frame_of = r // slots if frame_major else r % frames
    pick_slot = (slot_of == iota((rows, slots), 1)).astype(BF)
    by_slot = dot_nn(pick_slot, hid.astype(F32).astype(BF))
    return jnp.sum(jnp.where(frame_of == iota((rows, frames), 1), by_slot, 0.0), axis=1, keepdims=True)


def row_swap(slots, frames, to_frame_major):
    rows = slots * frames
    r = iota((rows, 1), 0)
    if to_frame_major:
        source = (r % slots) * frames + r // slots
    else:
        source = (r % frames) * slots + r // frames
    return (iota((rows, rows), 1) == source).astype(BF)


def send_kernel(
    slots,
    frames,
    x_hbm,
    cot_hbm,
    hid_hbm,
    w_out_hbm,
    out_ref,
    token_ref,
    x_ref,
    cot_ref,
    hid_ref,
    w_ref,
    sem,
):
    width = x_ref.shape[1]
    copies = [
        pltpu.make_async_copy(hid_hbm, hid_ref, sem.at[0]),
        pltpu.make_async_copy(x_hbm, x_ref, sem.at[1]),
        pltpu.make_async_copy(cot_hbm, cot_ref, sem.at[2]),
        pltpu.make_async_copy(w_out_hbm, w_ref, sem.at[3]),
    ]
    for cp in copies:
        cp.start()
    swap = row_swap(slots, frames, True)
    copies[0].wait()
    hid_t = hidden_column(hid_ref[...], slots, frames, True)
    hid_s = hidden_column(hid_ref[...], slots, frames, False)
    copies[1].wait()
    moved = dot_nn(swap, x_ref[...])
    first = jnp.where(
        (iota((moved.shape[0], 128), 1) == 0) & (hid_t > 0.5), HIDDEN_MARK, moved[:, :128]
    )
    out_ref[:, :128] = first.astype(BF)
    out_ref[:, 128:width] = moved[:, 128:].astype(BF)
    copies[2].wait()
    token_ref[...] = jnp.sum(
        jnp.where(hid_s > 0.5, cot_ref[...].astype(F32), 0.0), axis=0, keepdims=True
    )
    copies[3].wait()
    gc = dot_nt(cot_ref[...], w_ref[...]).astype(BF)
    out_ref[:, width:] = dot_nn(swap, gc).astype(BF)


def final_kernel(
    slots,
    frames,
    shared,
    recv_ref,
    x_hbm,
    cot_hbm,
    hid_ref,
    tok_ref,
    w_ref,
    sums_ref,
    out_hbm,
    grad_hbm,
    token_ref,
    gain_ref,
    coef_ref,
    x_ref,
    cot_ref,
    out_s,
    grad_s,
    sem,
):
    hw, d = w_ref.shape
    wide = hw + d
    copies = [
        pltpu.make_async_copy(cot_hbm, cot_ref, sem.at[0]),
        pltpu.make_async_copy(x_hbm, x_ref, sem.at[1]),
    ]
    for cp in copies:
        cp.start()
    swap = row_swap(slots, frames, False)
    hid = hidden_column(hid_ref[...], slots, frames, False) > 0.5
    delta = dot_nn(swap, recv_ref[:, hw:wide])
    ctx = dot_nn(swap, recv_ref[:, :hw]).astype(BF)
    copies[0].wait()
    grad_s[...] = jnp.where(hid, 0.0, cot_ref[...].astype(F32) + delta).astype(BF)
    stores = [
        pltpu.make_async_copy(grad_s, grad_hbm, sem.at[2]),
        pltpu.make_async_copy(out_s, out_hbm, sem.at[3]),
    ]
    stores[0].start()
    attn = dot_nn(ctx, w_ref[...]).astype(BF)
    copies[1].wait()
    x_in = jnp.where(hid, tok_ref[...].astype(F32), x_ref[...].astype(F32))
    out_s[...] = (x_in + attn.astype(F32)).astype(BF)
    stores[1].start()
    if shared:
        total = jnp.zeros((32, LANES), F32)
        for j in range(recv_ref.shape[0] // 32):
            total = total + recv_ref[j * 32 : (j + 1) * 32, wide:].astype(F32)
        total = total[:16] + total[16:]
        parts = d // LANES
        for c in range(parts):
            here = pl.ds(c * LANES, LANES)
            token_ref[here] = total[c : c + 1].reshape(LANES)
            gain_ref[here] = total[parts + c : parts + c + 1].reshape(LANES)
        coef_ref[...] = total[2 * parts : 2 * parts + 1, : coef_ref.shape[1]]
    else:
        for c in range(d // hw):
            here = pl.ds(c * hw, hw)
            token_ref[here] = sums_ref[c : c + 1].reshape(hw)
            gain_ref[here] = sums_ref[2 + c : 3 + c].reshape(hw)
        coef_ref[...] = sums_ref[4:5, : coef_ref.shape[1]]
    for cp in stores:
        cp.wait()


def split_two(value):
    high = value.astype(BF)
    return high, (value - high.astype(F32)).astype(BF)


def merge_kernel(
    nf, sb, guests, wide, head_rows, flag_ref, buf_ref, own_ref, got_ref, core_ref, cross_ref, out_ref, sums_ref
):
    hw = got_ref.shape[1]
    segs = wide // hw
    seg_rows = nf * guests
    total_rows = out_ref.shape[0]
    i = iota((8, got_ref.shape[0]), 0)
    k = iota((8, got_ref.shape[0]), 1) - segs * seg_rows
    pick = ((i < SUMS) & ((k == i) | (k == i + SUMS))).astype(BF)
    sums = (own_ref[...] + dot_nn(pick, got_ref[...])) + (core_ref[...] + cross_ref[...])
    sums_ref[...] = sums
    if out_ref.shape[1] > wide:
        flat = jnp.concatenate(
            [sums[a : a + 1, c : c + LANES] for a in range(SUMS) for c in range(0, hw, LANES)]
            + [jnp.zeros((1, LANES), F32)],
            axis=0,
        )
        block = jnp.concatenate(split_two(flat), axis=0)
        for j in range(total_rows // block.shape[0]):
            out_ref[j * block.shape[0] : (j + 1) * block.shape[0], wide:] = block
    r = iota((head_rows, 1), 0)
    slot = (r // (nf * sb)) * sb + r % sb
    from_row = ((r // sb) % nf) * guests + slot
    guest = jnp.where(slot < guests, 1, 0)
    take = guest * jnp.where(flag_ref[0] == 1, 0, 1)
    for s in range(segs):
        source = jnp.where(guest == 1, s * seg_rows + from_row, 1 << 20)
        pick = (iota((head_rows, got_ref.shape[0]), 1) == source).astype(BF)
        here = slice(s * hw, (s + 1) * hw)
        out_ref[:head_rows, here] = jnp.where(
            take == 1, dot_nn(pick, got_ref[...]), buf_ref[:head_rows, here].astype(F32)
        ).astype(BF)


def local_tables(half_slots, guests, heads, first_half, clip_ref, kind_ref, adj_ref, adj_s):
    total = clip_ref.shape[1]
    kind_count, joint_max = adj_ref.shape[0], adj_ref.shape[1]
    keys = half_slots + EP
    adj_s[...] = jnp.zeros(adj_s.shape, F32)
    adj_s[:, :joint_max, :joint_max] = adj_ref[...].astype(F32)
    i = iota((keys, 1), 0)
    slot = jnp.where(i < half_slots, i + jnp.where(first_half == 1, 0, half_slots), i)
    valid = ((i < half_slots) & (i >= jnp.where(first_half == 1, 0, guests))) | (
        (i >= half_slots) & (i < jnp.where(first_half == 1, half_slots + guests, 0))
    )
    lanes = iota((keys, total), 1)
    at = lanes == slot
    clip_row = clip_ref[...].astype(F32)
    clip = jnp.sum(jnp.where(at, clip_row, 0.0), axis=1, keepdims=True)
    kind = jnp.sum(jnp.where(at, kind_ref[...].astype(F32), 0.0), axis=1, keepdims=True)
    first = jnp.min(
        jnp.where(clip_row == clip, lanes.astype(F32), 1.0 * total), axis=1, keepdims=True
    )
    joint = slot.astype(F32) - first
    clip = jnp.where(valid, clip, -1.0 - i.astype(F32))
    pick = (iota((keys, adj_s.shape[1]), 1).astype(F32) == joint).astype(BF)
    picked = jnp.zeros((keys, adj_s.shape[2]), F32)
    for k in range(kind_count):
        picked = picked + jnp.where(kind == 1.0 * k, dot_nn(pick, adj_s[k].astype(BF)), 0.0)
    link = dot_nt(pick, picked.astype(BF))
    eye = iota((keys, keys), 0) == iota((keys, keys), 1)
    clip_across = jnp.sum(jnp.where(eye, clip, 0.0), axis=0, keepdims=True)
    link = jnp.where(clip == clip_across, link, -1.0)
    tile = (iota((EP, heads * EQ), 1) % EQ == iota((EP, heads * EQ), 0)).astype(BF)
    return link[:, :half_slots], dot_nn(link[:, half_slots:].astype(BF), tile)


def stage_kernel(
    half_slots, guests, heads, nf, sb, count, flag_ref, send_ref, clip_ref, kind_ref, adj_ref, *refs
):
    link_ref, link_e_ref = refs[:2]
    ext_refs = refs[2 : 2 + count]
    adj_s = refs[-1]

    @pl.when(flag_ref[1] == count)
    def _():
        for j, ref in enumerate(ext_refs):
            ext_rows, hw = ref.shape
            pieces = [
                send_ref[(j * nf + f) * sb : (j * nf + f + 1) * sb, c : c + hw].astype(F32)[:guests]
                for c in range(0, send_ref.shape[1], hw)
                for f in range(nf)
            ]
            pieces.append(jnp.zeros((ext_rows - len(pieces) * guests, hw), F32))
            ref[...] = jnp.concatenate(pieces, axis=0).astype(BF)

    link, link_e = local_tables(
        half_slots, guests, heads, flag_ref[0], clip_ref, kind_ref, adj_ref, adj_s
    )
    link_ref[...] = link
    link_e_ref[...] = link_e


def frame_kernel(
    blocks,
    nf,
    sb,
    guests,
    *refs,
):
    (
        ext_ref,
        recv_ref,
        flag_ref,
        link_ref,
        link_e_ref,
        coef_ref,
        coef_e_ref,
        tok_ref,
        gain_ref,
        token_in_ref,
        w_hbm,
        out_s,
        pay_ref,
        sums_ref,
        x_s,
        xn_s,
        inv_s,
        hid_s,
        q_s,
        k_s,
        v_s,
        g_s,
        gu_s,
        gk_s,
        gv_s,
        ctx_s,
        gn_s,
        w_ref,
        sem,
    ) = refs
    d = gain_ref.shape[1]
    hw = w_ref.shape[1] // 3
    main = blocks * sb
    keys = main + EP
    rows = nf * main
    all_rows = rows + nf * EP
    heads = coef_ref.shape[0]
    hs = hw // heads
    seg_rows = nf * guests
    aligned = sb % 16 == 0

    copies = [pltpu.make_async_copy(w_hbm, w_ref, sem.at[0])]
    for cp in copies:
        cp.start()
    link = link_ref[...]
    link_e = link_e_ref[...]

    def gather(value):
        if aligned:
            return jnp.concatenate(
                [
                    value[(j * nf + f) * sb : (j * nf + f + 1) * sb]
                    for f in range(nf)
                    for j in range(blocks)
                ],
                axis=0,
            )
        r = iota((rows, 1), 0)
        slot = r % main
        source = ((slot // sb) * nf + r // main) * sb + slot % sb
        return dot_nn((iota((rows, rows), 1) == source).astype(BF), value).astype(BF)

    def scatter(value):
        if aligned:
            return jnp.concatenate(
                [
                    value[f * main + j * sb : f * main + (j + 1) * sb]
                    for j in range(blocks)
                    for f in range(nf)
                ],
                axis=0,
            )
        r = iota((rows, 1), 0)
        pair = r // sb
        source = (pair % nf) * main + (pair // nf) * sb + r % sb
        return dot_nn((iota((rows, rows), 1) == source).astype(BF), value).astype(BF)

    er = iota((nf * EP, 1), 0)
    guest_row = jnp.where(er % EP < guests, (er // EP) * guests + er % EP, 1 << 20)

    def guest_segment(seg):
        pick = (iota((nf * EP, ext_ref.shape[0]), 1) == guest_row + seg * seg_rows).astype(BF)
        return dot_nn(pick, ext_ref[...]).astype(BF)

    for c in range(d // hw):
        x_s[rows:, c * hw : (c + 1) * hw] = guest_segment(c)
    x_s[:rows] = gather(recv_ref[:, :d])
    tok = tok_ref[...]
    gain = gain_ref[...]
    for a in range(0, all_rows, 16):
        xb = x_s[a : a + 16]
        hid = xb[:, 0:1].astype(F32) > 0.5 * HIDDEN_MARK
        xf = jnp.where(hid, tok.astype(F32), xb.astype(F32))
        x_s[a : a + 16] = xf.astype(BF)
        inv = 1.0 / jnp.sqrt(jnp.mean(xf * xf, axis=1, keepdims=True) + 1e-6)
        inv_s[a : a + 16] = jnp.broadcast_to(inv, (16, 128))
        hid_s[a : a + 16] = jnp.broadcast_to(jnp.where(hid, 1.0, 0.0), (16, 128))
        xn_s[a : a + 16] = (xf * inv * gain).astype(BF)

    for cp in copies:
        cp.wait()
    for c, ref in enumerate((q_s, k_s, v_s)):
        part = dot_nn(xn_s[...], w_ref[:, c * hw : (c + 1) * hw]).astype(BF)
        if c == 0:
            part = part * BF(hs**-0.5)
        for f in range(nf):
            ref[f, :main] = part[f * main : (f + 1) * main]
            ref[f, main:] = part[rows + f * EP : rows + (f + 1) * EP]

    gc_main = gather(recv_ref[:, d:])
    gc_ext = guest_segment(d // hw)
    for f in range(nf):
        g_s[f, :main] = gc_main[f * main : (f + 1) * main]
        g_s[f, main:] = gc_ext[f * EP : (f + 1) * EP]

    own = (iota((heads * EQ, hw), 0) // EQ == iota((heads * EQ, hw), 1) // hs)
    bias_e = jnp.where(link_e < 0, MASKED, coef_e_ref[...] * link_e)
    coef_lanes = jnp.zeros((1, heads * EQ), F32)

    def spread(value):
        tall = jnp.concatenate([value] * heads, axis=0)
        return jnp.where(own, tall, jnp.zeros_like(tall))

    def fold(value):
        kept = jnp.where(own, value, 0.0)
        total = kept[0:EQ]
        for h in range(1, heads):
            total = total + kept[h * EQ : (h + 1) * EQ]
        return jnp.concatenate([total, jnp.zeros((EP - EQ, hw), F32)], axis=0)

    for f in range(nf):
        guest_rows = slice(rows + f * EP, rows + (f + 1) * EP)
        q_e = spread(q_s[f, main:].astype(F32)[:EQ]).astype(BF)
        g_e = spread(g_s[f, main:].astype(F32)[:EQ]).astype(BF)
        s_t = dot_nt(k_s[f], q_e) + bias_e
        p_t = jnp.exp(s_t - jnp.max(s_t, axis=0, keepdims=True))
        w_t = p_t * (1.0 / jnp.sum(p_t, axis=0, keepdims=True))
        w_b = w_t.astype(BF)
        gw = dot_nt(v_s[f], g_e)
        ds = w_t * (gw - jnp.sum(w_t * gw, axis=0, keepdims=True))
        coef_lanes = coef_lanes + jnp.sum(ds * link_e, axis=0, keepdims=True)
        ds_b = ds.astype(BF)
        ctx_s[guest_rows] = fold(dot_tn(w_b, v_s[f])).astype(BF)
        gu_s[guest_rows, :hw] = fold(dot_tn(ds_b, k_s[f]) * hs**-0.5).astype(BF)
        gk_s[f] = dot_nn(ds_b, q_e)
        gv_s[f] = dot_nn(w_b, g_e)

    lane = iota((1, 128), 1)
    coef_out = jnp.zeros((1, 128), F32)
    for h in range(heads):
        coef_out = coef_out + jnp.where(
            lane == h, jnp.sum(coef_lanes[:, h * EQ : (h + 1) * EQ]), 0.0
        )

    pair_w = 2 * hs
    low = iota((main, pair_w), 1) < hs
    zero = jnp.zeros((main, pair_w), BF)
    for p in range(heads // 2):
        cols = slice(p * pair_w, (p + 1) * pair_w)
        k_cols = slice(hw + p * pair_w, hw + (p + 1) * pair_w)
        v_cols = slice(2 * hw + p * pair_w, 2 * hw + (p + 1) * pair_w)
        bias = jnp.concatenate(
            [
                jnp.where(link < 0, MASKED, coef_ref[2 * p] * link),
                jnp.where(link < 0, MASKED, coef_ref[2 * p + 1] * link),
            ],
            axis=1,
        )
        ds_sum = jnp.zeros((keys, 2 * main), F32)
        for f in range(nf):
            main_rows = slice(f * main, (f + 1) * main)
            guest_rows = slice(rows + f * EP, rows + (f + 1) * EP)
            k = k_s[f, :, cols]
            v = v_s[f, :, cols]
            q = q_s[f, :main, cols]
            g = g_s[f, :main, cols]
            qq = jnp.concatenate([jnp.where(low, q, zero), jnp.where(low, zero, q)], axis=0)
            gg = jnp.concatenate([jnp.where(low, g, zero), jnp.where(low, zero, g)], axis=0)
            s_t = dot_nt(k, qq) + bias
            p_t = jnp.exp(s_t - jnp.max(s_t, axis=0, keepdims=True))
            w_t = p_t * (1.0 / jnp.sum(p_t, axis=0, keepdims=True))
            w_b = w_t.astype(BF)
            gw = dot_nt(v, gg)
            ds = w_t * (gw - jnp.sum(w_t * gw, axis=0, keepdims=True))
            ds_sum = ds_sum + ds
            ds_b = ds.astype(BF)
            ctx_t = dot_tn(v, w_b)
            ctx_t = jnp.concatenate([ctx_t[:hs, :main], ctx_t[hs:, main:]], axis=0)
            ctx_s[main_rows, cols] = ctx_t.T.astype(BF)
            gq_t = dot_tn(k, ds_b)
            gq_t = jnp.concatenate([gq_t[:hs, :main], gq_t[hs:, main:]], axis=0)
            gu_s[main_rows, cols] = (gq_t.T * hs**-0.5).astype(BF)
            gk = (gk_s[f, :, cols] + dot_nn(ds_b, qq)).astype(BF)
            gu_s[main_rows, k_cols] = gk[:main]
            gu_s[guest_rows, k_cols] = gk[main:]
            gv = (gv_s[f, :, cols] + dot_nn(w_b, gg)).astype(BF)
            gu_s[main_rows, v_cols] = gv[:main]
            gu_s[guest_rows, v_cols] = gv[main:]
        lanes = jnp.sum(ds_sum * jnp.concatenate([link, link], axis=1), axis=0, keepdims=True)
        coef_out = coef_out + jnp.where(lane == 2 * p, jnp.sum(lanes[:, :main]), 0.0)
        coef_out = coef_out + jnp.where(lane == 2 * p + 1, jnp.sum(lanes[:, main:]), 0.0)

    out_s[:, :hw] = scatter(ctx_s[:rows])
    gn_s[...] = dot_nt(gu_s[...], w_ref[...])
    guest_limit = jnp.where(flag_ref[0] == 1, guests, 0)
    main_limit = jnp.where(flag_ref[0] == 1, 0, guests)
    place = iota((16, 1), 0)
    token_sum = jnp.zeros((8, d), F32)
    gain_sum = jnp.zeros((8, d), F32)
    for a in range(0, all_rows, 16):
        gn = gn_s[a : a + 16]
        inv = inv_s[a : a + 16, 0:1]
        x_unit = x_s[a : a + 16].astype(F32) * inv
        g_gain = gn * gain
        gx = gn * x_unit
        mean_gx = jnp.mean(gx * gain, axis=1, keepdims=True)
        delta = (g_gain - x_unit * mean_gx) * inv
        if a >= rows:
            x_s[a : a + 16] = delta.astype(BF)
            valid = jnp.where(place < guest_limit, 1.0, 0.0)
        elif aligned:
            f, j = a // main, (a % main) // sb
            at = (j * nf + f) * sb + a % sb
            out_s[at : at + 16, hw : hw + d] = delta.astype(BF)
            valid = jnp.where(place + a % main >= main_limit, 1.0, 0.0)
        else:
            x_s[a : a + 16] = delta.astype(BF)
            valid = jnp.where(place + a % main >= main_limit, 1.0, 0.0)
        hid_valid = hid_s[a : a + 16, 0:1] * valid
        if a >= rows or a % main < guests:
            gx = gx * valid
        delta = delta * hid_valid
        gain_sum = gain_sum + (gx[:8] + gx[8:])
        token_sum = token_sum + (delta[:8] + delta[8:])
    if not aligned:
        out_s[:, hw : hw + d] = scatter(x_s[:rows])
    gain_sum = jnp.sum(gain_sum, axis=0, keepdims=True)
    token_sum = token_in_ref[...] + jnp.sum(token_sum, axis=0, keepdims=True)
    coef_row = jnp.concatenate([coef_out, jnp.zeros((1, hw - coef_out.shape[1]), F32)], axis=1)
    sums = jnp.concatenate(
        [token_sum[:, :hw], token_sum[:, hw:], gain_sum[:, :hw], gain_sum[:, hw:], coef_row]
        + [jnp.zeros((8 - SUMS, hw), F32)],
        axis=0,
    )
    high, low_part = split_two(sums)
    sums_ref[...] = high.astype(F32) + low_part.astype(F32)
    pair = jnp.concatenate([high.astype(F32), low_part.astype(F32)], axis=0).astype(BF)
    orow = iota((pay_ref.shape[0], 1), 0)
    k = orow - (1 + d // hw) * seg_rows
    source = jnp.where(
        k < 0, 1 << 20, jnp.where(k < SUMS, k, jnp.where(k < 2 * SUMS, k - SUMS + 8, 1 << 20))
    )
    total = dot_nn((iota((pay_ref.shape[0], 16), 1) == source).astype(BF), pair)
    inner = orow % seg_rows
    for s in range(1 + d // hw):
        piece = ctx_s[rows:] if s == 0 else x_s[rows:, (s - 1) * hw : s * hw]
        source = jnp.where(
            orow // seg_rows == s, (inner // guests) * EP + inner % guests, 1 << 20
        )
        total = total + dot_nn(
            (iota((pay_ref.shape[0], nf * EP), 1) == source).astype(BF), piece
        )
    pay_ref[...] = total.astype(BF)


VMEM = pl.BlockSpec(memory_space=pltpu.VMEM)
SMEM = pl.BlockSpec(memory_space=pltpu.SMEM)
HBM = pl.BlockSpec(memory_space=pl.ANY)


def on_device(
    n,
    joints_x,
    cotangent,
    hidden,
    stream_clip,
    stream_kind,
    adjacency,
    mask_token,
    norm_gain,
    w_qkv,
    w_out,
    graph_coef,
):
    _, slots, frames, d = joints_x.shape
    hw = w_out.shape[0]
    heads = graph_coef.shape[0]
    total = stream_clip.shape[1]
    half = n // 2
    nf = frames // half
    half_slots = total // 2
    guests = BIG_CLIP - half_slots
    rows = slots * frames
    wide = d + hw
    segs = wide // hw
    me = lax.axis_index("seq")
    first_half = me < half
    groups = [list(range(half)), list(range(half, n))]

    x = joints_x.reshape(rows, d)
    cot = cotangent.reshape(rows, d)
    hid = hidden[0]
    tok = mask_token.reshape(1, d)
    flag = jnp.stack([first_half.astype(jnp.int32), me])

    send, token_cot = pl.pallas_call(
        functools.partial(send_kernel, slots, frames),
        out_shape=(
            jax.ShapeDtypeStruct((rows, wide), BF),
            jax.ShapeDtypeStruct((1, d), F32),
        ),
        in_specs=[HBM] * 4,
        out_specs=(VMEM, VMEM),
        scratch_shapes=[
            pltpu.VMEM((rows, d), BF),
            pltpu.VMEM((rows, d), BF),
            pltpu.VMEM(hid.shape, jnp.int32),
            pltpu.VMEM(w_out.shape, BF),
            pltpu.SemaphoreType.DMA((4,)),
        ],
        compiler_params=pltpu.CompilerParams(vmem_limit_bytes=SEND_LIMIT),
        name="send",
    )(x, cot, hid, w_out)

    recv = lax.all_to_all(send, "seq", 0, 0, axis_index_groups=groups, tiled=True)

    def buffer_row(f, e):
        return ((e // slots) * nf + f) * slots + e % slots

    run = min(slots, guests)
    starts = [
        (buffer_row(f, e), min(run, guests - e)) for f in range(nf) for e in range(0, guests, run)
    ]
    ext_rows = -(-segs * nf * guests // 16) * 16
    direct = slots >= guests and slots % 16 == 0 and half <= 8
    joint_pad = -(-adjacency.shape[1] // 256) * 256
    keys = half_slots + EP
    count = half if direct else 0
    link, link_e, *packed = pl.pallas_call(
        functools.partial(stage_kernel, half_slots, guests, heads, nf, slots, count),
        out_shape=(
            jax.ShapeDtypeStruct((keys, half_slots), F32),
            jax.ShapeDtypeStruct((keys, heads * EQ), F32),
        )
        + (jax.ShapeDtypeStruct((ext_rows, hw), BF),) * count,
        in_specs=[SMEM] + [VMEM] * 4,
        out_specs=(VMEM,) * (2 + count),
        scratch_shapes=[pltpu.VMEM((adjacency.shape[0], joint_pad, joint_pad), F32)],
        compiler_params=pltpu.CompilerParams(vmem_limit_bytes=VMEM_LIMIT),
        name="stage",
    )(flag, send, stream_clip, stream_kind, adjacency)
    if direct:
        ext = lax.ppermute(packed[0], "seq", [(half, 0)])
        for j in range(1, half):
            ext = ext + lax.ppermute(packed[j], "seq", [(half, j)])
    else:
        pieces = [
            recv[a : a + c, s * hw : (s + 1) * hw] for s in range(segs) for a, c in starts
        ]
        pieces.append(jnp.zeros((ext_rows - segs * nf * guests, hw), BF))
        ext = lax.ppermute(
            jnp.concatenate(pieces, axis=0), "seq", [(half + i, i) for i in range(half)]
        )

    main = half_slots
    all_rows = rows + nf * EP
    block_rows = nf * slots
    shared = block_rows % 32 == 0
    out_wide = wide + (LANES if shared else 0)
    head_rows = -(-guests // slots) * block_rows
    head_rows = -(-head_rows // 16) * 16
    pay_rows = -(-(segs * nf * guests + 2 * SUMS) // 8) * 8
    per_frame = (nf, main + EP, hw)
    out, pay, own_sums = pl.pallas_call(
        functools.partial(frame_kernel, half, nf, slots, guests),
        out_shape=(
            jax.ShapeDtypeStruct((rows, out_wide), BF),
            jax.ShapeDtypeStruct((pay_rows, hw), BF),
            jax.ShapeDtypeStruct((8, hw), F32),
        ),
        in_specs=[VMEM, VMEM, SMEM, VMEM, VMEM, SMEM, VMEM, VMEM, VMEM, VMEM, HBM],
        out_specs=(VMEM, VMEM, VMEM),
        scratch_shapes=[
            pltpu.VMEM((all_rows, d), BF),
            pltpu.VMEM((all_rows, d), BF),
            pltpu.VMEM((all_rows, 128), F32),
            pltpu.VMEM((all_rows, 128), F32),
            pltpu.VMEM(per_frame, BF),
            pltpu.VMEM(per_frame, BF),
            pltpu.VMEM(per_frame, BF),
            pltpu.VMEM(per_frame, BF),
            pltpu.VMEM((all_rows, 3 * hw), BF),
            pltpu.VMEM(per_frame, F32),
            pltpu.VMEM(per_frame, F32),
            pltpu.VMEM((all_rows, hw), BF),
            pltpu.VMEM((all_rows, d), F32),
            pltpu.VMEM((d, 3 * hw), BF),
            pltpu.SemaphoreType.DMA((3,)),
        ],
        compiler_params=pltpu.CompilerParams(vmem_limit_bytes=FRAMES_LIMIT),
        name="frames",
    )(
        ext,
        recv,
        flag,
        link,
        link_e,
        graph_coef,
        jnp.repeat(graph_coef, EQ).reshape(1, heads * EQ),
        tok,
        norm_gain.reshape(1, d),
        token_cot,
        w_qkv,
    )

    flip = [(i, (i + half) % n) for i in range(n)]
    got = lax.ppermute(pay, "seq", flip)
    core = lax.ppermute(own_sums, "dp", [(0, 1), (1, 0)])
    cross = lax.ppermute(
        own_sums, ("dp", "seq"), [(c * n + i, (1 - c) * n + j) for c in range(2) for i, j in flip]
    )
    merged, sums = pl.pallas_call(
        functools.partial(merge_kernel, nf, slots, guests, wide, head_rows),
        out_shape=(
            jax.ShapeDtypeStruct((rows, out_wide), BF),
            jax.ShapeDtypeStruct((8, hw), F32),
        ),
        in_specs=[SMEM] + [VMEM] * 5,
        out_specs=(VMEM, VMEM),
        input_output_aliases={1: 0},
        compiler_params=pltpu.CompilerParams(vmem_limit_bytes=VMEM_LIMIT),
        name="merge",
    )(flag, out, own_sums, got, core, cross)
    returned = lax.all_to_all(merged, "seq", 0, 0, axis_index_groups=groups, tiled=True)

    if not shared:
        k = 1
        while k < half:
            sums = sums + lax.ppermute(sums, "seq", [(i, i ^ k) for i in range(n)])
            k *= 2

    layer_out, grad_x, token, gain, coef = pl.pallas_call(
        functools.partial(final_kernel, slots, frames, shared),
        out_shape=(
            jax.ShapeDtypeStruct((rows, d), BF),
            jax.ShapeDtypeStruct((rows, d), BF),
            jax.ShapeDtypeStruct((d,), F32),
            jax.ShapeDtypeStruct((d,), F32),
            jax.ShapeDtypeStruct((1, heads), F32),
        ),
        in_specs=[VMEM, HBM, HBM, VMEM, VMEM, VMEM, VMEM],
        out_specs=(HBM, HBM, VMEM, VMEM, VMEM),
        scratch_shapes=[
            pltpu.VMEM((rows, d), BF),
            pltpu.VMEM((rows, d), BF),
            pltpu.VMEM((rows, d), BF),
            pltpu.VMEM((rows, d), BF),
            pltpu.SemaphoreType.DMA((4,)),
        ],
        compiler_params=pltpu.CompilerParams(vmem_limit_bytes=VMEM_LIMIT),
        name="final",
    )(returned, x, cot, hid, tok, w_out, sums)

    shape = (1, slots, frames, d)
    return (
        layer_out.reshape(shape),
        grad_x.reshape(shape),
        token,
        gain,
        coef.reshape(-1),
    )


def solution(mesh):
    return jax.shard_map(
        functools.partial(on_device, mesh.shape["seq"]),
        mesh=mesh,
        in_specs=(
            P("dp", "seq", None, None),
            P("dp", "seq", None, None),
            P("dp", "seq", None),
            P("dp", None),
            P("dp", None),
            P(),
            P(),
            P(),
            P(),
            P(),
            P(),
        ),
        out_specs=(P("dp", "seq", None, None), P("dp", "seq", None, None), P(), P(), P()),
        check_vma=False,
    )
```

time: 195 us -> 76.1 us (0.39)
  matrix products: 45.6 us -> 0 us
  waiting for transfers between devices: 41.4 us -> 14.1 us
  local copies, waits for them, and re-layouts: 26.9 us -> 0.23 us
  Pallas kernels: 0 us -> 23.7 us
  blocking collectives: 40.2 us -> 21 us
  other arithmetic: 15.6 us -> 0.1 us
  starting transfers between devices: 23.2 us -> 15.5 us
    psum x1 -> x0, blocking collectives: 40.2 us -> none  [on_device(): lax.psum((token_term, gain_term, coef_term), ('dp', 'seq'))]
    dot_general x11 -> x0, matrix products: 36.6 us -> none  [the longest x9 34.9 us: product(): return jnp.einsum(form, left, right, preferred_element_type=jnp.float32)]
    all_to_all x4 -> x1, waiting for transfers between devices: 41.4 us -> 8.25 us  [on_device(): lax.all_to_all(send, 'seq', 0, 0, axis_index_groups=groups, tiled=True)]
    pallas_call x0 -> x5, Pallas kernels: none -> 23.7 us  [the longest x1 13.8 us: on_device(): pl.pallas_call(functools.partial(frame_kernel, half, nf, slots, guests),...]
    unnamed x47 -> x24, local copies, waits for them, and re-layouts: 23 us -> 0.07 us
    all_to_all x0 -> x1, blocking collectives: none -> 21 us  [on_device(): lax.all_to_all(merged, 'seq', 0, 0, axis_index_groups=groups, tiled=True)]
    all_to_all x4 -> x1, starting transfers between devices: 23.2 us -> 6.33 us  [on_device(): lax.all_to_all(send, 'seq', 0, 0, axis_index_groups=groups, tiled=True)]
    convert_element_type x5 -> x0, other arithmetic: 9.4 us -> none  [the longest x1 2.58 us: normalize(): x_normed = (x_unit * norm_gain).astype(jnp.bfloat16)]
  transfers between devices with their start and end apart: 4 -> 12, of which waited for: 4 -> 4; matrix products, arithmetic and copies ran while one was open for 18% -> 0% of each run, Pallas kernels for 0% -> 2%
where the time goes in v2:
time: 76.1 us; the launch traced here: 75.7 us
  Pallas kernels  23.7 us (31%)
  blocking collectives  21 us (28%)
  starting transfers between devices  15.5 us (20%)
  waiting for transfers between devices  14.1 us (19%)
  between operations  1.1 us (1%)
    all_to_all x1, blocking collectives, on_device(): lax.all_to_all(merged, 'seq', 0, 0, axis_index_groups=groups, tiled=True)  21 us
    pallas_call x1, Pallas kernels, on_device(): pl.pallas_call(functools.partial(frame_kernel, half, nf, slots, guests),...  13.8 us
    all_to_all x1, waiting for transfers between devices, on_device(): lax.all_to_all(send, 'seq', 0, 0, axis_index_groups=groups, tiled=True)  8.25 us
    all_to_all x1, starting transfers between devices, on_device(): lax.all_to_all(send, 'seq', 0, 0, axis_index_groups=groups, tiled=True)  6.33 us
    ppermute x7, starting transfers between devices, on_device(): ext = ext + lax.ppermute(packed[j], 'seq', [(half, j)])  4.81 us
    pallas_call x1, Pallas kernels, on_device(): pl.pallas_call(functools.partial(send_kernel, slots, frames), out_shape=(...  4.43 us
    pallas_call x1, Pallas kernels, on_device(): pl.pallas_call(functools.partial(final_kernel, slots, frames, shared), ou...  3.57 us
    ppermute x1, waiting for transfers between devices, on_device(): ext = lax.ppermute(packed[0], 'seq', [(half, 0)])  3.19 us
  transfers between devices with their start and end apart: 12, of which 4 were waited for; matrix products, arithmetic and copies ran while one was open for 0% of the time, Pallas kernels for 2%

profile of v2, /device:TPU:0, one launch (start us, length us, event | category | flops | bytes accessed | tf_op | source)
XLA Modules:
  0.0 75.7 jit_solution(16750880114240496383)
XLA Ops:
  0.6 4.4 %send.1 = (bf16[256,2304]{1,0:T(8,128)(2,1)}, f32[1,1536]{1,0:T(1,128)}) custom-call(bf16[256,1536]{1,0:T(8,128)(2,1)} %bitcast.16, bf16[256,1536]{1,0:T(8,128)(2,1)} %bitcast.18, s32[16,16]{1,0:T(8,128)} %bitcast.20, bf16[768,1536]{1,0:T(8,128)(2,1)} %w_ref.1), custom_call_target="tpu_custom_call" | custom-call | tf_op jit(solution)/shard_map/send/pallas_call | solution.py:584
  5.1 0.0 copy-start.1
  5.1 0.0 copy-start.4
  5.1 0.0 copy-start.8
  5.1 0.0 copy-start.9
  5.1 6.3 %all-to-all-start = ((bf16[8,32,2304]{2,1,0:T(8,128)(2,1)}), bf16[8,32,2304]{2,1,0:T(8,128)(2,1)S(1)}, u32[]{:S(2)}, u32[]{:S(2)}) async-start(bf16[8,32,2304]{2,1,0:T(8,128)(2,1)} %bitcast.15), calls=%async_computation | async-start | bytes 2359296 | tf_op jit(solution)/shard_map/all_to_all | solution.py:603
  11.4 0.0 copy-start.10
  11.5 0.0 copy-start.7
  11.5 0.0 copy-start.6
  11.5 0.1 pad_add_fusion.flag_ref.refs_2_
  11.6 0.0 copy-done.1
  11.6 0.0 copy-done.4
  11.6 0.0 copy-done.8
  11.6 0.0 copy-done.9
  11.6 1.2 %stage.1 = (f32[144,128]{1,0:T(8,128)S(1)}, f32[144,96]{1,0:T(8,128)S(1)}, bf16[32,768]{1,0:T(8,128)(2,1)S(1)}, bf16[32,768]{1,0:T(8,128)(2,1)S(1)}, bf16[32,768...) custom-call(s32[2]{0:T(128)S(1)} %pad_add_fusion.flag_ref.refs_2_, ...), custom_call_target="tpu_custom_call" | custom-call | tf_op jit(solution)/shard_map/stage/pallas_call | solution.py:617
  12.8 1.3 %collective-permute-start = (bf16[32,768]{1,0:T(8,128)(2,1)S(1)}, bf16[32,768]{1,0:T(8,128)(2,1)S(1)}, u32[]{:S(2)}, u32[]{:S(2)}) collective-permute-start(bf16[32,768]{1,0:T(8,128)(2,1)S(1)} %get-tuple-element.28), channel_id=1, source_target_pairs={{8,0},{24,16}} | collective-permute-start | bytes 147464 | tf_op jit(solution)/shard_map/ppermute | solution.py:631
  14.1 0.7 collective-permute-start.1
  14.8 0.7 collective-permute-start.2
  15.4 0.7 collective-permute-start.3
  16.1 0.7 collective-permute-start.4
  16.8 3.2 %collective-permute-done = bf16[32,768]{1,0:T(8,128)(2,1)S(1)} collective-permute-done((bf16[32,768]{1,0:T(8,128)(2,1)S(1)}, bf16[32,768]{1,0:T(8,128)(2,1)S(1)}, u32[]{:S(2)}, u32[]{:S(2)}) %collective-permute-start) | collective-permute-done | bytes 49184 | tf_op jit(solution)/shard_map/ppermute | solution.py:631
  20.0 0.7 collective-permute-start.5
  20.6 0.0 collective-permute-done.1
  20.6 0.7 collective-permute-start.6
  21.3 0.0 collective-permute-done.2
  21.3 0.8 %collective-permute-start.7 = (bf16[32,768]{1,0:T(8,128)(2,1)S(1)}, bf16[32,768]{1,0:T(8,128)(2,1)S(1)}, u32[]{:S(2)}, u32[]{:S(2)}) collective-permute-start(bf16[32,768]{1,0:T(8,128)(2,1)S(1)} %get-tuple-element.35), channel_id=1, source_target_pairs={{8,7},{24,23}} | collective-permute-start | bytes 147464 | tf_op jit(solution)/shard_map/ppermute | solution.py:633
  22.2 0.0 copy-done.11
  22.2 0.0 copy-done.10
  22.2 0.1 broadcast_in_dim.3
  22.3 0.1 reshape_reshape.3.refs_6_
  22.4 0.0 collective-permute-done.3
  22.4 0.0 collective-permute-done.4
  22.4 0.0 collective-permute-done.5
  22.4 0.0 collective-permute-done.6
  22.4 0.0 collective-permute-done.7
  22.5 8.3 %all-to-all-done = bf16[8,32,2304]{2,1,0:T(8,128)(2,1)S(1)} async-done(((bf16[8,32,2304]{2,1,0:T(8,128)(2,1)}), bf16[8,32,2304]{2,1,0:T(8,128)(2,1)S(1)}, u32[]{:S(2)}, u32[]{:S(2)}) %all-to-all-start) | async-done | bytes 1179680 | tf_op jit(solution)/shard_map/all_to_all | solution.py:603
  30.7 13.8 %frames.1 = (bf16[256,2560]{1,0:T(8,128)(2,1)S(1)}, bf16[40,768]{1,0:T(8,128)(2,1)S(1)}, f32[8,768]{1,0:T(8,128)S(1)}) custom-call(bf16[32,768]{1,0:T(8,128)(2,1)S(1)} %add_add_fusion.refs_0_, bf16[256,2304]{1,0:T(8,128)(2,1)S(1)} %bitcast.14, s32[2]{0:T(128)S(1)} %pad_add_fusion.flag_ref.refs_2_, f32[144,128]{1,0:T(8,128)S(1)} %get-tuple-element.36.refs_3_, ...), custom_call_target="tpu_custom_call" | custom-call | tf_op jit(solution)/shard_map/frames/pallas_call | solution.py:652
  44.5 0.1 collective-permute-start.8
  44.6 0.9 %collective-permute-start.10 = (f32[8,768]{1,0:T(8,128)S(1)}, f32[8,768]{1,0:T(8,128)S(1)}, u32[]{:S(2)}, u32[]{:S(2)}) collective-permute-start(f32[8,768]{1,0:T(8,128)S(1)} %get-tuple-element.40.own_ref), channel_id=1, source_target_pairs={{0,24},{1,25},{2,26},{3,27},{4,28},{5,29},{6,30},{7,31},{8,16},{9,... | collective-permute-start | bytes 73736 | tf_op jit(solution)/shard_map/ppermute | solution.py:697
  45.5 2.1 %collective-permute-start.9 = (f32[8,768]{1,0:T(8,128)S(1)}, f32[8,768]{1,0:T(8,128)S(1)}, u32[]{:S(2)}, u32[]{:S(2)}) collective-permute-start(f32[8,768]{1,0:T(8,128)S(1)} %get-tuple-element.40.own_ref), channel_id=1, source_target_pairs={{0,16},{16,0},{1,17},{17,1},{2,18},{18,2},{3,19},{19,3},{4,20},{20... | collective-permute-start | bytes 73736 | tf_op jit(solution)/shard_map/ppermute | solution.py:696
  47.6 2.2 %collective-permute-done.10.cross_ref = f32[8,768]{1,0:T(8,128)S(1)} collective-permute-done((f32[8,768]{1,0:T(8,128)S(1)}, f32[8,768]{1,0:T(8,128)S(1)}, u32[]{:S(2)}, u32[]{:S(2)}) %collective-permute-start.10) | collective-permute-done | bytes 24608 | tf_op jit(solution)/shard_map/ppermute | solution.py:697
  49.8 0.0 collective-permute-done.9.core_ref
  49.8 0.4 collective-permute-done.8.got_ref
  50.2 0.7 merge.1
  51.0 0.0 copy-start
  51.0 0.0 copy-start.5
  51.0 21.0 %all_to_all.22 = bf16[8,32,2560]{2,1,0:T(8,128)(2,1)S(1)} all-to-all(bf16[8,32,2560]{2,1,0:T(8,128)(2,1)S(1)} %bitcast.12), channel_id=1, replica_groups={{0,1,2,3,4,5,6,7},{8,9,10,11,12,13,14,15},{16,17,18,19,20,21,22,23},{24..., dimensions={0} | all-to-all | bytes 2621440 | tf_op jit(solution)/shard_map/all_to_all | solution.py:712
  72.0 3.6 %final.1 = (bf16[256,1536]{1,0:T(8,128)(2,1)}, bf16[256,1536]{1,0:T(8,128)(2,1)}, f32[1536]{0:T(1024)}, f32[1536]{0:T(1024)}, f32[1,12]{1,0:T(1,128)}) custom-call(bf16[256,2560]{1,0:T(8,128)(2,1)S(1)} %bitcast.13, bf16[256,1536]{1,0:T(8,128)(2,1)S(1)} %bitcast.17, bf16[256,1536]{1,0:T(8,128)(2,1)S(1)} %bitcast.19, s32[16,16]{1,0:T(8,128)S(1)} %bitcast.21, ...), custom_call_target="tpu_custom_call" | custom-call | tf_op jit(solution)/shard_map/final/pallas_call | solution.py:720
  (12 shorter events, 0.1 us)
Async XLA Ops:
  5.1 6.5 %copy-start.1 = (bf16[256,2304]{1,0:T(8,128)(2,1)S(1)}, bf16[256,2304]{1,0:T(8,128)(2,1)}, u32[]{:S(2)}) copy-start(bf16[256,2304]{1,0:T(8,128)(2,1)} %get-tuple-element.27.send_ref) | copy-start | bytes 3538948
  5.1 6.5 %copy-start.4 = (s32[4,136,136]{2,1,0:T(8,128)S(1)}, s32[4,136,136]{2,1,0:T(8,128)}, u32[]{:S(2)}) copy-start(s32[4,136,136]{2,1,0:T(8,128)} %adj_ref.1) | copy-start | bytes 887812
  5.1 6.5 %copy-start.8 = (s32[1,256]{1,0:T(1,128)S(1)}, s32[1,256]{1,0:T(1,128)}, u32[]{:S(2)}) copy-start(s32[1,256]{1,0:T(1,128)} %clip_ref.1) | copy-start | bytes 3076
  5.1 6.5 %copy-start.9 = (s32[1,256]{1,0:T(1,128)S(1)}, s32[1,256]{1,0:T(1,128)}, u32[]{:S(2)}) copy-start(s32[1,256]{1,0:T(1,128)} %kind_ref.1) | copy-start | bytes 3076
  5.1 25.6 %all-to-all-start = ((bf16[8,32,2304]{2,1,0:T(8,128)(2,1)}), bf16[8,32,2304]{2,1,0:T(8,128)(2,1)S(1)}, u32[]{:S(2)}, u32[]{:S(2)}) async-start(bf16[8,32,2304]{2,1,0:T(8,128)(2,1)} %bitcast.15), calls=%async_computation | async-start | bytes 2359296 | tf_op jit(solution)/shard_map/all_to_all | solution.py:603
  11.4 10.7 %copy-start.11 = (bf16[1536]{0:T(1024)(128)(2,1)S(1)}, bf16[1536]{0:T(1024)(128)(2,1)}, u32[]{:S(2)}) copy-start(bf16[1536]{0:T(1024)(128)(2,1)} %param.17) | copy-start | bytes 9220
  11.4 10.7 %copy-start.10 = (f32[1536]{0:T(1024)S(1)}, f32[1536]{0:T(1024)}, u32[]{:S(2)}) copy-start(f32[1536]{0:T(1024)} %param.18) | copy-start | bytes 18436
  11.5 10.8 %copy-start.7 = (f32[12]{0:T(128)S(1)}, f32[12]{0:T(128)}, u32[]{:S(2)}) copy-start(f32[12]{0:T(128)} %refs_5_.1) | copy-start | bytes 148
  11.5 19.3 %copy-start.6 = (f32[1,1536]{1,0:T(1,128)S(1)}, f32[1,1536]{1,0:T(1,128)}, u32[]{:S(2)}) copy-start(f32[1,1536]{1,0:T(1,128)} %get-tuple-element.38.refs_9_) | copy-start | bytes 18436
  12.8 7.2 %collective-permute-start = (bf16[32,768]{1,0:T(8,128)(2,1)S(1)}, bf16[32,768]{1,0:T(8,128)(2,1)S(1)}, u32[]{:S(2)}, u32[]{:S(2)}) collective-permute-start(bf16[32,768]{1,0:T(8,128)(2,1)S(1)} %get-tuple-element.28), channel_id=1, source_target_pairs={{8,0},{24,16}} | collective-permute-start | bytes 147464 | tf_op jit(solution)/shard_map/ppermute | solution.py:631
  14.1 6.5 %collective-permute-start.1 = (bf16[32,768]{1,0:T(8,128)(2,1)S(1)}, bf16[32,768]{1,0:T(8,128)(2,1)S(1)}, u32[]{:S(2)}, u32[]{:S(2)}) collective-permute-start(bf16[32,768]{1,0:T(8,128)(2,1)S(1)} %get-tuple-element.29), channel_id=1, source_target_pairs={{8,1},{24,17}} | collective-permute-start | bytes 147464 | tf_op jit(solution)/shard_map/ppermute | solution.py:633
  14.8 6.6 %collective-permute-start.2 = (bf16[32,768]{1,0:T(8,128)(2,1)S(1)}, bf16[32,768]{1,0:T(8,128)(2,1)S(1)}, u32[]{:S(2)}, u32[]{:S(2)}) collective-permute-start(bf16[32,768]{1,0:T(8,128)(2,1)S(1)} %get-tuple-element.30), channel_id=1, source_target_pairs={{8,2},{24,18}} | collective-permute-start | bytes 147464 | tf_op jit(solution)/shard_map/ppermute | solution.py:633
  15.4 7.0 %collective-permute-start.3 = (bf16[32,768]{1,0:T(8,128)(2,1)S(1)}, bf16[32,768]{1,0:T(8,128)(2,1)S(1)}, u32[]{:S(2)}, u32[]{:S(2)}) collective-permute-start(bf16[32,768]{1,0:T(8,128)(2,1)S(1)} %get-tuple-element.31), channel_id=1, source_target_pairs={{8,3},{24,19}} | collective-permute-start | bytes 147464 | tf_op jit(solution)/shard_map/ppermute | solution.py:633
  16.1 6.3 %collective-permute-start.4 = (bf16[32,768]{1,0:T(8,128)(2,1)S(1)}, bf16[32,768]{1,0:T(8,128)(2,1)S(1)}, u32[]{:S(2)}, u32[]{:S(2)}) collective-permute-start(bf16[32,768]{1,0:T(8,128)(2,1)S(1)} %get-tuple-element.32), channel_id=1, source_target_pairs={{8,4},{24,20}} | collective-permute-start | bytes 147464 | tf_op jit(solution)/shard_map/ppermute | solution.py:633
  20.0 2.4 %collective-permute-start.5 = (bf16[32,768]{1,0:T(8,128)(2,1)S(1)}, bf16[32,768]{1,0:T(8,128)(2,1)S(1)}, u32[]{:S(2)}, u32[]{:S(2)}) collective-permute-start(bf16[32,768]{1,0:T(8,128)(2,1)S(1)} %get-tuple-element.33), channel_id=1, source_target_pairs={{8,5},{24,21}} | collective-permute-start | bytes 147464 | tf_op jit(solution)/shard_map/ppermute | solution.py:633
  20.6 1.8 %collective-permute-start.6 = (bf16[32,768]{1,0:T(8,128)(2,1)S(1)}, bf16[32,768]{1,0:T(8,128)(2,1)S(1)}, u32[]{:S(2)}, u32[]{:S(2)}) collective-permute-start(bf16[32,768]{1,0:T(8,128)(2,1)S(1)} %get-tuple-element.34), channel_id=1, source_target_pairs={{8,6},{24,22}} | collective-permute-start | bytes 147464 | tf_op jit(solution)/shard_map/ppermute | solution.py:633
  21.3 1.1 %collective-permute-start.7 = (bf16[32,768]{1,0:T(8,128)(2,1)S(1)}, bf16[32,768]{1,0:T(8,128)(2,1)S(1)}, u32[]{:S(2)}, u32[]{:S(2)}) collective-permute-start(bf16[32,768]{1,0:T(8,128)(2,1)S(1)} %get-tuple-element.35), channel_id=1, source_target_pairs={{8,7},{24,23}} | collective-permute-start | bytes 147464 | tf_op jit(solution)/shard_map/ppermute | solution.py:633
  44.5 5.7 %collective-permute-start.8 = (bf16[40,768]{1,0:T(8,128)(2,1)S(1)}, bf16[40,768]{1,0:T(8,128)(2,1)S(1)}, u32[]{:S(2)}, u32[]{:S(2)}) collective-permute-start(bf16[40,768]{1,0:T(8,128)(2,1)S(1)} %get-tuple-element.41), channel_id=1, source_target_pairs={{0,8},{1,9},{2,10},{3,11},{4,12},{5,13},{6,14},{7,15},{8,0},{9,1},... | collective-permute-start | bytes 184328 | tf_op jit(solution)/shard_map/ppermute | solution.py:695
  44.6 5.2 %collective-permute-start.10 = (f32[8,768]{1,0:T(8,128)S(1)}, f32[8,768]{1,0:T(8,128)S(1)}, u32[]{:S(2)}, u32[]{:S(2)}) collective-permute-start(f32[8,768]{1,0:T(8,128)S(1)} %get-tuple-element.40.own_ref), channel_id=1, source_target_pairs={{0,24},{1,25},{2,26},{3,27},{4,28},{5,29},{6,30},{7,31},{8,16},{9,... | collective-permute-start | bytes 73736 | tf_op jit(solution)/shard_map/ppermute | solution.py:697
  45.5 4.3 %collective-permute-start.9 = (f32[8,768]{1,0:T(8,128)S(1)}, f32[8,768]{1,0:T(8,128)S(1)}, u32[]{:S(2)}, u32[]{:S(2)}) collective-permute-start(f32[8,768]{1,0:T(8,128)S(1)} %get-tuple-element.40.own_ref), channel_id=1, source_target_pairs={{0,16},{16,0},{1,17},{17,1},{2,18},{18,2},{3,19},{19,3},{4,20},{20... | collective-permute-start | bytes 73736 | tf_op jit(solution)/shard_map/ppermute | solution.py:696
  50.2 21.7 %copy-start.2 = (bf16[1,16,16,1536]{3,2,1,0:T(8,128)(2,1)S(1)}, bf16[1,16,16,1536]{3,2,1,0:T(8,128)(2,1)}, u32[]{:S(2)}) copy-start(bf16[1,16,16,1536]{3,2,1,0:T(8,128)(2,1)} %param.11) | copy-start | bytes 2359300
  50.2 21.7 %copy-start.3 = (bf16[1,16,16,1536]{3,2,1,0:T(8,128)(2,1)S(1)}, bf16[1,16,16,1536]{3,2,1,0:T(8,128)(2,1)}, u32[]{:S(2)}) copy-start(bf16[1,16,16,1536]{3,2,1,0:T(8,128)(2,1)} %param.12) | copy-start | bytes 2359300
  51.0 21.0 %copy-start = (bf16[768,1536]{1,0:T(8,128)(2,1)S(1)}, bf16[768,1536]{1,0:T(8,128)(2,1)}, u32[]{:S(2)}) copy-start(bf16[768,1536]{1,0:T(8,128)(2,1)} %w_ref.1) | copy-start | bytes 7077892
  51.0 21.0 %copy-start.5 = (s32[1,16,16]{2,1,0:T(8,128)S(1)}, s32[1,16,16]{2,1,0:T(8,128)}, u32[]{:S(2)}) copy-start(s32[1,16,16]{2,1,0:T(8,128)} %param.13) | copy-start | bytes 3076

commit v3 on v2

--- a/solution.py
+++ b/solution.py
@@ -134,20 +134,6 @@
         cp.start()
     swap = row_swap(slots, frames, False)
     hid = hidden_column(hid_ref[...], slots, frames, False) > 0.5
-    delta = dot_nn(swap, recv_ref[:, hw:wide])
-    ctx = dot_nn(swap, recv_ref[:, :hw]).astype(BF)
-    copies[0].wait()
-    grad_s[...] = jnp.where(hid, 0.0, cot_ref[...].astype(F32) + delta).astype(BF)
-    stores = [
-        pltpu.make_async_copy(grad_s, grad_hbm, sem.at[2]),
-        pltpu.make_async_copy(out_s, out_hbm, sem.at[3]),
-    ]
-    stores[0].start()
-    attn = dot_nn(ctx, w_ref[...]).astype(BF)
-    copies[1].wait()
-    x_in = jnp.where(hid, tok_ref[...].astype(F32), x_ref[...].astype(F32))
-    out_s[...] = (x_in + attn.astype(F32)).astype(BF)
-    stores[1].start()
     if shared:
         total = jnp.zeros((32, LANES), F32)
         for j in range(recv_ref.shape[0] // 32):
@@ -165,6 +151,23 @@
             token_ref[here] = sums_ref[c : c + 1].reshape(hw)
             gain_ref[here] = sums_ref[2 + c : 3 + c].reshape(hw)
         coef_ref[...] = sums_ref[4:5, : coef_ref.shape[1]]
+    ctx = dot_nn(swap, recv_ref[:, :hw]).astype(BF)
+    attn = dot_nn(ctx, w_ref[...]).astype(BF)
+    delta = dot_nn(swap, recv_ref[:, hw:wide])
+    for cp in copies:
+        cp.wait()
+    stores = []
+    half = swap.shape[0] // 2
+    for h in range(2):
+        r = slice(h * half, (h + 1) * half)
+        here = pl.ds(h * half, half)
+        grad_s[r] = jnp.where(hid[r], 0.0, cot_ref[r].astype(F32) + delta[r]).astype(BF)
+        stores.append(pltpu.make_async_copy(grad_s.at[here], grad_hbm.at[here], sem.at[2 + 2 * h]))
+        stores[-1].start()
+        x_in = jnp.where(hid[r], tok_ref[...].astype(F32), x_ref[r].astype(F32))
+        out_s[r] = (x_in + attn[r].astype(F32)).astype(BF)
+        stores.append(pltpu.make_async_copy(out_s.at[here], out_hbm.at[here], sem.at[3 + 2 * h]))
+        stores[-1].start()
     for cp in stores:
         cp.wait()
 
@@ -406,22 +409,33 @@
             total = total + kept[h * EQ : (h + 1) * EQ]
         return jnp.concatenate([total, jnp.zeros((EP - EQ, hw), F32)], axis=0)
 
-    for f in range(nf):
+    def attend(scores, grad_w):
+        n = range(len(scores))
+        top = [jnp.max(scores[i], axis=0, keepdims=True) for i in n]
+        raw = [jnp.exp(scores[i] - top[i]) for i in n]
+        w_t = [raw[i] * (1.0 / jnp.sum(raw[i], axis=0, keepdims=True)) for i in n]
+        w_b = [w_t[i].astype(BF) for i in n]
+        ds = [
+            w_t[i] * (grad_w[i] - jnp.sum(w_t[i] * grad_w[i], axis=0, keepdims=True)) for i in n
+        ]
+        return w_t, w_b, ds, [ds[i].astype(BF) for i in n]
+
+    fs = range(nf)
+    q_e = [spread(q_s[f, main:].astype(F32)[:EQ]).astype(BF) for f in fs]
+    g_e = [spread(g_s[f, main:].astype(F32)[:EQ]).astype(BF) for f in fs]
+    s_t = [dot_nt(k_s[f], q_e[f]) + bias_e for f in fs]
+    gw = [dot_nt(v_s[f], g_e[f]) for f in fs]
+    w_t, w_b, ds, ds_b = attend(s_t, gw)
+    for f in fs:
+        coef_lanes = coef_lanes + jnp.sum(ds[f] * link_e, axis=0, keepdims=True)
+    ctx_e = [dot_tn(w_b[f], v_s[f]) for f in fs]
+    gq_e = [dot_tn(ds_b[f], k_s[f]) for f in fs]
+    for f in fs:
         guest_rows = slice(rows + f * EP, rows + (f + 1) * EP)
-        q_e = spread(q_s[f, main:].astype(F32)[:EQ]).astype(BF)
-        g_e = spread(g_s[f, main:].astype(F32)[:EQ]).astype(BF)
-        s_t = dot_nt(k_s[f], q_e) + bias_e
-        p_t = jnp.exp(s_t - jnp.max(s_t, axis=0, keepdims=True))
-        w_t = p_t * (1.0 / jnp.sum(p_t, axis=0, keepdims=True))
-        w_b = w_t.astype(BF)
-        gw = dot_nt(v_s[f], g_e)
-        ds = w_t * (gw - jnp.sum(w_t * gw, axis=0, keepdims=True))
-        coef_lanes = coef_lanes + jnp.sum(ds * link_e, axis=0, keepdims=True)
-        ds_b = ds.astype(BF)
-        ctx_s[guest_rows] = fold(dot_tn(w_b, v_s[f])).astype(BF)
-        gu_s[guest_rows, :hw] = fold(dot_tn(ds_b, k_s[f]) * hs**-0.5).astype(BF)
-        gk_s[f] = dot_nn(ds_b, q_e)
-        gv_s[f] = dot_nn(w_b, g_e)
+        gk_s[f] = dot_nn(ds_b[f], q_e[f])
+        gv_s[f] = dot_nn(w_b[f], g_e[f])
+        ctx_s[guest_rows] = fold(ctx_e[f]).astype(BF)
+        gu_s[guest_rows, :hw] = fold(gq_e[f] * hs**-0.5).astype(BF)
 
     lane = iota((1, 128), 1)
     coef_out = jnp.zeros((1, 128), F32)
@@ -433,52 +447,59 @@
     pair_w = 2 * hs
     low = iota((main, pair_w), 1) < hs
     zero = jnp.zeros((main, pair_w), BF)
-    for p in range(heads // 2):
-        cols = slice(p * pair_w, (p + 1) * pair_w)
-        k_cols = slice(hw + p * pair_w, hw + (p + 1) * pair_w)
-        v_cols = slice(2 * hw + p * pair_w, 2 * hw + (p + 1) * pair_w)
-        bias = jnp.concatenate(
-            [
-                jnp.where(link < 0, MASKED, coef_ref[2 * p] * link),
-                jnp.where(link < 0, MASKED, coef_ref[2 * p + 1] * link),
-            ],
-            axis=1,
+    link_two = jnp.concatenate([link, link], axis=1)
+
+    def two_heads(value):
+        return jnp.concatenate(
+            [jnp.where(low, value, zero), jnp.where(low, zero, value)], axis=0
         )
-        ds_sum = jnp.zeros((keys, 2 * main), F32)
-        for f in range(nf):
+
+    for first_pair in range(0, heads // 2, 3):
+        pairs = range(first_pair, min(first_pair + 3, heads // 2))
+        items = [(p, f) for p in pairs for f in range(nf)]
+        bias = {
+            p: jnp.concatenate(
+                [
+                    jnp.where(link < 0, MASKED, coef_ref[2 * p] * link),
+                    jnp.where(link < 0, MASKED, coef_ref[2 * p + 1] * link),
+                ],
+                axis=1,
+            )
+            for p in pairs
+        }
+        cols = {p: slice(p * pair_w, (p + 1) * pair_w) for p in pairs}
+        k = [k_s[f, :, cols[p]] for p, f in items]
+        v = [v_s[f, :, cols[p]] for p, f in items]
+        qq = [two_heads(q_s[f, :main, cols[p]]) for p, f in items]
+        gg = [two_heads(g_s[f, :main, cols[p]]) for p, f in items]
+        s_t = [dot_nt(k[i], qq[i]) + bias[p] for i, (p, f) in enumerate(items)]
+        gw = [dot_nt(v[i], gg[i]) for i in range(len(items))]
+        w_t, w_b, ds, ds_b = attend(s_t, gw)
+        ctx_t = [dot_tn(v[i], w_b[i]) for i in range(len(items))]
+        gv = [gv_s[f, :, cols[p]] + dot_nn(w_b[i], gg[i]) for i, (p, f) in enumerate(items)]
+        gq_t = [dot_tn(k[i], ds_b[i]) for i in range(len(items))]
+        gk = [gk_s[f, :, cols[p]] + dot_nn(ds_b[i], qq[i]) for i, (p, f) in enumerate(items)]
+        for i, (p, f) in enumerate(items):
             main_rows = slice(f * main, (f + 1) * main)
             guest_rows = slice(rows + f * EP, rows + (f + 1) * EP)
-            k = k_s[f, :, cols]
-            v = v_s[f, :, cols]
-            q = q_s[f, :main, cols]
-            g = g_s[f, :main, cols]
-            qq = jnp.concatenate([jnp.where(low, q, zero), jnp.where(low, zero, q)], axis=0)
-            gg = jnp.concatenate([jnp.where(low, g, zero), jnp.where(low, zero, g)], axis=0)
-            s_t = dot_nt(k, qq) + bias
-            p_t = jnp.exp(s_t - jnp.max(s_t, axis=0, keepdims=True))
-            w_t = p_t * (1.0 / jnp.sum(p_t, axis=0, keepdims=True))
-            w_b = w_t.astype(BF)
-            gw = dot_nt(v, gg)
-            ds = w_t * (gw - jnp.sum(w_t * gw, axis=0, keepdims=True))
-            ds_sum = ds_sum + ds
-            ds_b = ds.astype(BF)
-            ctx_t = dot_tn(v, w_b)
-            ctx_t = jnp.concatenate([ctx_t[:hs, :main], ctx_t[hs:, main:]], axis=0)
-            ctx_s[main_rows, cols] = ctx_t.T.astype(BF)
-            gq_t = dot_tn(k, ds_b)
-            gq_t = jnp.concatenate([gq_t[:hs, :main], gq_t[hs:, main:]], axis=0)
-            gu_s[main_rows, cols] = (gq_t.T * hs**-0.5).astype(BF)
-            gk = (gk_s[f, :, cols] + dot_nn(ds_b, qq)).astype(BF)
-            gu_s[main_rows, k_cols] = gk[:main]
-            gu_s[guest_rows, k_cols] = gk[main:]
-            gv = (gv_s[f, :, cols] + dot_nn(w_b, gg)).astype(BF)
-            gu_s[main_rows, v_cols] = gv[:main]
-            gu_s[guest_rows, v_cols] = gv[main:]
-        lanes = jnp.sum(ds_sum * jnp.concatenate([link, link], axis=1), axis=0, keepdims=True)
-        coef_out = coef_out + jnp.where(lane == 2 * p, jnp.sum(lanes[:, :main]), 0.0)
-        coef_out = coef_out + jnp.where(lane == 2 * p + 1, jnp.sum(lanes[:, main:]), 0.0)
+            both = jnp.concatenate([ctx_t[i][:hs, :main], ctx_t[i][hs:, main:]], axis=0)
+            ctx_s[main_rows, cols[p]] = both.T.astype(BF)
+            both = jnp.concatenate([gq_t[i][:hs, :main], gq_t[i][hs:, main:]], axis=0)
+            gu_s[main_rows, cols[p]] = (both.T * hs**-0.5).astype(BF)
+            for value, offset in ((gk[i].astype(BF), hw), (gv[i].astype(BF), 2 * hw)):
+                here = slice(offset + p * pair_w, offset + (p + 1) * pair_w)
+                gu_s[main_rows, here] = value[:main]
+                gu_s[guest_rows, here] = value[main:]
+        for p in pairs:
+            ds_sum = functools.reduce(
+                lambda x, y: x + y, [ds[i] for i, item in enumerate(items) if item[0] == p]
+            )
+            lanes = jnp.sum(ds_sum * link_two, axis=0, keepdims=True)
+            coef_out = coef_out + jnp.where(lane == 2 * p, jnp.sum(lanes[:, :main]), 0.0)
+            coef_out = coef_out + jnp.where(lane == 2 * p + 1, jnp.sum(lanes[:, main:]), 0.0)
 
     out_s[:, :hw] = scatter(ctx_s[:rows])
+
     gn_s[...] = dot_nt(gu_s[...], w_ref[...])
     guest_limit = jnp.where(flag_ref[0] == 1, guests, 0)
     main_limit = jnp.where(flag_ref[0] == 1, 0, guests)
@@ -733,7 +754,7 @@
             pltpu.VMEM((rows, d), BF),
             pltpu.VMEM((rows, d), BF),
             pltpu.VMEM((rows, d), BF),
-            pltpu.SemaphoreType.DMA((4,)),
+            pltpu.SemaphoreType.DMA((6,)),
         ],
         compiler_params=pltpu.CompilerParams(vmem_limit_bytes=VMEM_LIMIT),
         name="final",

time: 76.1 us -> 73.3 us (0.963)
  Pallas kernels: 23.7 us -> 21.1 us
    pallas_call x1, Pallas kernels: 13.8 us -> 11.6 us  [on_device(): pl.pallas_call(functools.partial(frame_kernel, half, nf, slots, guests),...]
where the time goes in v3:
time: 73.3 us; the launch traced here: 73 us
  Pallas kernels  21.1 us (29%)
  blocking collectives  21 us (29%)
  starting transfers between devices  15.4 us (21%)
  waiting for transfers between devices  14.3 us (20%)
  between operations  0.94 us (1%)
    all_to_all x1, blocking collectives, on_device(): lax.all_to_all(merged, 'seq', 0, 0, axis_index_groups=groups, tiled=True)  21 us
    pallas_call x1, Pallas kernels, on_device(): pl.pallas_call(functools.partial(frame_kernel, half, nf, slots, guests),...  11.6 us
    all_to_all x1, waiting for transfers between devices, on_device(): lax.all_to_all(send, 'seq', 0, 0, axis_index_groups=groups, tiled=True)  8.44 us
    all_to_all x1, starting transfers between devices, on_device(): lax.all_to_all(send, 'seq', 0, 0, axis_index_groups=groups, tiled=True)  6.33 us
    ppermute x7, starting transfers between devices, on_device(): ext = ext + lax.ppermute(packed[j], 'seq', [(half, j)])  4.63 us
    pallas_call x1, Pallas kernels, on_device(): pl.pallas_call(functools.partial(send_kernel, slots, frames), out_shape=(...  4.43 us
    ppermute x1, waiting for transfers between devices, on_device(): ext = lax.ppermute(packed[0], 'seq', [(half, 0)])  3.19 us
    pallas_call x1, Pallas kernels, on_device(): pl.pallas_call(functools.partial(final_kernel, slots, frames, shared), ou...  3.15 us
  transfers between devices with their start and end apart: 12, of which 4 were waited for; matrix products, arithmetic and copies ran while one was open for 0% of the time, Pallas kernels for 2%

profile of v3, /device:TPU:0, one launch (start us, length us, event | category | flops | bytes accessed | tf_op | source)
XLA Modules:
  0.0 73.0 jit_solution(8437341076018324045)
XLA Ops:
  0.6 4.4 %send.1 = (bf16[256,2304]{1,0:T(8,128)(2,1)}, f32[1,1536]{1,0:T(1,128)}) custom-call(bf16[256,1536]{1,0:T(8,128)(2,1)} %bitcast.16, bf16[256,1536]{1,0:T(8,128)(2,1)} %bitcast.18, s32[16,16]{1,0:T(8,128)} %bitcast.20, bf16[768,1536]{1,0:T(8,128)(2,1)} %w_ref.1), custom_call_target="tpu_custom_call" | custom-call | tf_op jit(solution)/shard_map/send/pallas_call | solution.py:605
  5.1 0.0 copy-start.1
  5.1 0.0 copy-start.4
  5.1 0.0 copy-start.8
  5.1 0.0 copy-start.9
  5.1 6.3 %all-to-all-start = ((bf16[8,32,2304]{2,1,0:T(8,128)(2,1)}), bf16[8,32,2304]{2,1,0:T(8,128)(2,1)S(1)}, u32[]{:S(2)}, u32[]{:S(2)}) async-start(bf16[8,32,2304]{2,1,0:T(8,128)(2,1)} %bitcast.15), calls=%async_computation | async-start | bytes 2359296 | tf_op jit(solution)/shard_map/all_to_all | solution.py:624
  11.4 0.0 copy-start.10
  11.5 0.0 copy-start.7
  11.5 0.0 copy-start.6
  11.5 0.1 pad_add_fusion.flag_ref.refs_2_
  11.6 0.0 copy-done.1
  11.6 0.0 copy-done.4
  11.6 0.0 copy-done.8
  11.6 0.0 copy-done.9
  11.6 1.2 %stage.1 = (f32[144,128]{1,0:T(8,128)S(1)}, f32[144,96]{1,0:T(8,128)S(1)}, bf16[32,768]{1,0:T(8,128)(2,1)S(1)}, bf16[32,768]{1,0:T(8,128)(2,1)S(1)}, bf16[32,768...) custom-call(s32[2]{0:T(128)S(1)} %pad_add_fusion.flag_ref.refs_2_, ...), custom_call_target="tpu_custom_call" | custom-call | tf_op jit(solution)/shard_map/stage/pallas_call | solution.py:638
  12.8 1.3 %collective-permute-start = (bf16[32,768]{1,0:T(8,128)(2,1)S(1)}, bf16[32,768]{1,0:T(8,128)(2,1)S(1)}, u32[]{:S(2)}, u32[]{:S(2)}) collective-permute-start(bf16[32,768]{1,0:T(8,128)(2,1)S(1)} %get-tuple-element.28), channel_id=1, source_target_pairs={{8,0},{24,16}} | collective-permute-start | bytes 147464 | tf_op jit(solution)/shard_map/ppermute | solution.py:652
  14.1 0.7 collective-permute-start.1
  14.8 0.7 collective-permute-start.2
  15.4 0.7 collective-permute-start.3
  16.1 0.7 collective-permute-start.4
  16.8 3.2 %collective-permute-done = bf16[32,768]{1,0:T(8,128)(2,1)S(1)} collective-permute-done((bf16[32,768]{1,0:T(8,128)(2,1)S(1)}, bf16[32,768]{1,0:T(8,128)(2,1)S(1)}, u32[]{:S(2)}, u32[]{:S(2)}) %collective-permute-start) | collective-permute-done | bytes 49184 | tf_op jit(solution)/shard_map/ppermute | solution.py:652
  20.0 0.7 collective-permute-start.5
  20.6 0.0 collective-permute-done.1
  20.6 0.7 collective-permute-start.6
  21.3 0.0 collective-permute-done.2
  21.3 0.7 collective-permute-start.7
  22.0 0.0 copy-done.10
  22.0 0.1 broadcast_in_dim.3
  22.1 0.1 reshape_reshape.3.refs_6_
  22.2 0.0 collective-permute-done.3
  22.2 0.0 collective-permute-done.4
  22.2 0.0 collective-permute-done.5
  22.2 0.0 collective-permute-done.6
  22.2 0.0 collective-permute-done.7
  22.3 8.4 %all-to-all-done = bf16[8,32,2304]{2,1,0:T(8,128)(2,1)S(1)} async-done(((bf16[8,32,2304]{2,1,0:T(8,128)(2,1)}), bf16[8,32,2304]{2,1,0:T(8,128)(2,1)S(1)}, u32[]{:S(2)}, u32[]{:S(2)}) %all-to-all-start) | async-done | bytes 1179680 | tf_op jit(solution)/shard_map/all_to_all | solution.py:624
  30.7 11.6 %frames.1 = (bf16[256,2560]{1,0:T(8,128)(2,1)S(1)}, bf16[40,768]{1,0:T(8,128)(2,1)S(1)}, f32[8,768]{1,0:T(8,128)S(1)}) custom-call(bf16[32,768]{1,0:T(8,128)(2,1)S(1)} %add_add_fusion.refs_0_, bf16[256,2304]{1,0:T(8,128)(2,1)S(1)} %bitcast.14, s32[2]{0:T(128)S(1)} %pad_add_fusion.flag_ref.refs_2_, f32[144,128]{1,0:T(8,128)S(1)} %get-tuple-element.36.refs_3_, ...), custom_call_target="tpu_custom_call" | custom-call | tf_op jit(solution)/shard_map/frames/pallas_call | solution.py:673
  42.3 0.1 collective-permute-start.8
  42.4 0.9 %collective-permute-start.10 = (f32[8,768]{1,0:T(8,128)S(1)}, f32[8,768]{1,0:T(8,128)S(1)}, u32[]{:S(2)}, u32[]{:S(2)}) collective-permute-start(f32[8,768]{1,0:T(8,128)S(1)} %get-tuple-element.40.own_ref), channel_id=1, source_target_pairs={{0,24},{1,25},{2,26},{3,27},{4,28},{5,29},{6,30},{7,31},{8,16},{9,... | collective-permute-start | bytes 73736 | tf_op jit(solution)/shard_map/ppermute | solution.py:718
  43.3 2.1 %collective-permute-start.9 = (f32[8,768]{1,0:T(8,128)S(1)}, f32[8,768]{1,0:T(8,128)S(1)}, u32[]{:S(2)}, u32[]{:S(2)}) collective-permute-start(f32[8,768]{1,0:T(8,128)S(1)} %get-tuple-element.40.own_ref), channel_id=1, source_target_pairs={{0,16},{16,0},{1,17},{17,1},{2,18},{18,2},{3,19},{19,3},{4,20},{20... | collective-permute-start | bytes 73736 | tf_op jit(solution)/shard_map/ppermute | solution.py:717
  45.4 2.2 %collective-permute-done.10.cross_ref = f32[8,768]{1,0:T(8,128)S(1)} collective-permute-done((f32[8,768]{1,0:T(8,128)S(1)}, f32[8,768]{1,0:T(8,128)S(1)}, u32[]{:S(2)}, u32[]{:S(2)}) %collective-permute-start.10) | collective-permute-done | bytes 24608 | tf_op jit(solution)/shard_map/ppermute | solution.py:718
  47.6 0.0 collective-permute-done.9.core_ref
  47.6 0.4 collective-permute-done.8.got_ref
  48.0 0.7 merge.1
  48.8 0.0 copy-start
  48.8 0.0 copy-start.5
  48.8 21.0 %all_to_all.22 = bf16[8,32,2560]{2,1,0:T(8,128)(2,1)S(1)} all-to-all(bf16[8,32,2560]{2,1,0:T(8,128)(2,1)S(1)} %bitcast.12), channel_id=1, replica_groups={{0,1,2,3,4,5,6,7},{8,9,10,11,12,13,14,15},{16,17,18,19,20,21,22,23},{24..., dimensions={0} | all-to-all | bytes 2621440 | tf_op jit(solution)/shard_map/all_to_all | solution.py:733
  69.8 0.0 copy-done.3
  69.8 3.1 %final.1 = (bf16[256,1536]{1,0:T(8,128)(2,1)}, bf16[256,1536]{1,0:T(8,128)(2,1)}, f32[1536]{0:T(1024)}, f32[1536]{0:T(1024)}, f32[1,12]{1,0:T(1,128)}) custom-call(bf16[256,2560]{1,0:T(8,128)(2,1)S(1)} %bitcast.13, bf16[256,1536]{1,0:T(8,128)(2,1)S(1)} %bitcast.17, bf16[256,1536]{1,0:T(8,128)(2,1)S(1)} %bitcast.19, s32[16,16]{1,0:T(8,128)S(1)} %bitcast.21, ...), custom_call_target="tpu_custom_call" | custom-call | tf_op jit(solution)/shard_map/final/pallas_call | solution.py:741
  (12 shorter events, 0.1 us)
Async XLA Ops:
  5.1 6.5 %copy-start.1 = (bf16[256,2304]{1,0:T(8,128)(2,1)S(1)}, bf16[256,2304]{1,0:T(8,128)(2,1)}, u32[]{:S(2)}) copy-start(bf16[256,2304]{1,0:T(8,128)(2,1)} %get-tuple-element.27.send_ref) | copy-start | bytes 3538948
  5.1 6.5 %copy-start.4 = (s32[4,136,136]{2,1,0:T(8,128)S(1)}, s32[4,136,136]{2,1,0:T(8,128)}, u32[]{:S(2)}) copy-start(s32[4,136,136]{2,1,0:T(8,128)} %adj_ref.1) | copy-start | bytes 887812
  5.1 6.5 %copy-start.8 = (s32[1,256]{1,0:T(1,128)S(1)}, s32[1,256]{1,0:T(1,128)}, u32[]{:S(2)}) copy-start(s32[1,256]{1,0:T(1,128)} %clip_ref.1) | copy-start | bytes 3076
  5.1 6.5 %copy-start.9 = (s32[1,256]{1,0:T(1,128)S(1)}, s32[1,256]{1,0:T(1,128)}, u32[]{:S(2)}) copy-start(s32[1,256]{1,0:T(1,128)} %kind_ref.1) | copy-start | bytes 3076
  5.1 25.6 %all-to-all-start = ((bf16[8,32,2304]{2,1,0:T(8,128)(2,1)}), bf16[8,32,2304]{2,1,0:T(8,128)(2,1)S(1)}, u32[]{:S(2)}, u32[]{:S(2)}) async-start(bf16[8,32,2304]{2,1,0:T(8,128)(2,1)} %bitcast.15), calls=%async_computation | async-start | bytes 2359296 | tf_op jit(solution)/shard_map/all_to_all | solution.py:624
  11.4 10.5 %copy-start.11 = (bf16[1536]{0:T(1024)(128)(2,1)S(1)}, bf16[1536]{0:T(1024)(128)(2,1)}, u32[]{:S(2)}) copy-start(bf16[1536]{0:T(1024)(128)(2,1)} %param.17) | copy-start | bytes 9220
  11.4 10.6 %copy-start.10 = (f32[1536]{0:T(1024)S(1)}, f32[1536]{0:T(1024)}, u32[]{:S(2)}) copy-start(f32[1536]{0:T(1024)} %param.18) | copy-start | bytes 18436
  11.5 10.6 %copy-start.7 = (f32[12]{0:T(128)S(1)}, f32[12]{0:T(128)}, u32[]{:S(2)}) copy-start(f32[12]{0:T(128)} %refs_5_.1) | copy-start | bytes 148
  11.5 19.3 %copy-start.6 = (f32[1,1536]{1,0:T(1,128)S(1)}, f32[1,1536]{1,0:T(1,128)}, u32[]{:S(2)}) copy-start(f32[1,1536]{1,0:T(1,128)} %get-tuple-element.38.refs_9_) | copy-start | bytes 18436
  12.8 7.2 %collective-permute-start = (bf16[32,768]{1,0:T(8,128)(2,1)S(1)}, bf16[32,768]{1,0:T(8,128)(2,1)S(1)}, u32[]{:S(2)}, u32[]{:S(2)}) collective-permute-start(bf16[32,768]{1,0:T(8,128)(2,1)S(1)} %get-tuple-element.28), channel_id=1, source_target_pairs={{8,0},{24,16}} | collective-permute-start | bytes 147464 | tf_op jit(solution)/shard_map/ppermute | solution.py:652
  14.1 6.5 %collective-permute-start.1 = (bf16[32,768]{1,0:T(8,128)(2,1)S(1)}, bf16[32,768]{1,0:T(8,128)(2,1)S(1)}, u32[]{:S(2)}, u32[]{:S(2)}) collective-permute-start(bf16[32,768]{1,0:T(8,128)(2,1)S(1)} %get-tuple-element.29), channel_id=1, source_target_pairs={{8,1},{24,17}} | collective-permute-start | bytes 147464 | tf_op jit(solution)/shard_map/ppermute | solution.py:654
  14.8 6.5 %collective-permute-start.2 = (bf16[32,768]{1,0:T(8,128)(2,1)S(1)}, bf16[32,768]{1,0:T(8,128)(2,1)S(1)}, u32[]{:S(2)}, u32[]{:S(2)}) collective-permute-start(bf16[32,768]{1,0:T(8,128)(2,1)S(1)} %get-tuple-element.30), channel_id=1, source_target_pairs={{8,2},{24,18}} | collective-permute-start | bytes 147464 | tf_op jit(solution)/shard_map/ppermute | solution.py:654
  15.4 6.8 %collective-permute-start.3 = (bf16[32,768]{1,0:T(8,128)(2,1)S(1)}, bf16[32,768]{1,0:T(8,128)(2,1)S(1)}, u32[]{:S(2)}, u32[]{:S(2)}) collective-permute-start(bf16[32,768]{1,0:T(8,128)(2,1)S(1)} %get-tuple-element.31), channel_id=1, source_target_pairs={{8,3},{24,19}} | collective-permute-start | bytes 147464 | tf_op jit(solution)/shard_map/ppermute | solution.py:654
  16.1 6.1 %collective-permute-start.4 = (bf16[32,768]{1,0:T(8,128)(2,1)S(1)}, bf16[32,768]{1,0:T(8,128)(2,1)S(1)}, u32[]{:S(2)}, u32[]{:S(2)}) collective-permute-start(bf16[32,768]{1,0:T(8,128)(2,1)S(1)} %get-tuple-element.32), channel_id=1, source_target_pairs={{8,4},{24,20}} | collective-permute-start | bytes 147464 | tf_op jit(solution)/shard_map/ppermute | solution.py:654
  20.0 2.3 %collective-permute-start.5 = (bf16[32,768]{1,0:T(8,128)(2,1)S(1)}, bf16[32,768]{1,0:T(8,128)(2,1)S(1)}, u32[]{:S(2)}, u32[]{:S(2)}) collective-permute-start(bf16[32,768]{1,0:T(8,128)(2,1)S(1)} %get-tuple-element.33), channel_id=1, source_target_pairs={{8,5},{24,21}} | collective-permute-start | bytes 147464 | tf_op jit(solution)/shard_map/ppermute | solution.py:654
  20.6 1.6 %collective-permute-start.6 = (bf16[32,768]{1,0:T(8,128)(2,1)S(1)}, bf16[32,768]{1,0:T(8,128)(2,1)S(1)}, u32[]{:S(2)}, u32[]{:S(2)}) collective-permute-start(bf16[32,768]{1,0:T(8,128)(2,1)S(1)} %get-tuple-element.34), channel_id=1, source_target_pairs={{8,6},{24,22}} | collective-permute-start | bytes 147464 | tf_op jit(solution)/shard_map/ppermute | solution.py:654
  21.3 0.9 %collective-permute-start.7 = (bf16[32,768]{1,0:T(8,128)(2,1)S(1)}, bf16[32,768]{1,0:T(8,128)(2,1)S(1)}, u32[]{:S(2)}, u32[]{:S(2)}) collective-permute-start(bf16[32,768]{1,0:T(8,128)(2,1)S(1)} %get-tuple-element.35), channel_id=1, source_target_pairs={{8,7},{24,23}} | collective-permute-start | bytes 147464 | tf_op jit(solution)/shard_map/ppermute | solution.py:654
  42.3 5.7 %collective-permute-start.8 = (bf16[40,768]{1,0:T(8,128)(2,1)S(1)}, bf16[40,768]{1,0:T(8,128)(2,1)S(1)}, u32[]{:S(2)}, u32[]{:S(2)}) collective-permute-start(bf16[40,768]{1,0:T(8,128)(2,1)S(1)} %get-tuple-element.41), channel_id=1, source_target_pairs={{0,8},{1,9},{2,10},{3,11},{4,12},{5,13},{6,14},{7,15},{8,0},{9,1},... | collective-permute-start | bytes 184328 | tf_op jit(solution)/shard_map/ppermute | solution.py:716
  42.4 5.2 %collective-permute-start.10 = (f32[8,768]{1,0:T(8,128)S(1)}, f32[8,768]{1,0:T(8,128)S(1)}, u32[]{:S(2)}, u32[]{:S(2)}) collective-permute-start(f32[8,768]{1,0:T(8,128)S(1)} %get-tuple-element.40.own_ref), channel_id=1, source_target_pairs={{0,24},{1,25},{2,26},{3,27},{4,28},{5,29},{6,30},{7,31},{8,16},{9,... | collective-permute-start | bytes 73736 | tf_op jit(solution)/shard_map/ppermute | solution.py:718
  43.3 4.3 %collective-permute-start.9 = (f32[8,768]{1,0:T(8,128)S(1)}, f32[8,768]{1,0:T(8,128)S(1)}, u32[]{:S(2)}, u32[]{:S(2)}) collective-permute-start(f32[8,768]{1,0:T(8,128)S(1)} %get-tuple-element.40.own_ref), channel_id=1, source_target_pairs={{0,16},{16,0},{1,17},{17,1},{2,18},{18,2},{3,19},{19,3},{4,20},{20... | collective-permute-start | bytes 73736 | tf_op jit(solution)/shard_map/ppermute | solution.py:717
  48.0 21.7 %copy-start.2 = (bf16[1,16,16,1536]{3,2,1,0:T(8,128)(2,1)S(1)}, bf16[1,16,16,1536]{3,2,1,0:T(8,128)(2,1)}, u32[]{:S(2)}) copy-start(bf16[1,16,16,1536]{3,2,1,0:T(8,128)(2,1)} %param.11) | copy-start | bytes 2359300
  48.0 21.7 %copy-start.3 = (bf16[1,16,16,1536]{3,2,1,0:T(8,128)(2,1)S(1)}, bf16[1,16,16,1536]{3,2,1,0:T(8,128)(2,1)}, u32[]{:S(2)}) copy-start(bf16[1,16,16,1536]{3,2,1,0:T(8,128)(2,1)} %param.12) | copy-start | bytes 2359300
  48.8 21.0 %copy-start = (bf16[768,1536]{1,0:T(8,128)(2,1)S(1)}, bf16[768,1536]{1,0:T(8,128)(2,1)}, u32[]{:S(2)}) copy-start(bf16[768,1536]{1,0:T(8,128)(2,1)} %w_ref.1) | copy-start | bytes 7077892
  48.8 21.0 %copy-start.5 = (s32[1,16,16]{2,1,0:T(8,128)S(1)}, s32[1,16,16]{2,1,0:T(8,128)}, u32[]{:S(2)}) copy-start(s32[1,16,16]{2,1,0:T(8,128)} %param.13) | copy-start | bytes 3076

commit v4 on v3

--- a/solution.py
+++ b/solution.py
@@ -105,19 +105,14 @@
 def final_kernel(
     slots,
     frames,
-    shared,
     recv_ref,
     x_hbm,
     cot_hbm,
     hid_ref,
     tok_ref,
     w_ref,
-    sums_ref,
     out_hbm,
     grad_hbm,
-    token_ref,
-    gain_ref,
-    coef_ref,
     x_ref,
     cot_ref,
     out_s,
@@ -134,23 +129,6 @@
         cp.start()
     swap = row_swap(slots, frames, False)
     hid = hidden_column(hid_ref[...], slots, frames, False) > 0.5
-    if shared:
-        total = jnp.zeros((32, LANES), F32)
-        for j in range(recv_ref.shape[0] // 32):
-            total = total + recv_ref[j * 32 : (j + 1) * 32, wide:].astype(F32)
-        total = total[:16] + total[16:]
-        parts = d // LANES
-        for c in range(parts):
-            here = pl.ds(c * LANES, LANES)
-            token_ref[here] = total[c : c + 1].reshape(LANES)
-            gain_ref[here] = total[parts + c : parts + c + 1].reshape(LANES)
-        coef_ref[...] = total[2 * parts : 2 * parts + 1, : coef_ref.shape[1]]
-    else:
-        for c in range(d // hw):
-            here = pl.ds(c * hw, hw)
-            token_ref[here] = sums_ref[c : c + 1].reshape(hw)
-            gain_ref[here] = sums_ref[2 + c : 3 + c].reshape(hw)
-        coef_ref[...] = sums_ref[4:5, : coef_ref.shape[1]]
     ctx = dot_nn(swap, recv_ref[:, :hw]).astype(BF)
     attn = dot_nn(ctx, w_ref[...]).astype(BF)
     delta = dot_nn(swap, recv_ref[:, hw:wide])
@@ -172,13 +150,24 @@
         cp.wait()
 
 
+def sums_kernel(here_ref, core_ref, token_ref, gain_ref, coef_ref):
+    total = here_ref[...] + core_ref[...]
+    width = total.shape[1]
+    parts = token_ref.shape[0] // width
+    for c in range(parts):
+        at = pl.ds(c * width, width)
+        token_ref[at] = total[c : c + 1].reshape(width)
+        gain_ref[at] = total[parts + c : parts + c + 1].reshape(width)
+    coef_ref[...] = total[2 * parts : 2 * parts + 1, : coef_ref.shape[1]]
+
+
 def split_two(value):
     high = value.astype(BF)
     return high, (value - high.astype(F32)).astype(BF)
 
 
 def merge_kernel(
-    nf, sb, guests, wide, head_rows, flag_ref, buf_ref, own_ref, got_ref, core_ref, cross_ref, out_ref, sums_ref
+    nf, sb, guests, wide, head_rows, flag_ref, buf_ref, own_ref, got_ref, out_ref, *sums_ref
 ):
     hw = got_ref.shape[1]
     segs = wide // hw
@@ -187,8 +176,9 @@
     i = iota((8, got_ref.shape[0]), 0)
     k = iota((8, got_ref.shape[0]), 1) - segs * seg_rows
     pick = ((i < SUMS) & ((k == i) | (k == i + SUMS))).astype(BF)
-    sums = (own_ref[...] + dot_nn(pick, got_ref[...])) + (core_ref[...] + cross_ref[...])
-    sums_ref[...] = sums
+    sums = own_ref[...] + dot_nn(pick, got_ref[...])
+    if sums_ref:
+        sums_ref[0][...] = sums
     if out_ref.shape[1] > wide:
         flat = jnp.concatenate(
             [sums[a : a + 1, c : c + LANES] for a in range(SUMS) for c in range(0, hw, LANES)]
@@ -714,41 +704,40 @@
 
     flip = [(i, (i + half) % n) for i in range(n)]
     got = lax.ppermute(pay, "seq", flip)
-    core = lax.ppermute(own_sums, "dp", [(0, 1), (1, 0)])
-    cross = lax.ppermute(
-        own_sums, ("dp", "seq"), [(c * n + i, (1 - c) * n + j) for c in range(2) for i, j in flip]
-    )
-    merged, sums = pl.pallas_call(
+    merged, *sums = pl.pallas_call(
         functools.partial(merge_kernel, nf, slots, guests, wide, head_rows),
         out_shape=(
             jax.ShapeDtypeStruct((rows, out_wide), BF),
-            jax.ShapeDtypeStruct((8, hw), F32),
-        ),
-        in_specs=[SMEM] + [VMEM] * 5,
-        out_specs=(VMEM, VMEM),
+        )
+        + (() if shared else (jax.ShapeDtypeStruct((8, hw), F32),)),
+        in_specs=[SMEM] + [VMEM] * 3,
+        out_specs=(VMEM,) * (1 if shared else 2),
         input_output_aliases={1: 0},
         compiler_params=pltpu.CompilerParams(vmem_limit_bytes=VMEM_LIMIT),
         name="merge",
-    )(flag, out, own_sums, got, core, cross)
+    )(flag, out, own_sums, got)
     returned = lax.all_to_all(merged, "seq", 0, 0, axis_index_groups=groups, tiled=True)
 
-    if not shared:
+    if shared:
+        parts = returned.reshape(half, block_rows, out_wide)[:, :32, wide:].astype(F32)
+        parts = jnp.sum(parts, axis=0)
+        sums = parts[:16] + parts[16:]
+    else:
+        sums = sums[0]
         k = 1
         while k < half:
             sums = sums + lax.ppermute(sums, "seq", [(i, i ^ k) for i in range(n)])
             k *= 2
 
-    layer_out, grad_x, token, gain, coef = pl.pallas_call(
-        functools.partial(final_kernel, slots, frames, shared),
+    core = lax.ppermute(sums, "dp", [(0, 1), (1, 0)])
+    layer_out, grad_x = pl.pallas_call(
+        functools.partial(final_kernel, slots, frames),
         out_shape=(
             jax.ShapeDtypeStruct((rows, d), BF),
             jax.ShapeDtypeStruct((rows, d), BF),
-            jax.ShapeDtypeStruct((d,), F32),
-            jax.ShapeDtypeStruct((d,), F32),
-            jax.ShapeDtypeStruct((1, heads), F32),
         ),
-        in_specs=[VMEM, HBM, HBM, VMEM, VMEM, VMEM, VMEM],
-        out_specs=(HBM, HBM, VMEM, VMEM, VMEM),
+        in_specs=[VMEM, HBM, HBM, VMEM, VMEM, VMEM],
+        out_specs=(HBM, HBM),
         scratch_shapes=[
             pltpu.VMEM((rows, d), BF),
             pltpu.VMEM((rows, d), BF),
@@ -758,7 +747,19 @@
         ],
         compiler_params=pltpu.CompilerParams(vmem_limit_bytes=VMEM_LIMIT),
         name="final",
-    )(returned, x, cot, hid, tok, w_out, sums)
+    )(returned, x, cot, hid, tok, w_out)
+    token, gain, coef = pl.pallas_call(
+        sums_kernel,
+        out_shape=(
+            jax.ShapeDtypeStruct((d,), F32),
+            jax.ShapeDtypeStruct((d,), F32),
+            jax.ShapeDtypeStruct((1, heads), F32),
+        ),
+        in_specs=[VMEM, VMEM],
+        out_specs=(VMEM, VMEM, VMEM),
+        compiler_params=pltpu.CompilerParams(vmem_limit_bytes=VMEM_LIMIT),
+        name="sums",
+    )(sums, core)
 
     shape = (1, slots, frames, d)
     return (

time: 73.3 us -> 70.4 us (0.960)
  starting transfers between devices: 15.4 us -> 12.4 us
  blocking collectives: 21 us -> 18.3 us
  waiting for transfers between devices: 14.3 us -> 16.8 us
    ppermute x1, waiting for transfers between devices: 0.44 us -> 5.11 us  [on_device(): got = lax.ppermute(pay, 'seq', flip)]
    ppermute x2 -> x1, starting transfers between devices: 3.03 us -> 0.07 us  [on_device(): core = lax.ppermute(sums, 'dp', [(0, 1), (1, 0)])]
    all_to_all x1, blocking collectives: 21 us -> 18.3 us  [on_device(): lax.all_to_all(merged, 'seq', 0, 0, axis_index_groups=groups, tiled=True)]
    ppermute x2 -> x1, waiting for transfers between devices: 2.18 us -> 0.01 us  [on_device(): core = lax.ppermute(sums, 'dp', [(0, 1), (1, 0)])]
    pallas_call x1 -> x2, Pallas kernels: 3.15 us -> 3.14 us  [the longest x1 2.53 us: on_device(): pl.pallas_call(functools.partial(final_kernel, slots, frames), out_shape=...]
  transfers between devices with their start and end apart: 12 -> 11, of which waited for: 4 -> 3; matrix products, arithmetic and copies ran while one was open for 0% -> 0% of each run, Pallas kernels for 2% -> 5%
where the time goes in v4:
time: 70.4 us; the launch traced here: 70 us
  Pallas kernels  21.1 us (30%)
  blocking collectives  18.3 us (26%)
  waiting for transfers between devices  16.8 us (24%)
  starting transfers between devices  12.4 us (18%)
  between operations  0.99 us (1%)
    all_to_all x1, blocking collectives, on_device(): lax.all_to_all(merged, 'seq', 0, 0, axis_index_groups=groups, tiled=True)  18.3 us
    pallas_call x1, Pallas kernels, on_device(): pl.pallas_call(functools.partial(frame_kernel, half, nf, slots, guests),...  11.6 us
    all_to_all x1, waiting for transfers between devices, on_device(): lax.all_to_all(send, 'seq', 0, 0, axis_index_groups=groups, tiled=True)  8.44 us
    all_to_all x1, starting transfers between devices, on_device(): lax.all_to_all(send, 'seq', 0, 0, axis_index_groups=groups, tiled=True)  6.33 us
    ppermute x1, waiting for transfers between devices, on_device(): got = lax.ppermute(pay, 'seq', flip)  5.11 us
    ppermute x7, starting transfers between devices, on_device(): ext = ext + lax.ppermute(packed[j], 'seq', [(half, j)])  4.63 us
    pallas_call x1, Pallas kernels, on_device(): pl.pallas_call(functools.partial(send_kernel, slots, frames), out_shape=(...  4.45 us
    ppermute x1, waiting for transfers between devices, on_device(): ext = lax.ppermute(packed[0], 'seq', [(half, 0)])  3.19 us
  transfers between devices with their start and end apart: 11, of which 3 were waited for; matrix products, arithmetic and copies ran while one was open for 0% of the time, Pallas kernels for 5%

profile of v4, /device:TPU:0, one launch (start us, length us, event | category | flops | bytes accessed | tf_op | source)
XLA Modules:
  0.0 70.0 jit_solution(2764854656992072159)
XLA Ops:
  0.6 4.5 %send.1 = (bf16[256,2304]{1,0:T(8,128)(2,1)}, f32[1,1536]{1,0:T(1,128)}) custom-call(bf16[256,1536]{1,0:T(8,128)(2,1)} %bitcast.16, bf16[256,1536]{1,0:T(8,128)(2,1)} %bitcast.18, s32[16,16]{1,0:T(8,128)} %bitcast.20, bf16[768,1536]{1,0:T(8,128)(2,1)} %w_ref.1), custom_call_target="tpu_custom_call" | custom-call | tf_op jit(solution)/shard_map/send/pallas_call | solution.py:595
  5.1 0.0 copy-start.1
  5.1 0.0 copy-start.4
  5.1 0.0 copy-start.8
  5.1 0.0 copy-start.9
  5.1 6.3 %all-to-all-start = ((bf16[8,32,2304]{2,1,0:T(8,128)(2,1)}), bf16[8,32,2304]{2,1,0:T(8,128)(2,1)S(1)}, u32[]{:S(2)}, u32[]{:S(2)}) async-start(bf16[8,32,2304]{2,1,0:T(8,128)(2,1)} %bitcast.15), calls=%async_computation | async-start | bytes 2359296 | tf_op jit(solution)/shard_map/all_to_all | solution.py:614
  11.5 0.0 copy-start.7
  11.5 0.0 copy-start.10
  11.5 0.0 copy-start.6
  11.5 0.1 pad_add_fusion.flag_ref.refs_2_
  11.6 0.0 copy-done.1
  11.6 0.0 copy-done.9
  11.6 1.2 %stage.1 = (f32[144,128]{1,0:T(8,128)S(1)}, f32[144,96]{1,0:T(8,128)S(1)}, bf16[32,768]{1,0:T(8,128)(2,1)S(1)}, bf16[32,768]{1,0:T(8,128)(2,1)S(1)}, bf16[32,768...) custom-call(s32[2]{0:T(128)S(1)} %pad_add_fusion.flag_ref.refs_2_, ...), custom_call_target="tpu_custom_call" | custom-call | tf_op jit(solution)/shard_map/stage/pallas_call | solution.py:628
  12.8 1.3 %collective-permute-start = (bf16[32,768]{1,0:T(8,128)(2,1)S(1)}, bf16[32,768]{1,0:T(8,128)(2,1)S(1)}, u32[]{:S(2)}, u32[]{:S(2)}) collective-permute-start(bf16[32,768]{1,0:T(8,128)(2,1)S(1)} %get-tuple-element.26), channel_id=1, source_target_pairs={{8,0},{24,16}} | collective-permute-start | bytes 147464 | tf_op jit(solution)/shard_map/ppermute | solution.py:642
  14.1 0.7 collective-permute-start.1
  14.8 0.7 collective-permute-start.2
  15.4 0.7 collective-permute-start.3
  16.1 0.7 collective-permute-start.4
  16.8 3.2 %collective-permute-done = bf16[32,768]{1,0:T(8,128)(2,1)S(1)} collective-permute-done((bf16[32,768]{1,0:T(8,128)(2,1)S(1)}, bf16[32,768]{1,0:T(8,128)(2,1)S(1)}, u32[]{:S(2)}, u32[]{:S(2)}) %collective-permute-start) | collective-permute-done | bytes 49184 | tf_op jit(solution)/shard_map/ppermute | solution.py:642
  20.0 0.7 collective-permute-start.5
  20.6 0.0 collective-permute-done.1
  20.7 0.7 collective-permute-start.6
  21.3 0.0 collective-permute-done.2
  21.3 0.7 collective-permute-start.7
  22.0 0.0 copy-done.11
  22.0 0.1 broadcast_in_dim.3
  22.1 0.1 reshape_reshape.3.refs_6_
  22.2 0.0 collective-permute-done.3
  22.2 0.0 collective-permute-done.4
  22.2 0.0 collective-permute-done.5
  22.3 0.0 collective-permute-done.6
  22.3 0.0 collective-permute-done.7
  22.3 8.4 %all-to-all-done = bf16[8,32,2304]{2,1,0:T(8,128)(2,1)S(1)} async-done(((bf16[8,32,2304]{2,1,0:T(8,128)(2,1)}), bf16[8,32,2304]{2,1,0:T(8,128)(2,1)S(1)}, u32[]{:S(2)}, u32[]{:S(2)}) %all-to-all-start) | async-done | bytes 1179680 | tf_op jit(solution)/shard_map/all_to_all | solution.py:614
  30.7 11.6 %frames.1 = (bf16[256,2560]{1,0:T(8,128)(2,1)S(1)}, bf16[40,768]{1,0:T(8,128)(2,1)S(1)}, f32[8,768]{1,0:T(8,128)S(1)}) custom-call(bf16[32,768]{1,0:T(8,128)(2,1)S(1)} %add_add_fusion.refs_0_, bf16[256,2304]{1,0:T(8,128)(2,1)S(1)} %bitcast.14, s32[2]{0:T(128)S(1)} %pad_add_fusion.flag_ref.refs_2_, f32[144,128]{1,0:T(8,128)S(1)} %get-tuple-element.34.refs_3_, ...), custom_call_target="tpu_custom_call" | custom-call | tf_op jit(solution)/shard_map/frames/pallas_call | solution.py:663
  42.4 0.1 collective-permute-start.8
  42.5 5.1 %collective-permute-done.8.got_ref = bf16[40,768]{1,0:T(8,128)(2,1)S(1)} collective-permute-done((bf16[40,768]{1,0:T(8,128)(2,1)S(1)}, bf16[40,768]{1,0:T(8,128)(2,1)S(1)}, u32[]{:S(2)}, u32[]{:S(2)}) %collective-permute-start.8) | collective-permute-done | bytes 61472 | tf_op jit(solution)/shard_map/ppermute | solution.py:706
  47.6 0.7 %merge.1 = bf16[256,2560]{1,0:T(8,128)(2,1)S(1)} custom-call(s32[2]{0:T(128)S(1)} %pad_add_fusion.flag_ref.refs_2_, bf16[256,2560]{1,0:T(8,128)(2,1)S(1)} %get-tuple-element.37.buf_ref, f32[8,768]{1,0:T(8,128)S(1)} %get-tuple-element.38.own_ref, bf16[40,768]{1,0:T(8,128)(2,1)S(1)} %collective-permute-done.8.got_ref), custom_call_target="tpu_custom_call", output_to_operand_aliasing={{}: (1, {})} | custom-call | tf_op jit(solution)/shard_map/merge/pallas_call | solution.py:707
  48.3 0.0 copy-start
  48.3 0.0 copy-start.5
  48.3 18.3 %all_to_all.22 = bf16[8,32,2560]{2,1,0:T(8,128)(2,1)S(1)} all-to-all(bf16[8,32,2560]{2,1,0:T(8,128)(2,1)S(1)} %bitcast.13), channel_id=1, replica_groups={{0,1,2,3,4,5,6,7},{8,9,10,11,12,13,14,15},{16,17,18,19,20,21,22,23},{24..., dimensions={0} | all-to-all | bytes 2621440 | tf_op jit(solution)/shard_map/all_to_all | solution.py:719
  66.7 0.1 collective-permute-start.9
  66.8 0.0 copy-done.2
  66.8 0.0 copy-done.3
  66.8 0.0 copy-done
  66.8 0.0 copy-done.5
  66.8 2.5 %final.1 = (bf16[256,1536]{1,0:T(8,128)(2,1)}, bf16[256,1536]{1,0:T(8,128)(2,1)}) custom-call(bf16[256,2560]{1,0:T(8,128)(2,1)S(1)} %bitcast.12, bf16[256,1536]{1,0:T(8,128)(2,1)S(1)} %bitcast.17, bf16[256,1536]{1,0:T(8,128)(2,1)S(1)} %bitcast.19, s32[16,16]{1,0:T(8,128)S(1)} %bitcast.21, bf16[1,1536]{1,0:T(2,128)(2,1)S(1)} %reshape.39.refs_7_.tok_ref, ...), custom_call_target="tpu_custom_call" | custom-call | tf_op jit(solution)/shard_map/final/pallas_call | solution.py:733
  69.4 0.0 collective-permute-done.9.core_ref
  69.4 0.6 sums.1
  (13 shorter events, 0.1 us)
Async XLA Ops:
  5.1 6.5 %copy-start.1 = (bf16[256,2304]{1,0:T(8,128)(2,1)S(1)}, bf16[256,2304]{1,0:T(8,128)(2,1)}, u32[]{:S(2)}) copy-start(bf16[256,2304]{1,0:T(8,128)(2,1)} %get-tuple-element.25.send_ref) | copy-start | bytes 3538948
  5.1 6.5 %copy-start.4 = (s32[4,136,136]{2,1,0:T(8,128)S(1)}, s32[4,136,136]{2,1,0:T(8,128)}, u32[]{:S(2)}) copy-start(s32[4,136,136]{2,1,0:T(8,128)} %adj_ref.1) | copy-start | bytes 887812
  5.1 6.5 %copy-start.8 = (s32[1,256]{1,0:T(1,128)S(1)}, s32[1,256]{1,0:T(1,128)}, u32[]{:S(2)}) copy-start(s32[1,256]{1,0:T(1,128)} %clip_ref.1) | copy-start | bytes 3076
  5.1 6.5 %copy-start.9 = (s32[1,256]{1,0:T(1,128)S(1)}, s32[1,256]{1,0:T(1,128)}, u32[]{:S(2)}) copy-start(s32[1,256]{1,0:T(1,128)} %kind_ref.1) | copy-start | bytes 3076
  5.1 25.6 %all-to-all-start = ((bf16[8,32,2304]{2,1,0:T(8,128)(2,1)}), bf16[8,32,2304]{2,1,0:T(8,128)(2,1)S(1)}, u32[]{:S(2)}, u32[]{:S(2)}) async-start(bf16[8,32,2304]{2,1,0:T(8,128)(2,1)} %bitcast.15), calls=%async_computation | async-start | bytes 2359296 | tf_op jit(solution)/shard_map/all_to_all | solution.py:614
  11.5 10.5 %copy-start.11 = (bf16[1536]{0:T(1024)(128)(2,1)S(1)}, bf16[1536]{0:T(1024)(128)(2,1)}, u32[]{:S(2)}) copy-start(bf16[1536]{0:T(1024)(128)(2,1)} %param.17) | copy-start | bytes 9220
  11.5 10.6 %copy-start.7 = (f32[12]{0:T(128)S(1)}, f32[12]{0:T(128)}, u32[]{:S(2)}) copy-start(f32[12]{0:T(128)} %refs_5_.1) | copy-start | bytes 148
  11.5 10.7 %copy-start.10 = (f32[1536]{0:T(1024)S(1)}, f32[1536]{0:T(1024)}, u32[]{:S(2)}) copy-start(f32[1536]{0:T(1024)} %param.18) | copy-start | bytes 18436
  11.5 19.3 %copy-start.6 = (f32[1,1536]{1,0:T(1,128)S(1)}, f32[1,1536]{1,0:T(1,128)}, u32[]{:S(2)}) copy-start(f32[1,1536]{1,0:T(1,128)} %get-tuple-element.36.refs_9_) | copy-start | bytes 18436
  12.8 7.2 %collective-permute-start = (bf16[32,768]{1,0:T(8,128)(2,1)S(1)}, bf16[32,768]{1,0:T(8,128)(2,1)S(1)}, u32[]{:S(2)}, u32[]{:S(2)}) collective-permute-start(bf16[32,768]{1,0:T(8,128)(2,1)S(1)} %get-tuple-element.26), channel_id=1, source_target_pairs={{8,0},{24,16}} | collective-permute-start | bytes 147464 | tf_op jit(solution)/shard_map/ppermute | solution.py:642
  14.1 6.5 %collective-permute-start.1 = (bf16[32,768]{1,0:T(8,128)(2,1)S(1)}, bf16[32,768]{1,0:T(8,128)(2,1)S(1)}, u32[]{:S(2)}, u32[]{:S(2)}) collective-permute-start(bf16[32,768]{1,0:T(8,128)(2,1)S(1)} %get-tuple-element.27), channel_id=1, source_target_pairs={{8,1},{24,17}} | collective-permute-start | bytes 147464 | tf_op jit(solution)/shard_map/ppermute | solution.py:644
  14.8 6.5 %collective-permute-start.2 = (bf16[32,768]{1,0:T(8,128)(2,1)S(1)}, bf16[32,768]{1,0:T(8,128)(2,1)S(1)}, u32[]{:S(2)}, u32[]{:S(2)}) collective-permute-start(bf16[32,768]{1,0:T(8,128)(2,1)S(1)} %get-tuple-element.28), channel_id=1, source_target_pairs={{8,2},{24,18}} | collective-permute-start | bytes 147464 | tf_op jit(solution)/shard_map/ppermute | solution.py:644
  15.4 6.8 %collective-permute-start.3 = (bf16[32,768]{1,0:T(8,128)(2,1)S(1)}, bf16[32,768]{1,0:T(8,128)(2,1)S(1)}, u32[]{:S(2)}, u32[]{:S(2)}) collective-permute-start(bf16[32,768]{1,0:T(8,128)(2,1)S(1)} %get-tuple-element.29), channel_id=1, source_target_pairs={{8,3},{24,19}} | collective-permute-start | bytes 147464 | tf_op jit(solution)/shard_map/ppermute | solution.py:644
  16.1 6.1 %collective-permute-start.4 = (bf16[32,768]{1,0:T(8,128)(2,1)S(1)}, bf16[32,768]{1,0:T(8,128)(2,1)S(1)}, u32[]{:S(2)}, u32[]{:S(2)}) collective-permute-start(bf16[32,768]{1,0:T(8,128)(2,1)S(1)} %get-tuple-element.30), channel_id=1, source_target_pairs={{8,4},{24,20}} | collective-permute-start | bytes 147464 | tf_op jit(solution)/shard_map/ppermute | solution.py:644
  20.0 2.3 %collective-permute-start.5 = (bf16[32,768]{1,0:T(8,128)(2,1)S(1)}, bf16[32,768]{1,0:T(8,128)(2,1)S(1)}, u32[]{:S(2)}, u32[]{:S(2)}) collective-permute-start(bf16[32,768]{1,0:T(8,128)(2,1)S(1)} %get-tuple-element.31), channel_id=1, source_target_pairs={{8,5},{24,21}} | collective-permute-start | bytes 147464 | tf_op jit(solution)/shard_map/ppermute | solution.py:644
  20.7 1.6 %collective-permute-start.6 = (bf16[32,768]{1,0:T(8,128)(2,1)S(1)}, bf16[32,768]{1,0:T(8,128)(2,1)S(1)}, u32[]{:S(2)}, u32[]{:S(2)}) collective-permute-start(bf16[32,768]{1,0:T(8,128)(2,1)S(1)} %get-tuple-element.32), channel_id=1, source_target_pairs={{8,6},{24,22}} | collective-permute-start | bytes 147464 | tf_op jit(solution)/shard_map/ppermute | solution.py:644
  21.3 0.9 %collective-permute-start.7 = (bf16[32,768]{1,0:T(8,128)(2,1)S(1)}, bf16[32,768]{1,0:T(8,128)(2,1)S(1)}, u32[]{:S(2)}, u32[]{:S(2)}) collective-permute-start(bf16[32,768]{1,0:T(8,128)(2,1)S(1)} %get-tuple-element.33), channel_id=1, source_target_pairs={{8,7},{24,23}} | collective-permute-start | bytes 147464 | tf_op jit(solution)/shard_map/ppermute | solution.py:644
  42.4 5.2 %collective-permute-start.8 = (bf16[40,768]{1,0:T(8,128)(2,1)S(1)}, bf16[40,768]{1,0:T(8,128)(2,1)S(1)}, u32[]{:S(2)}, u32[]{:S(2)}) collective-permute-start(bf16[40,768]{1,0:T(8,128)(2,1)S(1)} %get-tuple-element.39), channel_id=1, source_target_pairs={{0,8},{1,9},{2,10},{3,11},{4,12},{5,13},{6,14},{7,15},{8,0},{9,1},... | collective-permute-start | bytes 184328 | tf_op jit(solution)/shard_map/ppermute | solution.py:706
  47.6 19.2 %copy-start.2 = (bf16[1,16,16,1536]{3,2,1,0:T(8,128)(2,1)S(1)}, bf16[1,16,16,1536]{3,2,1,0:T(8,128)(2,1)}, u32[]{:S(2)}) copy-start(bf16[1,16,16,1536]{3,2,1,0:T(8,128)(2,1)} %param.11) | copy-start | bytes 2359300
  47.6 19.2 %copy-start.3 = (bf16[1,16,16,1536]{3,2,1,0:T(8,128)(2,1)S(1)}, bf16[1,16,16,1536]{3,2,1,0:T(8,128)(2,1)}, u32[]{:S(2)}) copy-start(bf16[1,16,16,1536]{3,2,1,0:T(8,128)(2,1)} %param.12) | copy-start | bytes 2359300
  48.3 18.5 %copy-start = (bf16[768,1536]{1,0:T(8,128)(2,1)S(1)}, bf16[768,1536]{1,0:T(8,128)(2,1)}, u32[]{:S(2)}) copy-start(bf16[768,1536]{1,0:T(8,128)(2,1)} %w_ref.1) | copy-start | bytes 7077892
  48.3 18.5 %copy-start.5 = (s32[1,16,16]{2,1,0:T(8,128)S(1)}, s32[1,16,16]{2,1,0:T(8,128)}, u32[]{:S(2)}) copy-start(s32[1,16,16]{2,1,0:T(8,128)} %param.13) | copy-start | bytes 3076
  66.7 2.7 %collective-permute-start.9 = (f32[16,256]{1,0:T(8,128)S(1)}, f32[16,256]{1,0:T(8,128)S(1)}, u32[]{:S(2)}, u32[]{:S(2)}) collective-permute-start(f32[16,256]{1,0:T(8,128)S(1)} %slice_add_fusion.here_ref), channel_id=1, source_target_pairs={{0,16},{16,0},{1,17},{17,1},{2,18},{18,2},{3,19},{19,3},{4,20},{20... | collective-permute-start | bytes 49160 | tf_op jit(solution)/shard_map/ppermute | solution.py:732

commit v5 on v4

--- a/solution.py
+++ b/solution.py
@@ -106,45 +106,35 @@
     slots,
     frames,
     recv_ref,
-    x_hbm,
-    cot_hbm,
+    x_ref,
+    cot_ref,
     hid_ref,
     tok_ref,
     w_ref,
     out_hbm,
     grad_hbm,
-    x_ref,
-    cot_ref,
     out_s,
     grad_s,
     sem,
 ):
     hw, d = w_ref.shape
     wide = hw + d
-    copies = [
-        pltpu.make_async_copy(cot_hbm, cot_ref, sem.at[0]),
-        pltpu.make_async_copy(x_hbm, x_ref, sem.at[1]),
-    ]
-    for cp in copies:
-        cp.start()
     swap = row_swap(slots, frames, False)
     hid = hidden_column(hid_ref[...], slots, frames, False) > 0.5
     ctx = dot_nn(swap, recv_ref[:, :hw]).astype(BF)
     attn = dot_nn(ctx, w_ref[...]).astype(BF)
     delta = dot_nn(swap, recv_ref[:, hw:wide])
-    for cp in copies:
-        cp.wait()
     stores = []
     half = swap.shape[0] // 2
     for h in range(2):
         r = slice(h * half, (h + 1) * half)
         here = pl.ds(h * half, half)
         grad_s[r] = jnp.where(hid[r], 0.0, cot_ref[r].astype(F32) + delta[r]).astype(BF)
-        stores.append(pltpu.make_async_copy(grad_s.at[here], grad_hbm.at[here], sem.at[2 + 2 * h]))
+        stores.append(pltpu.make_async_copy(grad_s.at[here], grad_hbm.at[here], sem.at[2 * h]))
         stores[-1].start()
         x_in = jnp.where(hid[r], tok_ref[...].astype(F32), x_ref[r].astype(F32))
         out_s[r] = (x_in + attn[r].astype(F32)).astype(BF)
-        stores.append(pltpu.make_async_copy(out_s.at[here], out_hbm.at[here], sem.at[3 + 2 * h]))
+        stores.append(pltpu.make_async_copy(out_s.at[here], out_hbm.at[here], sem.at[1 + 2 * h]))
         stores[-1].start()
     for cp in stores:
         cp.wait()
@@ -736,14 +726,12 @@
             jax.ShapeDtypeStruct((rows, d), BF),
             jax.ShapeDtypeStruct((rows, d), BF),
         ),
-        in_specs=[VMEM, HBM, HBM, VMEM, VMEM, VMEM],
+        in_specs=[VMEM] * 6,
         out_specs=(HBM, HBM),
         scratch_shapes=[
             pltpu.VMEM((rows, d), BF),
             pltpu.VMEM((rows, d), BF),
-            pltpu.VMEM((rows, d), BF),
-            pltpu.VMEM((rows, d), BF),
-            pltpu.SemaphoreType.DMA((6,)),
+            pltpu.SemaphoreType.DMA((4,)),
         ],
         compiler_params=pltpu.CompilerParams(vmem_limit_bytes=VMEM_LIMIT),
         name="final",

time: 70.4 us -> 70.2 us (level)
  no operation moved by 1% of the time
where the time goes in v5:
time: 70.2 us; the launch traced here: 69.8 us
  Pallas kernels  20.9 us (30%)
  blocking collectives  18.3 us (26%)
  waiting for transfers between devices  16.8 us (24%)
  starting transfers between devices  12.4 us (18%)
  between operations  0.99 us (1%)
    all_to_all x1, blocking collectives, on_device(): lax.all_to_all(merged, 'seq', 0, 0, axis_index_groups=groups, tiled=True)  18.3 us
    pallas_call x1, Pallas kernels, on_device(): pl.pallas_call(functools.partial(frame_kernel, half, nf, slots, guests),...  11.6 us
    all_to_all x1, waiting for transfers between devices, on_device(): lax.all_to_all(send, 'seq', 0, 0, axis_index_groups=groups, tiled=True)  8.44 us
    all_to_all x1, starting transfers between devices, on_device(): lax.all_to_all(send, 'seq', 0, 0, axis_index_groups=groups, tiled=True)  6.33 us
    ppermute x1, waiting for transfers between devices, on_device(): got = lax.ppermute(pay, 'seq', flip)  5.11 us
    ppermute x7, starting transfers between devices, on_device(): ext = ext + lax.ppermute(packed[j], 'seq', [(half, j)])  4.63 us
    pallas_call x1, Pallas kernels, on_device(): pl.pallas_call(functools.partial(send_kernel, slots, frames), out_shape=(...  4.45 us
    ppermute x1, waiting for transfers between devices, on_device(): ext = lax.ppermute(packed[0], 'seq', [(half, 0)])  3.19 us
  transfers between devices with their start and end apart: 11, of which 3 were waited for; matrix products, arithmetic and copies ran while one was open for 0% of the time, Pallas kernels for 5%

profile of v5, /device:TPU:0, one launch (start us, length us, event | category | flops | bytes accessed | tf_op | source)
XLA Modules:
  0.0 69.8 jit_solution(16243930005575631238)
XLA Ops:
  0.6 4.5 %send.1 = (bf16[256,2304]{1,0:T(8,128)(2,1)}, f32[1,1536]{1,0:T(1,128)}) custom-call(bf16[256,1536]{1,0:T(8,128)(2,1)} %bitcast.16, bf16[256,1536]{1,0:T(8,128)(2,1)} %bitcast.18, s32[16,16]{1,0:T(8,128)} %bitcast.20, bf16[768,1536]{1,0:T(8,128)(2,1)} %w_ref.1), custom_call_target="tpu_custom_call" | custom-call | tf_op jit(solution)/shard_map/send/pallas_call | solution.py:585
  5.1 0.0 copy-start.1
  5.1 0.0 copy-start.4
  5.1 0.0 copy-start.8
  5.1 0.0 copy-start.9
  5.1 6.3 %all-to-all-start = ((bf16[8,32,2304]{2,1,0:T(8,128)(2,1)}), bf16[8,32,2304]{2,1,0:T(8,128)(2,1)S(1)}, u32[]{:S(2)}, u32[]{:S(2)}) async-start(bf16[8,32,2304]{2,1,0:T(8,128)(2,1)} %bitcast.15), calls=%async_computation | async-start | bytes 2359296 | tf_op jit(solution)/shard_map/all_to_all | solution.py:604
  11.5 0.0 copy-start.7
  11.5 0.0 copy-start.10
  11.5 0.0 copy-start.6
  11.5 0.1 pad_add_fusion.flag_ref.refs_2_
  11.6 0.0 copy-done.1
  11.6 1.2 %stage.1 = (f32[144,128]{1,0:T(8,128)S(1)}, f32[144,96]{1,0:T(8,128)S(1)}, bf16[32,768]{1,0:T(8,128)(2,1)S(1)}, bf16[32,768]{1,0:T(8,128)(2,1)S(1)}, bf16[32,768...) custom-call(s32[2]{0:T(128)S(1)} %pad_add_fusion.flag_ref.refs_2_, ...), custom_call_target="tpu_custom_call" | custom-call | tf_op jit(solution)/shard_map/stage/pallas_call | solution.py:618
  12.8 1.3 %collective-permute-start = (bf16[32,768]{1,0:T(8,128)(2,1)S(1)}, bf16[32,768]{1,0:T(8,128)(2,1)S(1)}, u32[]{:S(2)}, u32[]{:S(2)}) collective-permute-start(bf16[32,768]{1,0:T(8,128)(2,1)S(1)} %get-tuple-element.26), channel_id=1, source_target_pairs={{8,0},{24,16}} | collective-permute-start | bytes 147464 | tf_op jit(solution)/shard_map/ppermute | solution.py:632
  14.1 0.7 collective-permute-start.1
  14.8 0.7 collective-permute-start.2
  15.4 0.7 collective-permute-start.3
  16.1 0.7 collective-permute-start.4
  16.8 3.2 %collective-permute-done = bf16[32,768]{1,0:T(8,128)(2,1)S(1)} collective-permute-done((bf16[32,768]{1,0:T(8,128)(2,1)S(1)}, bf16[32,768]{1,0:T(8,128)(2,1)S(1)}, u32[]{:S(2)}, u32[]{:S(2)}) %collective-permute-start) | collective-permute-done | bytes 49184 | tf_op jit(solution)/shard_map/ppermute | solution.py:632
  20.0 0.7 collective-permute-start.5
  20.6 0.0 collective-permute-done.1
  20.7 0.7 collective-permute-start.6
  21.3 0.0 collective-permute-done.2
  21.3 0.7 collective-permute-start.7
  22.0 0.1 broadcast_in_dim.3
  22.1 0.1 reshape_reshape.3.refs_6_
  22.2 0.0 copy-done.10
  22.2 0.0 collective-permute-done.3
  22.2 0.0 collective-permute-done.4
  22.2 0.0 collective-permute-done.5
  22.3 0.0 collective-permute-done.6
  22.3 0.0 collective-permute-done.7
  22.3 8.4 %all-to-all-done = bf16[8,32,2304]{2,1,0:T(8,128)(2,1)S(1)} async-done(((bf16[8,32,2304]{2,1,0:T(8,128)(2,1)}), bf16[8,32,2304]{2,1,0:T(8,128)(2,1)S(1)}, u32[]{:S(2)}, u32[]{:S(2)}) %all-to-all-start) | async-done | bytes 1179680 | tf_op jit(solution)/shard_map/all_to_all | solution.py:604
  30.7 0.0 copy-done.6
  30.7 11.6 %frames.1 = (bf16[256,2560]{1,0:T(8,128)(2,1)S(1)}, bf16[40,768]{1,0:T(8,128)(2,1)S(1)}, f32[8,768]{1,0:T(8,128)S(1)}) custom-call(bf16[32,768]{1,0:T(8,128)(2,1)S(1)} %add_add_fusion.refs_0_, bf16[256,2304]{1,0:T(8,128)(2,1)S(1)} %bitcast.14, s32[2]{0:T(128)S(1)} %pad_add_fusion.flag_ref.refs_2_, f32[144,128]{1,0:T(8,128)S(1)} %get-tuple-element.34.refs_3_, ...), custom_call_target="tpu_custom_call" | custom-call | tf_op jit(solution)/shard_map/frames/pallas_call | solution.py:653
  42.4 0.1 collective-permute-start.8
  42.5 5.1 %collective-permute-done.8.got_ref = bf16[40,768]{1,0:T(8,128)(2,1)S(1)} collective-permute-done((bf16[40,768]{1,0:T(8,128)(2,1)S(1)}, bf16[40,768]{1,0:T(8,128)(2,1)S(1)}, u32[]{:S(2)}, u32[]{:S(2)}) %collective-permute-start.8) | collective-permute-done | bytes 61472 | tf_op jit(solution)/shard_map/ppermute | solution.py:696
  47.6 0.7 %merge.1 = bf16[256,2560]{1,0:T(8,128)(2,1)S(1)} custom-call(s32[2]{0:T(128)S(1)} %pad_add_fusion.flag_ref.refs_2_, bf16[256,2560]{1,0:T(8,128)(2,1)S(1)} %get-tuple-element.37.buf_ref, f32[8,768]{1,0:T(8,128)S(1)} %get-tuple-element.38.own_ref, bf16[40,768]{1,0:T(8,128)(2,1)S(1)} %collective-permute-done.8.got_ref), custom_call_target="tpu_custom_call", output_to_operand_aliasing={{}: (1, {})} | custom-call | tf_op jit(solution)/shard_map/merge/pallas_call | solution.py:697
  48.3 0.0 copy-start
  48.3 0.0 copy-start.5
  48.3 18.3 %all_to_all.22 = bf16[8,32,2560]{2,1,0:T(8,128)(2,1)S(1)} all-to-all(bf16[8,32,2560]{2,1,0:T(8,128)(2,1)S(1)} %bitcast.13), channel_id=1, replica_groups={{0,1,2,3,4,5,6,7},{8,9,10,11,12,13,14,15},{16,17,18,19,20,21,22,23},{24..., dimensions={0} | all-to-all | bytes 2621440 | tf_op jit(solution)/shard_map/all_to_all | solution.py:709
  66.7 0.1 collective-permute-start.9
  66.8 0.0 copy-done.2
  66.8 0.0 copy-done.3
  66.8 0.0 copy-done
  66.8 0.0 copy-done.5
  66.8 2.3 %final.1 = (bf16[256,1536]{1,0:T(8,128)(2,1)}, bf16[256,1536]{1,0:T(8,128)(2,1)}) custom-call(bf16[256,2560]{1,0:T(8,128)(2,1)S(1)} %bitcast.12, bf16[256,1536]{1,0:T(8,128)(2,1)S(1)} %bitcast.17, bf16[256,1536]{1,0:T(8,128)(2,1)S(1)} %bitcast.19, s32[16,16]{1,0:T(8,128)S(1)} %bitcast.21, bf16[1,1536]{1,0:T(2,128)(2,1)S(1)} %reshape.39.refs_7_.tok_ref, ...), custom_call_target="tpu_custom_call" | custom-call | tf_op jit(solution)/shard_map/final/pallas_call | solution.py:723
  69.2 0.0 collective-permute-done.9.core_ref
  69.2 0.6 sums.1
  (13 shorter events, 0.1 us)
Async XLA Ops:
  5.1 6.5 %copy-start.1 = (bf16[256,2304]{1,0:T(8,128)(2,1)S(1)}, bf16[256,2304]{1,0:T(8,128)(2,1)}, u32[]{:S(2)}) copy-start(bf16[256,2304]{1,0:T(8,128)(2,1)} %get-tuple-element.25.send_ref) | copy-start | bytes 3538948
  5.1 6.5 %copy-start.4 = (s32[4,136,136]{2,1,0:T(8,128)S(1)}, s32[4,136,136]{2,1,0:T(8,128)}, u32[]{:S(2)}) copy-start(s32[4,136,136]{2,1,0:T(8,128)} %adj_ref.1) | copy-start | bytes 887812
  5.1 6.5 %copy-start.8 = (s32[1,256]{1,0:T(1,128)S(1)}, s32[1,256]{1,0:T(1,128)}, u32[]{:S(2)}) copy-start(s32[1,256]{1,0:T(1,128)} %clip_ref.1) | copy-start | bytes 3076
  5.1 6.5 %copy-start.9 = (s32[1,256]{1,0:T(1,128)S(1)}, s32[1,256]{1,0:T(1,128)}, u32[]{:S(2)}) copy-start(s32[1,256]{1,0:T(1,128)} %kind_ref.1) | copy-start | bytes 3076
  5.1 25.6 %all-to-all-start = ((bf16[8,32,2304]{2,1,0:T(8,128)(2,1)}), bf16[8,32,2304]{2,1,0:T(8,128)(2,1)S(1)}, u32[]{:S(2)}, u32[]{:S(2)}) async-start(bf16[8,32,2304]{2,1,0:T(8,128)(2,1)} %bitcast.15), calls=%async_computation | async-start | bytes 2359296 | tf_op jit(solution)/shard_map/all_to_all | solution.py:604
  11.5 10.5 %copy-start.11 = (bf16[1536]{0:T(1024)(128)(2,1)S(1)}, bf16[1536]{0:T(1024)(128)(2,1)}, u32[]{:S(2)}) copy-start(bf16[1536]{0:T(1024)(128)(2,1)} %param.17) | copy-start | bytes 9220
  11.5 10.6 %copy-start.7 = (f32[12]{0:T(128)S(1)}, f32[12]{0:T(128)}, u32[]{:S(2)}) copy-start(f32[12]{0:T(128)} %refs_5_.1) | copy-start | bytes 148
  11.5 10.7 %copy-start.10 = (f32[1536]{0:T(1024)S(1)}, f32[1536]{0:T(1024)}, u32[]{:S(2)}) copy-start(f32[1536]{0:T(1024)} %param.18) | copy-start | bytes 18436
  11.5 19.3 %copy-start.6 = (f32[1,1536]{1,0:T(1,128)S(1)}, f32[1,1536]{1,0:T(1,128)}, u32[]{:S(2)}) copy-start(f32[1,1536]{1,0:T(1,128)} %get-tuple-element.36.refs_9_) | copy-start | bytes 18436
  12.8 7.2 %collective-permute-start = (bf16[32,768]{1,0:T(8,128)(2,1)S(1)}, bf16[32,768]{1,0:T(8,128)(2,1)S(1)}, u32[]{:S(2)}, u32[]{:S(2)}) collective-permute-start(bf16[32,768]{1,0:T(8,128)(2,1)S(1)} %get-tuple-element.26), channel_id=1, source_target_pairs={{8,0},{24,16}} | collective-permute-start | bytes 147464 | tf_op jit(solution)/shard_map/ppermute | solution.py:632
  14.1 6.5 %collective-permute-start.1 = (bf16[32,768]{1,0:T(8,128)(2,1)S(1)}, bf16[32,768]{1,0:T(8,128)(2,1)S(1)}, u32[]{:S(2)}, u32[]{:S(2)}) collective-permute-start(bf16[32,768]{1,0:T(8,128)(2,1)S(1)} %get-tuple-element.27), channel_id=1, source_target_pairs={{8,1},{24,17}} | collective-permute-start | bytes 147464 | tf_op jit(solution)/shard_map/ppermute | solution.py:634
  14.8 6.5 %collective-permute-start.2 = (bf16[32,768]{1,0:T(8,128)(2,1)S(1)}, bf16[32,768]{1,0:T(8,128)(2,1)S(1)}, u32[]{:S(2)}, u32[]{:S(2)}) collective-permute-start(bf16[32,768]{1,0:T(8,128)(2,1)S(1)} %get-tuple-element.28), channel_id=1, source_target_pairs={{8,2},{24,18}} | collective-permute-start | bytes 147464 | tf_op jit(solution)/shard_map/ppermute | solution.py:634
  15.4 6.8 %collective-permute-start.3 = (bf16[32,768]{1,0:T(8,128)(2,1)S(1)}, bf16[32,768]{1,0:T(8,128)(2,1)S(1)}, u32[]{:S(2)}, u32[]{:S(2)}) collective-permute-start(bf16[32,768]{1,0:T(8,128)(2,1)S(1)} %get-tuple-element.29), channel_id=1, source_target_pairs={{8,3},{24,19}} | collective-permute-start | bytes 147464 | tf_op jit(solution)/shard_map/ppermute | solution.py:634
  16.1 6.1 %collective-permute-start.4 = (bf16[32,768]{1,0:T(8,128)(2,1)S(1)}, bf16[32,768]{1,0:T(8,128)(2,1)S(1)}, u32[]{:S(2)}, u32[]{:S(2)}) collective-permute-start(bf16[32,768]{1,0:T(8,128)(2,1)S(1)} %get-tuple-element.30), channel_id=1, source_target_pairs={{8,4},{24,20}} | collective-permute-start | bytes 147464 | tf_op jit(solution)/shard_map/ppermute | solution.py:634
  20.0 2.3 %collective-permute-start.5 = (bf16[32,768]{1,0:T(8,128)(2,1)S(1)}, bf16[32,768]{1,0:T(8,128)(2,1)S(1)}, u32[]{:S(2)}, u32[]{:S(2)}) collective-permute-start(bf16[32,768]{1,0:T(8,128)(2,1)S(1)} %get-tuple-element.31), channel_id=1, source_target_pairs={{8,5},{24,21}} | collective-permute-start | bytes 147464 | tf_op jit(solution)/shard_map/ppermute | solution.py:634
  20.7 1.6 %collective-permute-start.6 = (bf16[32,768]{1,0:T(8,128)(2,1)S(1)}, bf16[32,768]{1,0:T(8,128)(2,1)S(1)}, u32[]{:S(2)}, u32[]{:S(2)}) collective-permute-start(bf16[32,768]{1,0:T(8,128)(2,1)S(1)} %get-tuple-element.32), channel_id=1, source_target_pairs={{8,6},{24,22}} | collective-permute-start | bytes 147464 | tf_op jit(solution)/shard_map/ppermute | solution.py:634
  21.3 0.9 %collective-permute-start.7 = (bf16[32,768]{1,0:T(8,128)(2,1)S(1)}, bf16[32,768]{1,0:T(8,128)(2,1)S(1)}, u32[]{:S(2)}, u32[]{:S(2)}) collective-permute-start(bf16[32,768]{1,0:T(8,128)(2,1)S(1)} %get-tuple-element.33), channel_id=1, source_target_pairs={{8,7},{24,23}} | collective-permute-start | bytes 147464 | tf_op jit(solution)/shard_map/ppermute | solution.py:634
  42.4 5.2 %collective-permute-start.8 = (bf16[40,768]{1,0:T(8,128)(2,1)S(1)}, bf16[40,768]{1,0:T(8,128)(2,1)S(1)}, u32[]{:S(2)}, u32[]{:S(2)}) collective-permute-start(bf16[40,768]{1,0:T(8,128)(2,1)S(1)} %get-tuple-element.39), channel_id=1, source_target_pairs={{0,8},{1,9},{2,10},{3,11},{4,12},{5,13},{6,14},{7,15},{8,0},{9,1},... | collective-permute-start | bytes 184328 | tf_op jit(solution)/shard_map/ppermute | solution.py:696
  47.6 19.2 %copy-start.2 = (bf16[1,16,16,1536]{3,2,1,0:T(8,128)(2,1)S(1)}, bf16[1,16,16,1536]{3,2,1,0:T(8,128)(2,1)}, u32[]{:S(2)}) copy-start(bf16[1,16,16,1536]{3,2,1,0:T(8,128)(2,1)} %param.11) | copy-start | bytes 2359300
  47.6 19.2 %copy-start.3 = (bf16[1,16,16,1536]{3,2,1,0:T(8,128)(2,1)S(1)}, bf16[1,16,16,1536]{3,2,1,0:T(8,128)(2,1)}, u32[]{:S(2)}) copy-start(bf16[1,16,16,1536]{3,2,1,0:T(8,128)(2,1)} %param.12) | copy-start | bytes 2359300
  48.3 18.5 %copy-start = (bf16[768,1536]{1,0:T(8,128)(2,1)S(1)}, bf16[768,1536]{1,0:T(8,128)(2,1)}, u32[]{:S(2)}) copy-start(bf16[768,1536]{1,0:T(8,128)(2,1)} %w_ref.1) | copy-start | bytes 7077892
  48.3 18.5 %copy-start.5 = (s32[1,16,16]{2,1,0:T(8,128)S(1)}, s32[1,16,16]{2,1,0:T(8,128)}, u32[]{:S(2)}) copy-start(s32[1,16,16]{2,1,0:T(8,128)} %param.13) | copy-start | bytes 3076
  66.7 2.4 %collective-permute-start.9 = (f32[16,256]{1,0:T(8,128)S(1)}, f32[16,256]{1,0:T(8,128)S(1)}, u32[]{:S(2)}, u32[]{:S(2)}) collective-permute-start(f32[16,256]{1,0:T(8,128)S(1)} %slice_add_fusion.here_ref), channel_id=1, source_target_pairs={{0,16},{16,0},{1,17},{17,1},{2,18},{18,2},{3,19},{19,3},{4,20},{20... | collective-permute-start | bytes 49160 | tf_op jit(solution)/shard_map/ppermute | solution.py:722
